TPU v7x, 512 devices: a whole 4x8x8 slice. The times are simulated.
512 devices in a mesh: ctx: 64 (over y, z), kvh: 8 (over x, core).
Axes of the slice: x: 4, y: 8, z: 8, core: 2. Of those that a mesh axis runs over, the one named last changes fastest.
Arguments:
- queries: bfloat16 [256, 128, 128], P('ctx', 'kvh'), may hold values from -90 to 90
- cache_keys: bfloat16 [131072, 8, 128], P('ctx', 'kvh'), may hold values from -4 to 4
- cache_values: bfloat16 [131072, 8, 128], P('ctx', 'kvh'), may hold values from -6 to 6
- new_keys: bfloat16 [256, 8, 128], P('ctx', 'kvh'), may hold values from -4 to 4
- new_values: bfloat16 [256, 8, 128], P('ctx', 'kvh'), may hold values from -6 to 6
- cache_len: int32 [64], P('ctx'), may hold values from 1 to 2048, 81920 in all
- segment: int32 [256], replicated, may hold values from 0 to 3, never falling along the last dimension, each value on 1 to 128 neighbouring positions
- out_weight: bfloat16 [16384, 16384], P('kvh', 'ctx'), may hold values from -0.046875 to 0.046875
Outputs:
- mixed: bfloat16 [256, 16384], P('kvh', 'ctx')
Inputs may be any that keep to these rules, and one draw needn't show every extreme that they name: `cache_len`: some shard holds 2048 live entries in every draw. `segment`: never falls along the tokens.
All inputs are finite; a program needn't handle non-finite values.
Results may differ from a plain program's by a relative error of at most 0.019.
Values may be sent and summed in bfloat16 or wider, within the bound.
No kernel may reach another device: no remote copies, remote signals or barrier semaphores. Data moves between devices by JAX's collectives and lax.ppermute only.
A program may use at most 64 MiB of HBM per device.

v0:
```python
import jax
import jax.numpy as jnp
from jax import lax
from jax.sharding import PartitionSpec as P


def shard_part(
    rows, row_seg, row_pos, cache_k, cache_v, live, fresh_k, fresh_v, fresh_seg, fresh_pos
):
    count_heads = rows.shape[1]
    group_size = count_heads // cache_k.shape[1]
    head_size = rows.shape[2]
    factor = 1.0 / head_size**0.5
    cache_ok = jnp.arange(cache_k.shape[0], dtype=jnp.int32) < live
    fresh_ok = (fresh_seg[None, :] == row_seg[:, None]) & (fresh_pos[None, :] <= row_pos[:, None])
    dims = (((1,), (1,)), ((), ()))

    def one_head(head):
        group = head // group_size
        query = lax.dynamic_index_in_dim(rows, head, 1, keepdims=False)
        keys_c = lax.dynamic_index_in_dim(cache_k, group, 1, keepdims=False)
        vals_c = lax.dynamic_index_in_dim(cache_v, group, 1, keepdims=False)
        keys_n = lax.dynamic_index_in_dim(fresh_k, group, 1, keepdims=False)
        vals_n = lax.dynamic_index_in_dim(fresh_v, group, 1, keepdims=False)
        score_c = lax.dot_general(query, keys_c, dims, preferred_element_type=jnp.float32) * factor
        score_n = lax.dot_general(query, keys_n, dims, preferred_element_type=jnp.float32) * factor
        score_c = jnp.where(cache_ok[None, :], score_c, -jnp.inf)
        score_n = jnp.where(fresh_ok, score_n, -jnp.inf)
        largest = jnp.maximum(jnp.max(score_c, axis=1), jnp.max(score_n, axis=1))
        weight_c = jnp.exp(score_c - largest[:, None]).astype(jnp.bfloat16)
        weight_n = jnp.exp(score_n - largest[:, None]).astype(jnp.bfloat16)
        totals = jnp.sum(weight_c.astype(jnp.float32), axis=1) + jnp.sum(
            weight_n.astype(jnp.float32), axis=1
        )
        result = jnp.dot(weight_c, vals_c, preferred_element_type=jnp.float32)
        result = result + jnp.dot(weight_n, vals_n, preferred_element_type=jnp.float32)
        return (result, largest, totals)

    outs, tops, totals = lax.map(one_head, jnp.arange(count_heads, dtype=jnp.int32))
    return (jnp.transpose(outs, (1, 0, 2)), tops.T, totals.T)


def combine(pieces):
    outs, tops, totals = pieces
    best = jnp.max(tops, axis=0)
    scale = jnp.exp(tops - best[None])
    numer = jnp.sum(outs * scale[..., None], axis=0)
    denom = jnp.sum(totals * scale, axis=0)
    return numer / denom[..., None]


def local(queries, cache_keys, cache_values, new_keys, new_values, cache_len, segment, out_weight):
    cycle = lax.axis_size("ctx")
    myself = lax.axis_index("ctx")
    block = queries.shape[0]
    heads = queries.shape[1]
    head_size = queries.shape[2]
    live = cache_len[0]
    fresh_pos = myself * block + jnp.arange(block, dtype=jnp.int32)
    fresh_seg = lax.dynamic_slice_in_dim(segment, myself * block, block, 0)
    everyone = lax.all_gather(queries, "ctx", axis=0, tiled=True)
    count = everyone.shape[0]
    row_pos = jnp.arange(count, dtype=jnp.int32)
    outs, tops, totals = shard_part(
        everyone,
        segment,
        row_pos,
        cache_keys,
        cache_values,
        live,
        new_keys,
        new_values,
        fresh_seg,
        fresh_pos,
    )
    outs_four = outs.reshape(cycle, block, heads, head_size)
    tops_three = tops.reshape(cycle, block, heads)
    totals_three = totals.reshape(cycle, block, heads)
    attended = combine(
        (
            lax.all_to_all(outs_four, "ctx", split_axis=0, concat_axis=0, tiled=True),
            lax.all_to_all(tops_three, "ctx", split_axis=0, concat_axis=0, tiled=True),
            lax.all_to_all(totals_three, "ctx", split_axis=0, concat_axis=0, tiled=True),
        )
    )
    attended = attended.astype(jnp.bfloat16).reshape(block, heads * head_size)
    every_row = lax.all_gather(attended, "ctx", axis=0, tiled=True)
    return lax.psum_scatter(
        jnp.dot(every_row, out_weight, preferred_element_type=jnp.float32).astype(jnp.bfloat16),
        "kvh",
        scatter_dimension=0,
        tiled=True,
    )


def solution(mesh):
    in_specs = (
        P("ctx", "kvh", None),
        P("ctx", "kvh", None),
        P("ctx", "kvh", None),
        P("ctx", "kvh", None),
        P("ctx", "kvh", None),
        P("ctx"),
        P(),
        P("kvh", "ctx"),
    )
    out_specs = P("kvh", "ctx")
    return jax.shard_map(local, mesh=mesh, in_specs=in_specs, out_specs=out_specs, check_vma=False)
```

profile of v0, /device:TPU:1, one launch (start us, length us, event | category | flops | bytes accessed | tf_op | source)
XLA Modules:
  0.0 511.9 jit_solution(6443417746614448630)
XLA Ops:
  8.1 85.4 %all-gather.4.cloned.1.call-done = bf16[256,16,128]{2,1,0:T(8,128)(2,1)} async-done(((bf16[4,16,128]{2,1,0:T(8,128)(2,1)}), bf16[256,16,128]{2,1,0:T(8,128)(2,1)}) %all-gather.4.cloned.1.call-update) | async-done | bytes 1048592 | tf_op jit(solution)/shard_map/all_gather | solution.py:61
  95.9 200.0 %while.15 = (s32[]{:T(128)}, f32[16,256,128]{2,0,1:T(8,128)}, f32[16,256]{1,0:T(8,128)S(1)}, f32[16,256]{1,0:T(8,128)S(1)}, s32[16]{0:T(128)S(1)}, /*index=5*/bf...) while((s32[]{:T(128)}, f32[16,256,128]{2,0,1:T(8,128)}, ...), condition=%wide.region_5.6_spmd.clone, body=%wide.region_0.5_spmd.clone.sunk | while | flops 273724928 | bytes 8164611 | solution.py:39
  103.7 4.7 dynamic_update_slice.17
  116.2 4.7 dynamic_update_slice.17
  128.7 4.7 dynamic_update_slice.17
  141.2 4.7 dynamic_update_slice.17
  153.7 4.7 dynamic_update_slice.17
  166.2 4.7 dynamic_update_slice.17
  178.7 4.7 dynamic_update_slice.17
  203.7 4.7 dynamic_update_slice.17
  216.2 4.7 dynamic_update_slice.17
  228.7 4.7 dynamic_update_slice.17
  241.2 4.7 dynamic_update_slice.17
  253.7 4.7 dynamic_update_slice.17
  266.2 4.7 dynamic_update_slice.17
  278.7 4.7 dynamic_update_slice.17
  291.2 4.7 dynamic_update_slice.17
  296.7 8.6 %all-to-all-start.1 = ((f32[64,4,16]{2,1,0:T(4,128)}), f32[64,4,16]{2,1,0:T(4,128)S(1)}, u32[]{:S(2)}, u32[]{:S(2)}) async-start(f32[64,4,16]{2,1,0:T(4,128)} %bitcast.4), calls=%async_computation.1 | async-start | bytes 262144 | tf_op jit(solution)/shard_map/all_to_all | solution.py:82
  306.0 10.8 %all-to-all-done.1 = f32[64,4,16]{2,1,0:T(4,128)S(1)} async-done(((f32[64,4,16]{2,1,0:T(4,128)}), f32[64,4,16]{2,1,0:T(4,128)S(1)}, u32[]{:S(2)}, u32[]{:S(2)}) %all-to-all-start.1) | async-done | bytes 16416 | tf_op jit(solution)/shard_map/all_to_all | solution.py:82
  325.2 7.8 %all-to-all-done.2 = f32[64,4,16]{2,1,0:T(4,128)S(1)} async-done(((f32[64,4,16]{2,1,0:T(4,128)}), f32[64,4,16]{2,1,0:T(4,128)S(1)}, u32[]{:S(2)}, u32[]{:S(2)}) %all-to-all-start.2) | async-done | bytes 16416 | tf_op jit(solution)/shard_map/all_to_all | solution.py:83
  333.0 4.7 all-to-all-start
  339.2 40.8 %all-to-all-done = f32[64,4,16,128]{3,1,2,0:T(4,128)S(1)} async-done(((f32[64,4,16,128]{3,1,2,0:T(4,128)}), f32[64,4,16,128]{3,1,2,0:T(4,128)S(1)}, u32[]{:S(2)}, u32[]{:S(2)}) %all-to-all-start) | async-done | bytes 2097184 | tf_op jit(solution)/shard_map/all_to_all | solution.py:81
  383.0 84.2 %all-gather.6.cloned.1.call-done = bf16[64,4,2048]{2,1,0:T(4,128)(2,1)} async-done(((bf16[1,4,2048]{2,1,0:T(4,128)(2,1)}), bf16[64,4,2048]{2,1,0:T(4,128)(2,1)}) %all-gather.6.cloned.1.call-update) | async-done | bytes 1048592 | tf_op jit(solution)/shard_map/all_gather | solution.py:87
  469.6 35.8 %reduce-scatter.2.cloned.1.call-done = bf16[32,256]{1,0:T(8,128)(2,1)} async-done(((bf16[256,256]{1,0:T(8,128)(2,1)}), bf16[32,256]{1,0:T(8,128)(2,1)}) %reduce-scatter.2.cloned.1.call-update) | async-done | bytes 16400 | tf_op jit(solution)/shard_map/reduce_scatter | solution.py:88
  (226 shorter events, 123.3 us)
Async XLA Ops:
  6.5 462.0 %copy-start = (bf16[2048,256]{1,0:T(8,128)(2,1)S(1)}, bf16[2048,256]{1,0:T(8,128)(2,1)}, u32[]{:S(2)}) copy-start(bf16[2048,256]{1,0:T(8,128)(2,1)} %param.17) | copy-start | bytes 3145732
  6.5 89.4 %copy-start.3 = (s32[256]{0:T(256)S(1)}, s32[256]{0:T(256)}, u32[]{:S(2)}) copy-start(s32[256]{0:T(256)} %param.16) | copy-start | bytes 3076
  6.5 89.4 %copy-start.2 = (bf16[4,1,128]{2,0,1:T(4,128)(2,1)S(1)}, bf16[4,1,128]{2,0,1:T(4,128)(2,1)}, u32[]{:S(2)}) copy-start(bf16[4,1,128]{2,0,1:T(4,128)(2,1)} %param.13) | copy-start | bytes 3076
  6.5 89.4 %copy-start.1 = (bf16[4,1,128]{2,0,1:T(4,128)(2,1)S(1)}, bf16[4,1,128]{2,0,1:T(4,128)(2,1)}, u32[]{:S(2)}) copy-start(bf16[4,1,128]{2,0,1:T(4,128)(2,1)} %param.14) | copy-start | bytes 3076
  6.5 86.9 %all-gather.4.cloned.1.call-start = ((), (), s32[]{:S(2)}) async-start(), calls=%async_computation.4 | async-start | bytes 1064960 | tf_op jit(solution)/shard_map/all_gather | solution.py:61
  296.7 20.1 %all-to-all-start.1 = ((f32[64,4,16]{2,1,0:T(4,128)}), f32[64,4,16]{2,1,0:T(4,128)S(1)}, u32[]{:S(2)}, u32[]{:S(2)}) async-start(f32[64,4,16]{2,1,0:T(4,128)} %bitcast.4), calls=%async_computation.1 | async-start | bytes 262144 | tf_op jit(solution)/shard_map/all_to_all | solution.py:82
  316.8 16.2 %all-to-all-start.2 = ((f32[64,4,16]{2,1,0:T(4,128)}), f32[64,4,16]{2,1,0:T(4,128)S(1)}, u32[]{:S(2)}, u32[]{:S(2)}) async-start(f32[64,4,16]{2,1,0:T(4,128)} %bitcast.6), calls=%async_computation.2 | async-start | bytes 262144 | tf_op jit(solution)/shard_map/all_to_all | solution.py:83
  333.0 47.0 %all-to-all-start = ((f32[64,4,16,128]{3,1,2,0:T(4,128)}), f32[64,4,16,128]{3,1,2,0:T(4,128)S(1)}, u32[]{:S(2)}, u32[]{:S(2)}) async-start(f32[64,4,16,128]{3,1,2,0:T(4,128)} %copy.27), calls=%async_computation | async-start | bytes 4194304 | tf_op jit(solution)/shard_map/all_to_all | solution.py:81
  337.7 129.5 %all-gather.6.cloned.1.call-start = ((), (), s32[]{:S(2)}) async-start(), calls=%async_computation.6 | async-start | bytes 1064960 | tf_op jit(solution)/shard_map/all_gather | solution.py:87
  382.9 122.5 %reduce-scatter.2.cloned.1.call-start = ((), (), s32[]{:S(2)}) async-start(), calls=%async_computation.5 | async-start | bytes 147456 | tf_op jit(solution)/shard_map/reduce_scatter | solution.py:88
Sparse Core Ops, SparseCore 0:
  10.4 83.0 all-gather.3
  383.0 84.0 all-gather.5
  469.9 35.3 reduce-scatter.1
where the time goes:
time: 516 us; the launch traced here: 512 us
  waiting for transfers between devices  265 us (51%)
  local copies, waits for them, and re-layouts  96.3 us (19%)
  matrix products  70.9 us (14%)
  loops' own time  27.1 us (5%)
  other arithmetic  21 us (4%)
  starting transfers between devices  18 us (3%)
  between operations  13.2 us (3%)
    all_gather x1, waiting for transfers between devices, local(): everyone = lax.all_gather(queries, 'ctx', axis=0, tiled=True)  85.4 us
    all_gather x1, waiting for transfers between devices, local(): every_row = lax.all_gather(attended, 'ctx', axis=0, tiled=True)  84.2 us
    dynamic_update_slice x48, local copies, waits for them, and re-layouts, shard_part(): lax.map(one_head, jnp.arange(count_heads, dtype=jnp.int32))  76.2 us
    all_to_all x1, waiting for transfers between devices, local(): lax.all_to_all(outs_four, 'ctx', split_axis=0, concat_axis=0, tiled=True)  40.8 us
    reduce_scatter x1, waiting for transfers between devices, local(): lax.psum_scatter(jnp.dot(every_row, out_weight, preferred_element_type=jn...  35.8 us
    another operation x1, loops' own time, shard_part(): lax.map(one_head, jnp.arange(count_heads, dtype=jnp.int32))  27.1 us
    dot_general x16, matrix products, one_head(): lax.dot_general(query, keys_c, dims, preferred_element_type=jnp.float32)  25.6 us
    dot_general x16, matrix products, one_head(): result = jnp.dot(weight_c, vals_c, preferred_element_type=jnp.float32)  24.6 us
  transfers between devices with their start and end apart: 6, of which 6 were waited for; matrix products, arithmetic and copies ran while one was open for 1% of the time, Pallas kernels for 0%

commit v1 on v0

v1 whole, which is shorter than its diff:
```python
import functools

import jax
import jax.numpy as jnp
from jax import lax
from jax.experimental import pallas as pl
from jax.experimental.pallas import tpu as pltpu
from jax.sharding import PartitionSpec as P

BF = jnp.bfloat16
F32 = jnp.float32
LOG2E = 1.4426950408889634
LIMIT = 48 * 1024 * 1024
SIDE = 8
TAIL = 32
STEPS = ((0, 0), (0, 1), (1, 0), (-1, -1))


def shift(value, step):
    pairs = []
    for y in range(SIDE):
        for z in range(SIDE):
            to = ((y + step[0]) % SIDE) * SIDE + (z + step[1]) % SIDE
            pairs.append((y * SIDE + z, to))
    return lax.ppermute(value, "ctx", pairs)


def alike():
    half = range(SIDE // 2)
    return [
        [(2 * a + py) * SIDE + 2 * b + pz for a in half for b in half]
        for py in range(2)
        for pz in range(2)
    ]


def exchange(value):
    return lax.all_to_all(value, "ctx", 0, 0, axis_index_groups=alike(), tiled=True)


def quarters(value):
    copies = jnp.broadcast_to(value[None], (16,) + value.shape)
    mine = exchange(copies).reshape(16 * value.shape[0], value.shape[1])
    return [mine] + [shift(mine, step) for step in STEPS[1:]]


def call(body, out_shape, flops=0, moved=0, scratch=(), smem=0, args=()):
    vmem = pl.BlockSpec(memory_space=pltpu.VMEM)
    scalars = pl.BlockSpec(memory_space=pltpu.SMEM)
    specs = [scalars] * smem + [vmem] * (len(args) - smem)
    return pl.pallas_call(
        body,
        out_shape=out_shape,
        in_specs=specs,
        out_specs=jax.tree.map(lambda _: vmem, out_shape),
        scratch_shapes=list(scratch),
        compiler_params=pltpu.CompilerParams(vmem_limit_bytes=LIMIT),
        cost_estimate=pl.CostEstimate(flops=flops, bytes_accessed=moved, transcendentals=0),
    )(*args)


def prepare_body(live_ref, k_ref, v_ref, fk_ref, fv_ref, ka_ref, vt_ref):
    live = live_ref[0]
    slots, width = k_ref.shape
    step = 256
    first = k_ref[0:16, :].astype(F32)[0:1, :]
    for at in range(0, slots, step):
        alive = lax.broadcasted_iota(jnp.int32, (step, width), 0) + at < live
        keys = jnp.where(alive, k_ref[at : at + step, :].astype(F32), first)
        ka_ref[at : at + step, :] = keys.astype(BF)
        vals = jnp.where(alive, v_ref[at : at + step, :].astype(F32), 0.0)
        vt_ref[0:width, at : at + step] = vals.T.astype(BF)
        flags = lax.broadcasted_iota(jnp.int32, (16, step), 1) + at < live
        vt_ref[width:, at : at + step] = flags.astype(F32).astype(BF)
    ka_ref[slots:, :] = fk_ref[...]
    pad = jnp.zeros((128 - fv_ref.shape[0], width), F32)
    vt_ref[0:width, slots:] = jnp.concatenate([fv_ref[...].astype(F32), pad], 0).T.astype(BF)
    flags = lax.broadcasted_iota(jnp.int32, (16, 128), 1) < 4
    vt_ref[width:, slots:] = flags.astype(F32).astype(BF)


def prepare(live, keys, vals, fresh_k, fresh_v):
    slots, width = keys.shape
    out = [
        jax.ShapeDtypeStruct((slots + 16, width), BF),
        jax.ShapeDtypeStruct((width + 16, slots + 128), BF),
    ]
    return call(prepare_body, out, smem=1, args=(live, keys, vals, fresh_k, fresh_v))


def attend_body(step, place_ref, ka_ref, vt_ref, q_ref, o_ref, s0, s1, lse_ref):
    keys, width = ka_ref.shape
    slots = keys - 16
    rows = 256
    pieces = q_ref.shape[0] // rows
    factor = LOG2E / width**0.5
    y, z = place_ref[0], place_ref[1]
    first = 4 * (SIDE * y + z)
    from_y = lax.rem(y + SIDE - step[0], 2)
    from_z = lax.rem(z + SIDE - step[1], 2)
    lane = lax.broadcasted_iota(jnp.int32, (16, rows), 1)
    token0 = 8 * (lane // 64) + lax.rem(lane // 16, 4) + 32 * from_y + 4 * from_z
    line = lax.broadcasted_iota(jnp.int32, (16, rows), 0)
    never = 1 << 30
    opens = jnp.where(line < 4, line + first, never)
    ends = jnp.full((16, rows), never, jnp.int32)
    for j in range(4):
        ends = jnp.where(line == j, place_ref[4 + j], ends)
    scores = (s0, s1)
    cuts = [(at, 256) for at in range(0, slots, 256)] + [(slots, 16)]
    dims = (((1,), (1,)), ((), ()))

    def score(i, cut, best):
        at, deep = cut
        query = q_ref[i * rows : (i + 1) * rows, :]
        part = lax.dot_general(
            ka_ref[at : at + deep, :], query, dims, preferred_element_type=F32
        )
        if deep == 16:
            token = token0 + 64 * i
            part = jnp.where((token >= opens) & (token < ends), part, -jnp.inf)
        scores[i % 2][at : at + deep, :] = part
        top = jnp.max(part.reshape(deep // 8, 8, rows), axis=0)
        return top if best is None else jnp.maximum(best, top)

    def weigh(i, cut, peak, total):
        at, deep = cut
        part = scores[i % 2][at : at + deep, :]
        weight = jnp.exp2((part - peak) * factor).astype(BF)
        wide = deep
        if deep == 16:
            weight = jnp.concatenate([weight, jnp.zeros((112, rows), BF)], 0)
            wide = 128
        add = jnp.dot(vt_ref[:, at : at + wide], weight, preferred_element_type=F32)
        return add if total is None else total + add

    best = None
    for cut in cuts:
        best = score(0, cut, best)
    for i in range(pieces):
        peak = jnp.max(best, axis=0, keepdims=True)
        best, total = None, None
        for cut in cuts:
            if i + 1 < pieces:
                best = score(i + 1, cut, best)
            total = weigh(i, cut, peak, total)
        count = total[width : width + 1, :]
        out = total[0:width, :] * (1.0 / count)
        o_ref[i * rows : (i + 1) * rows, :] = out.T.astype(BF)
        lse = peak * factor + jnp.log(count) * LOG2E
        for b in range(rows // 128):
            at = i * (rows // 128) + b
            lse_ref[at : at + 1, :] = lse[:, b * 128 : (b + 1) * 128]
    o_ref[pieces * rows :, :] = parts_of(lse_ref[...], 8)


def parts_of(lse, lines):
    parts = []
    for _ in range(3):
        top = lse.astype(BF).astype(F32)
        parts.append(top)
        lse = lse - top
    parts.append(jnp.zeros((lines, 128), F32))
    return jnp.concatenate(parts, 0).astype(BF)


def attend(place, ka, vt, query, step):
    rows, width = query.shape
    keys = ka.shape[0]
    scratch = [pltpu.VMEM((keys, 256), F32)] * 2 + [pltpu.VMEM((8, 128), F32)]
    return call(
        functools.partial(attend_body, step),
        jax.ShapeDtypeStruct((rows + TAIL, width), BF),
        flops=8 * rows * keys * 256,
        moved=(ka.size + vt.size + 2 * query.size) * 2,
        scratch=scratch,
        smem=1,
        args=(place, ka, vt, query),
    )


def diagonal(rows):
    return lax.broadcasted_iota(jnp.int32, (rows, 128), 0) == lax.broadcasted_iota(
        jnp.int32, (rows, 128), 1
    )


def spread(row, eye):
    return jnp.sum(jnp.where(eye, row, 0.0), axis=1, keepdims=True)


def first_body(*refs):
    ins, out_ref = refs[:-1], refs[-1]
    rows = ins[0].shape[0] - TAIL
    eye = diagonal(128)
    logs = []
    for ref in ins:
        tail = ref[rows:, :].astype(F32)
        logs.append(tail[0:8] + tail[8:16] + tail[16:24])
    top = functools.reduce(jnp.maximum, logs)
    weights = [jnp.exp2(log - top) for log in logs]
    total = functools.reduce(jnp.add, weights)
    lse = top + jnp.log(total) * LOG2E
    weights = [w / total for w in weights]
    parts = []
    for _ in range(3):
        high = lse.astype(BF).astype(F32)
        parts.append(high)
        lse = lse - high
    empty = jnp.zeros((5, 128), F32)
    for b in range(rows // 128):
        merged = None
        for ref, weight in zip(ins, weights):
            term = ref[b * 128 : (b + 1) * 128, :].astype(F32) * spread(weight[b : b + 1], eye)
            merged = term if merged is None else merged + term
        merged = merged.astype(BF)
        tail = jnp.concatenate([p[b : b + 1] for p in parts] + [empty], 0).astype(BF)
        for j in range(2):
            out_ref[2 * b + j, 0:64, :] = merged[64 * j : 64 * j + 64, :]
            out_ref[2 * b + j, 64:72, :] = tail


def first_merge(ins):
    rows, width = ins[0].shape
    out = jax.ShapeDtypeStruct(((rows - TAIL) // 64, 72, width), BF)
    return call(first_body, out, args=tuple(ins))


def second_body(place_ref, got_ref, out_ref, logs):
    parts = got_ref.shape[0]
    for c in range(parts):
        tail = got_ref[c, 64:72, :].astype(F32)
        logs[c : c + 1, :] = tail[0:1] + tail[1:2] + tail[2:3]
    odd = lax.rem(place_ref[1] // 2, 2)
    lse = logs[...]
    lse = jnp.where(odd == 1, pltpu.roll(lse, 64, 1), lse)
    weight = jnp.exp2(lse - jnp.max(lse, axis=0, keepdims=True))
    weight = weight / jnp.sum(weight, axis=0, keepdims=True)
    eye = diagonal(64)
    total = None
    for c in range(parts):
        term = got_ref[c, 0:64, :].astype(F32) * spread(weight[c : c + 1, :], eye)
        total = term if total is None else total + term
    out_ref[...] = total.astype(BF)


def second_merge(place, got):
    return call(
        second_body,
        jax.ShapeDtypeStruct((64, got.shape[2]), BF),
        scratch=[pltpu.VMEM((got.shape[0], 128), F32)],
        smem=1,
        args=(place, got),
    )


def project_body(place_ref, w_ref, *refs):
    ins, out_ref, rows, left, placed = refs[:4], refs[4], refs[5], refs[6], refs[7]
    deep = w_ref.shape[0]
    width = ins[0].shape[1]
    heads = deep // width
    tokens = ins[0].shape[0] // heads
    for i, ref in enumerate(ins):
        rows[...] = ref[...].astype(F32)
        for h in range(heads):
            left[i * tokens : (i + 1) * tokens, h * width : (h + 1) * width] = rows[
                pl.ds(h, tokens, stride=heads), :
            ].astype(BF)
    mixed = jnp.dot(left[...], w_ref[...], preferred_element_type=F32)
    y, z = place_ref[0], place_ref[1]
    for i, step in enumerate(STEPS):
        from_y = lax.rem(y + SIDE - step[0], 2)
        from_z = lax.rem(z + SIDE - step[1], 2)
        for n in range(tokens // 4):
            to = 16 * (n // 4) + 2 * (n % 4) + 8 * from_y + from_z
            placed[to] = mixed[i * tokens + 4 * n : i * tokens + 4 * n + 4, :]
    for k in range(out_ref.shape[0]):
        out_ref[k] = jnp.concatenate([placed[8 * k + n] for n in range(8)], 0).astype(BF)


def project(place, weight, ins):
    deep, cols = weight.shape
    rows, width = ins[0].shape
    tokens = 4 * rows * width // deep
    return call(
        project_body,
        jax.ShapeDtypeStruct((8, tokens // 8, cols), BF),
        flops=2 * tokens * deep * cols,
        scratch=[
            pltpu.VMEM((rows, width), F32),
            pltpu.VMEM((tokens, deep), BF),
            pltpu.VMEM((tokens // 4, 4, cols), F32),
        ],
        smem=1,
        args=(place, weight, *ins),
    )


def final_body(got_ref, out_ref):
    total = got_ref[0].astype(F32)
    for i in range(1, got_ref.shape[0]):
        total = total + got_ref[i].astype(F32)
    out_ref[...] = total.astype(BF)


def local(queries, cache_keys, cache_values, new_keys, new_values, cache_len, segment, out_weight):
    me = lax.axis_index("ctx")
    block, heads, width = queries.shape
    asked = quarters(queries.reshape(block * heads, width))

    own_seg = lax.dynamic_slice_in_dim(segment, me * block, block, 0)
    ends = jnp.sum(segment[None, :] <= own_seg[:, None], axis=1).astype(jnp.int32)
    zero = jnp.zeros((), jnp.int32)
    place = jnp.concatenate([jnp.stack([me // SIDE, me % SIDE, zero, zero]), ends])

    pad = ((0, 16 - block), (0, 0))
    ka, vt = prepare(
        cache_len,
        cache_keys[:, 0, :],
        cache_values[:, 0, :],
        jnp.pad(new_keys[:, 0, :], pad),
        jnp.pad(new_values[:, 0, :], pad),
    )
    partial = [attend(place, ka, vt, q, step) for q, step in zip(asked, STEPS)]
    back = [shift(p, (-s[0], -s[1])) for p, s in zip(partial[1:], STEPS[1:])]
    own = second_merge(place, exchange(first_merge([partial[0]] + back)))
    parts = project(place, out_weight, quarters(own))
    got = lax.all_to_all(parts, "kvh", 0, 0, tiled=True)
    return call(final_body, jax.ShapeDtypeStruct(got.shape[1:], BF), args=(got,))


def solution(mesh):
    in_specs = (
        P("ctx", "kvh", None),
        P("ctx", "kvh", None),
        P("ctx", "kvh", None),
        P("ctx", "kvh", None),
        P("ctx", "kvh", None),
        P("ctx"),
        P(),
        P("kvh", "ctx"),
    )
    out_specs = P("kvh", "ctx")
    return jax.shard_map(local, mesh=mesh, in_specs=in_specs, out_specs=out_specs, check_vma=False)
```

time: 516 us -> 143 us (0.28)
  waiting for transfers between devices: 265 us -> 7.7 us
  local copies, waits for them, and re-layouts: 96.3 us -> 4.03 us
  blocking collectives: 0 us -> 81.2 us
  matrix products: 70.9 us -> 0 us
  loops' own time: 27.1 us -> 0 us
  Pallas kernels: 0 us -> 21.8 us
  other arithmetic: 21 us -> 0.26 us
  between operations: 13.2 us -> 0.87 us
  starting transfers between devices: 18 us -> 26.5 us
    all_gather x2 -> x0, waiting for transfers between devices: 170 us -> none  [the longest x1 85.4 us: local(): everyone = lax.all_gather(queries, 'ctx', axis=0, tiled=True)]
    all_to_all x0 -> x4, blocking collectives: none -> 81.2 us  [the longest x3 64 us: exchange(): lax.all_to_all(value, 'ctx', 0, 0, axis_index_groups=alike(), tiled=True)]
    dynamic_update_slice x48 -> x0, local copies, waits for them, and re-layouts: 76.2 us -> none  [shard_part(): lax.map(one_head, jnp.arange(count_heads, dtype=jnp.int32))]
    dot_general x65 -> x0, matrix products: 70.9 us -> none  [the longest x16 25.6 us: one_head(): lax.dot_general(query, keys_c, dims, preferred_element_type=jnp.float32)]
    all_to_all x3 -> x0, waiting for transfers between devices: 59.3 us -> none  [the longest x1 40.8 us: local(): lax.all_to_all(outs_four, 'ctx', split_axis=0, concat_axis=0, tiled=True)]
    reduce_scatter x1 -> x0, waiting for transfers between devices: 35.8 us -> none  [local(): lax.psum_scatter(jnp.dot(every_row, out_weight, preferred_element_type=jn...]
    another operation x1 -> x0, loops' own time: 27.1 us -> none  [shard_part(): lax.map(one_head, jnp.arange(count_heads, dtype=jnp.int32))]
    ppermute x0 -> x9, starting transfers between devices: none -> 26.5 us  [shift(): return lax.ppermute(value, 'ctx', pairs)]
  transfers between devices with their start and end apart: 6 -> 9, of which waited for: 6 -> 3; matrix products, arithmetic and copies ran while one was open for 1% -> 0% of each run, Pallas kernels for 0% -> 12%
where the time goes in v1:
time: 143 us; the launch traced here: 142 us
  blocking collectives  81.2 us (57%)
  starting transfers between devices  26.5 us (19%)
  Pallas kernels  21.8 us (15%)
  waiting for transfers between devices  7.7 us (5%)
  local copies, waits for them, and re-layouts  4.03 us (3%)
    all_to_all x3, blocking collectives, exchange(): lax.all_to_all(value, 'ctx', 0, 0, axis_index_groups=alike(), tiled=True)  64 us
    ppermute x9, starting transfers between devices, shift(): return lax.ppermute(value, 'ctx', pairs)  26.5 us
    pallas_call x9, Pallas kernels, call(): pl.pallas_call(body, out_shape=out_shape, in_specs=specs, out_specs=jax.t...  21.8 us
    all_to_all x1, blocking collectives, local(): got = lax.all_to_all(parts, 'kvh', 0, 0, tiled=True)  17.2 us
    ppermute x9, waiting for transfers between devices, shift(): return lax.ppermute(value, 'ctx', pairs)  7.7 us
    unnamed x12, local copies, waits for them, and re-layouts  3.08 us
  transfers between devices with their start and end apart: 9, of which 3 were waited for; matrix products, arithmetic and copies ran while one was open for 0% of the time, Pallas kernels for 12%

profile of v1, /device:TPU:1, one launch (start us, length us, event | category | flops | bytes accessed | tf_op | source)
XLA Modules:
  0.0 142.3 jit_solution(2922114943156140518)
XLA Ops:
  0.0 0.8 broadcast_in_dim.7
  0.8 28.4 %all_to_all.20 = bf16[16,64,128]{2,1,0:T(8,128)(2,1)S(1)} all-to-all(bf16[16,64,128]{2,1,0:T(8,128)(2,1)S(1)} %broadcast_in_dim.7), channel_id=1, replica_groups={{0,16,32,48,128,144,160,176,256,272,288,304,384,400,416,432},{8,24,40,5..., dimensions={0} | all-to-all | bytes 524288 | tf_op jit(solution)/shard_map/all_to_all | solution.py:38
  29.2 3.7 %collective-permute-start = (bf16[1024,128]{1,0:T(8,128)(2,1)S(1)}, bf16[1024,128]{1,0:T(8,128)(2,1)S(1)}, u32[]{:S(2)}, u32[]{:S(2)}) collective-permute-start(bf16[1024,128]{1,0:T(8,128)(2,1)S(1)} %bitcast.15), channel_id=1, source_target_pairs={{0,8},{8,16},{16,24},{24,32},{32,40},{40,48},{48,56},{56,0},{64,72... | collective-permute-start | bytes 786440 | tf_op jit(solution)/shard_map/ppermute | solution.py:25
  35.7 1.0 copy-done.2
  37.3 2.4 %collective-permute-start.4 = (bf16[1024,128]{1,0:T(8,128)(2,1)S(1)}, bf16[1024,128]{1,0:T(8,128)(2,1)S(1)}, u32[]{:S(2)}, u32[]{:S(2)}) collective-permute-start(bf16[1024,128]{1,0:T(8,128)(2,1)S(1)} %bitcast.16), channel_id=1, source_target_pairs={{0,504},{8,448},{16,456},{24,464},{32,472},{40,480},{48,488},{56,4... | collective-permute-start | bytes 786440 | tf_op jit(solution)/shard_map/ppermute | solution.py:25
  39.7 3.5 %collective-permute-start.2 = (bf16[1024,128]{1,0:T(8,128)(2,1)S(1)}, bf16[1024,128]{1,0:T(8,128)(2,1)S(1)}, u32[]{:S(2)}, u32[]{:S(2)}) collective-permute-start(bf16[1024,128]{1,0:T(8,128)(2,1)S(1)} %bitcast.17), channel_id=1, source_target_pairs={{0,64},{8,72},{16,80},{24,88},{32,96},{40,104},{48,112},{56,120},{... | collective-permute-start | bytes 786440 | tf_op jit(solution)/shard_map/ppermute | solution.py:25
  43.3 4.3 %shard_map.84 = bf16[1056,128]{1,0:T(8,128)(2,1)S(1)} custom-call(s32[8]{0:T(128)S(1)} %pad_add_fusion.place_ref, bf16[2064,128]{1,0:T(8,128)(2,1)S(1)} %get-tuple-element.7.ka_ref, bf16[144,2176]{1,0:T(8,128)(2,1)S(1)} %get-tuple-element.8.vt_ref, bf16[1024,128]{1,0:T(8,128)(2,1)S(1)} %collective-permute-done.q_ref), custom_call_target="tpu_custom_call" | custom-call | flops 4328521728 | bytes 1679360 | tf_op jit(solution)/shard_map/pallas_call | solution.py:51
  47.6 2.0 %collective-permute-start.1 = (bf16[1056,128]{1,0:T(8,128)(2,1)S(1)}, bf16[1056,128]{1,0:T(8,128)(2,1)S(1)}, u32[]{:S(2)}, u32[]{:S(2)}) collective-permute-start(bf16[1056,128]{1,0:T(8,128)(2,1)S(1)} %shard_map.84), channel_id=1, source_target_pairs={{0,56},{8,0},{16,8},{24,16},{32,24},{40,32},{48,40},{56,48},{64,12... | collective-permute-start | bytes 811016 | tf_op jit(solution)/shard_map/ppermute | solution.py:25
  49.6 4.3 %shard_map.85 = bf16[1056,128]{1,0:T(8,128)(2,1)S(1)} custom-call(s32[8]{0:T(128)S(1)} %pad_add_fusion.place_ref, bf16[2064,128]{1,0:T(8,128)(2,1)S(1)} %get-tuple-element.7.ka_ref, bf16[144,2176]{1,0:T(8,128)(2,1)S(1)} %get-tuple-element.8.vt_ref, bf16[1024,128]{1,0:T(8,128)(2,1)S(1)} %collective-permute-done.2.q_ref), custom_call_target="tpu_custom_call" | custom-call | flops 4328521728 | bytes 1679360 | tf_op jit(solution)/shard_map/pallas_call | solution.py:51
  53.9 3.3 %collective-permute-start.3 = (bf16[1056,128]{1,0:T(8,128)(2,1)S(1)}, bf16[1056,128]{1,0:T(8,128)(2,1)S(1)}, u32[]{:S(2)}, u32[]{:S(2)}) collective-permute-start(bf16[1056,128]{1,0:T(8,128)(2,1)S(1)} %shard_map.85), channel_id=1, source_target_pairs={{0,448},{8,456},{16,464},{24,472},{32,480},{40,488},{48,496},{56,5... | collective-permute-start | bytes 811016 | tf_op jit(solution)/shard_map/ppermute | solution.py:25
  57.2 4.3 %shard_map.86 = bf16[1056,128]{1,0:T(8,128)(2,1)S(1)} custom-call(s32[8]{0:T(128)S(1)} %pad_add_fusion.place_ref, bf16[2064,128]{1,0:T(8,128)(2,1)S(1)} %get-tuple-element.7.ka_ref, bf16[144,2176]{1,0:T(8,128)(2,1)S(1)} %get-tuple-element.8.vt_ref, bf16[1024,128]{1,0:T(8,128)(2,1)S(1)} %collective-permute-done.4.q_ref), custom_call_target="tpu_custom_call" | custom-call | flops 4328521728 | bytes 1679360 | tf_op jit(solution)/shard_map/pallas_call | solution.py:51
  61.6 3.2 %collective-permute-start.5 = (bf16[1056,128]{1,0:T(8,128)(2,1)S(1)}, bf16[1056,128]{1,0:T(8,128)(2,1)S(1)}, u32[]{:S(2)}, u32[]{:S(2)}) collective-permute-start(bf16[1056,128]{1,0:T(8,128)(2,1)S(1)} %shard_map.86), channel_id=1, source_target_pairs={{0,72},{8,80},{16,88},{24,96},{32,104},{40,112},{48,120},{56,64},{... | collective-permute-start | bytes 811016 | tf_op jit(solution)/shard_map/ppermute | solution.py:25
  64.8 4.3 %shard_map.83.refs_0_ = bf16[1056,128]{1,0:T(8,128)(2,1)S(1)} custom-call(s32[8]{0:T(128)S(1)} %pad_add_fusion.place_ref, bf16[2064,128]{1,0:T(8,128)(2,1)S(1)} %get-tuple-element.7.ka_ref, bf16[144,2176]{1,0:T(8,128)(2,1)S(1)} %get-tuple-element.8.vt_ref, bf16[1024,128]{1,0:T(8,128)(2,1)S(1)} %bitcast.18), custom_call_target="tpu_custom_call" | custom-call | flops 4328521728 | bytes 1679360 | tf_op jit(solution)/shard_map/pallas_call | solution.py:51
  69.1 3.0 %collective-permute-done.5.refs_3_ = bf16[1056,128]{1,0:T(8,128)(2,1)S(1)} collective-permute-done((bf16[1056,128]{1,0:T(8,128)(2,1)S(1)}, bf16[1056,128]{1,0:T(8,128)(2,1)S(1)}, u32[]{:S(2)}, u32[]{:S(2)}) %collective-permute-start.5) | collective-permute-done | bytes 270368 | tf_op jit(solution)/shard_map/ppermute | solution.py:25
  72.8 20.3 %all_to_all.21.got_ref = bf16[16,72,128]{2,1,0:T(8,128)(2,1)S(1)} all-to-all(bf16[16,72,128]{2,1,0:T(8,128)(2,1)S(1)} %shard_map.87), channel_id=1, replica_groups={{0,16,32,48,128,144,160,176,256,272,288,304,384,400,416,432},{8,24,40,5..., dimensions={0} | all-to-all | bytes 589824 | tf_op jit(solution)/shard_map/all_to_all | solution.py:38
  93.1 0.9 shard_map.88
  94.0 15.3 %all_to_all.22 = bf16[16,64,128]{2,1,0:T(8,128)(2,1)S(1)} all-to-all(bf16[16,64,128]{2,1,0:T(8,128)(2,1)S(1)} %broadcast_in_dim.8), channel_id=1, replica_groups={{0,16,32,48,128,144,160,176,256,272,288,304,384,400,416,432},{8,24,40,5..., dimensions={0} | all-to-all | bytes 524288 | tf_op jit(solution)/shard_map/all_to_all | solution.py:38
  109.3 1.9 %collective-permute-start.8 = (bf16[1024,128]{1,0:T(8,128)(2,1)S(1)}, bf16[1024,128]{1,0:T(8,128)(2,1)S(1)}, u32[]{:S(2)}, u32[]{:S(2)}) collective-permute-start(bf16[1024,128]{1,0:T(8,128)(2,1)S(1)} %bitcast.9), channel_id=1, source_target_pairs={{0,504},{8,448},{16,456},{24,464},{32,472},{40,480},{48,488},{56,4... | collective-permute-start | bytes 786440 | tf_op jit(solution)/shard_map/ppermute | solution.py:25
  111.2 2.7 %collective-permute-start.7 = (bf16[1024,128]{1,0:T(8,128)(2,1)S(1)}, bf16[1024,128]{1,0:T(8,128)(2,1)S(1)}, u32[]{:S(2)}, u32[]{:S(2)}) collective-permute-start(bf16[1024,128]{1,0:T(8,128)(2,1)S(1)} %bitcast.10), channel_id=1, source_target_pairs={{0,64},{8,72},{16,80},{24,88},{32,96},{40,104},{48,112},{56,120},{... | collective-permute-start | bytes 786440 | tf_op jit(solution)/shard_map/ppermute | solution.py:25
  114.0 3.7 %collective-permute-start.6 = (bf16[1024,128]{1,0:T(8,128)(2,1)S(1)}, bf16[1024,128]{1,0:T(8,128)(2,1)S(1)}, u32[]{:S(2)}, u32[]{:S(2)}) collective-permute-start(bf16[1024,128]{1,0:T(8,128)(2,1)S(1)} %bitcast.11), channel_id=1, source_target_pairs={{0,8},{8,16},{16,24},{24,32},{32,40},{40,48},{48,56},{56,0},{64,72... | collective-permute-start | bytes 786440 | tf_op jit(solution)/shard_map/ppermute | solution.py:25
  117.7 1.8 %collective-permute-done.7.refs_2_ = bf16[1024,128]{1,0:T(8,128)(2,1)S(1)} collective-permute-done((bf16[1024,128]{1,0:T(8,128)(2,1)S(1)}, bf16[1024,128]{1,0:T(8,128)(2,1)S(1)}, u32[]{:S(2)}, u32[]{:S(2)}) %collective-permute-start.7) | collective-permute-done | bytes 262176 | tf_op jit(solution)/shard_map/ppermute | solution.py:25
  119.6 2.9 %collective-permute-done.6.refs_1_ = bf16[1024,128]{1,0:T(8,128)(2,1)S(1)} collective-permute-done((bf16[1024,128]{1,0:T(8,128)(2,1)S(1)}, bf16[1024,128]{1,0:T(8,128)(2,1)S(1)}, u32[]{:S(2)}, u32[]{:S(2)}) %collective-permute-start.6) | collective-permute-done | bytes 262176 | tf_op jit(solution)/shard_map/ppermute | solution.py:25
  122.4 2.0 %shard_map.89 = bf16[8,32,256]{2,1,0:T(8,128)(2,1)S(1)} custom-call(s32[8]{0:T(128)S(1)} %pad_add_fusion.place_ref, bf16[2048,256]{1,0:T(8,128)(2,1)S(1)} %copy-done, bf16[1024,128]{1,0:T(8,128)(2,1)S(1)} %bitcast.12, bf16[1024,128]{1,0:T(8,128)(2,1)S(1)} %collective-permute-done.6.refs_1_, bf16[1024,128]{1,0:T(8,128)(2,1)S(1)} %collective-permute-done.7.refs_2_, ...), custom_call_target="tpu_custom_call" | custom-call | flops 268435456 | tf_op jit(solution)/shard_map/pallas_call | solution.py:51
  124.5 17.2 %all_to_all.23.got_ref = bf16[8,32,256]{2,1,0:T(8,128)(2,1)S(1)} all-to-all(bf16[8,32,256]{2,1,0:T(8,128)(2,1)S(1)} %shard_map.89), channel_id=1, replica_groups=mesh['ctx'=64,'kvh'=8] {'kvh'}, dimensions={0} | all-to-all | bytes 262144 | tf_op jit(solution)/shard_map/all_to_all | solution.py:328
  (27 shorter events, 4.1 us)
Async XLA Ops:
  0.0 35.7 %copy-start.1 = (bf16[2048,1,128]{2,0,1:T(8,128)(2,1)S(1)}, bf16[2048,1,128]{2,0,1:T(8,128)(2,1)}, u32[]{:S(2)}) copy-start(bf16[2048,1,128]{2,0,1:T(8,128)(2,1)} %param.9) | copy-start | bytes 1572868
  29.2 14.0 %collective-permute-start = (bf16[1024,128]{1,0:T(8,128)(2,1)S(1)}, bf16[1024,128]{1,0:T(8,128)(2,1)S(1)}, u32[]{:S(2)}, u32[]{:S(2)}) collective-permute-start(bf16[1024,128]{1,0:T(8,128)(2,1)S(1)} %bitcast.15), channel_id=1, source_target_pairs={{0,8},{8,16},{16,24},{24,32},{32,40},{40,48},{48,56},{56,0},{64,72... | collective-permute-start | bytes 786440 | tf_op jit(solution)/shard_map/ppermute | solution.py:25
  33.6 0.7 copy-start.4
  34.2 0.7 copy-start.5
  34.9 0.7 copy-start.3
  35.7 1.0 copy-start.2
  37.3 19.9 %collective-permute-start.4 = (bf16[1024,128]{1,0:T(8,128)(2,1)S(1)}, bf16[1024,128]{1,0:T(8,128)(2,1)S(1)}, u32[]{:S(2)}, u32[]{:S(2)}) collective-permute-start(bf16[1024,128]{1,0:T(8,128)(2,1)S(1)} %bitcast.16), channel_id=1, source_target_pairs={{0,504},{8,448},{16,456},{24,464},{32,472},{40,480},{48,488},{56,4... | collective-permute-start | bytes 786440 | tf_op jit(solution)/shard_map/ppermute | solution.py:25
  39.7 9.9 %collective-permute-start.2 = (bf16[1024,128]{1,0:T(8,128)(2,1)S(1)}, bf16[1024,128]{1,0:T(8,128)(2,1)S(1)}, u32[]{:S(2)}, u32[]{:S(2)}) collective-permute-start(bf16[1024,128]{1,0:T(8,128)(2,1)S(1)} %bitcast.17), channel_id=1, source_target_pairs={{0,64},{8,72},{16,80},{24,88},{32,96},{40,104},{48,112},{56,120},{... | collective-permute-start | bytes 786440 | tf_op jit(solution)/shard_map/ppermute | solution.py:25
  47.6 21.5 %collective-permute-start.1 = (bf16[1056,128]{1,0:T(8,128)(2,1)S(1)}, bf16[1056,128]{1,0:T(8,128)(2,1)S(1)}, u32[]{:S(2)}, u32[]{:S(2)}) collective-permute-start(bf16[1056,128]{1,0:T(8,128)(2,1)S(1)} %shard_map.84), channel_id=1, source_target_pairs={{0,56},{8,0},{16,8},{24,16},{32,24},{40,32},{48,40},{56,48},{64,12... | collective-permute-start | bytes 811016 | tf_op jit(solution)/shard_map/ppermute | solution.py:25
  53.9 15.2 %collective-permute-start.3 = (bf16[1056,128]{1,0:T(8,128)(2,1)S(1)}, bf16[1056,128]{1,0:T(8,128)(2,1)S(1)}, u32[]{:S(2)}, u32[]{:S(2)}) collective-permute-start(bf16[1056,128]{1,0:T(8,128)(2,1)S(1)} %shard_map.85), channel_id=1, source_target_pairs={{0,448},{8,456},{16,464},{24,472},{32,480},{40,488},{48,496},{56,5... | collective-permute-start | bytes 811016 | tf_op jit(solution)/shard_map/ppermute | solution.py:25
  61.6 10.5 %collective-permute-start.5 = (bf16[1056,128]{1,0:T(8,128)(2,1)S(1)}, bf16[1056,128]{1,0:T(8,128)(2,1)S(1)}, u32[]{:S(2)}, u32[]{:S(2)}) collective-permute-start(bf16[1056,128]{1,0:T(8,128)(2,1)S(1)} %shard_map.86), channel_id=1, source_target_pairs={{0,72},{8,80},{16,88},{24,96},{32,104},{40,112},{48,120},{56,64},{... | collective-permute-start | bytes 811016 | tf_op jit(solution)/shard_map/ppermute | solution.py:25
  72.8 49.7 %copy-start = (bf16[2048,256]{1,0:T(8,128)(2,1)S(1)}, bf16[2048,256]{1,0:T(8,128)(2,1)}, u32[]{:S(2)}) copy-start(bf16[2048,256]{1,0:T(8,128)(2,1)} %w_ref.1) | copy-start | bytes 3145732
  109.3 8.4 %collective-permute-start.8 = (bf16[1024,128]{1,0:T(8,128)(2,1)S(1)}, bf16[1024,128]{1,0:T(8,128)(2,1)S(1)}, u32[]{:S(2)}, u32[]{:S(2)}) collective-permute-start(bf16[1024,128]{1,0:T(8,128)(2,1)S(1)} %bitcast.9), channel_id=1, source_target_pairs={{0,504},{8,448},{16,456},{24,464},{32,472},{40,480},{48,488},{56,4... | collective-permute-start | bytes 786440 | tf_op jit(solution)/shard_map/ppermute | solution.py:25
  111.2 8.3 %collective-permute-start.7 = (bf16[1024,128]{1,0:T(8,128)(2,1)S(1)}, bf16[1024,128]{1,0:T(8,128)(2,1)S(1)}, u32[]{:S(2)}, u32[]{:S(2)}) collective-permute-start(bf16[1024,128]{1,0:T(8,128)(2,1)S(1)} %bitcast.10), channel_id=1, source_target_pairs={{0,64},{8,72},{16,80},{24,88},{32,96},{40,104},{48,112},{56,120},{... | collective-permute-start | bytes 786440 | tf_op jit(solution)/shard_map/ppermute | solution.py:25
  114.0 8.5 %collective-permute-start.6 = (bf16[1024,128]{1,0:T(8,128)(2,1)S(1)}, bf16[1024,128]{1,0:T(8,128)(2,1)S(1)}, u32[]{:S(2)}, u32[]{:S(2)}) collective-permute-start(bf16[1024,128]{1,0:T(8,128)(2,1)S(1)} %bitcast.11), channel_id=1, source_target_pairs={{0,8},{8,16},{16,24},{24,32},{32,40},{40,48},{48,56},{56,0},{64,72... | collective-permute-start | bytes 786440 | tf_op jit(solution)/shard_map/ppermute | solution.py:25

commit v2 on v0

v2 whole, which is shorter than its diff:
```python
import jax
import jax.numpy as jnp
from jax import lax
from jax.experimental import pallas as pl
from jax.experimental.pallas import tpu as pltpu
from jax.sharding import PartitionSpec as P

BF = jnp.bfloat16
F32 = jnp.float32
LOG2E = 1.4426950408889634
LIMIT = 48 * 1024 * 1024
HUGE = 2.0**100


def call(body, out_shape, flops=0, moved=0, scratch=(), smem=0, args=()):
    vmem = pl.BlockSpec(memory_space=pltpu.VMEM)
    scalars = pl.BlockSpec(memory_space=pltpu.SMEM)
    specs = [scalars] * smem + [vmem] * (len(args) - smem)
    return pl.pallas_call(
        body,
        out_shape=out_shape,
        in_specs=specs,
        out_specs=jax.tree.map(lambda _: vmem, out_shape),
        scratch_shapes=list(scratch),
        compiler_params=pltpu.CompilerParams(vmem_limit_bytes=LIMIT),
        cost_estimate=pl.CostEstimate(flops=flops, bytes_accessed=moved, transcendentals=0),
    )(*args)


def copies(value, count):
    return jnp.broadcast_to(value[None], (count,) + value.shape)


def prepare_body(live_ref, k_ref, v_ref, fk_ref, fv_ref, ka_ref, vt_ref):
    live = live_ref[0]
    slots, width = k_ref.shape
    fresh = fk_ref.shape[0]
    step = 256
    first = k_ref[0:16, :].astype(F32)[0:1, :]
    for at in range(0, slots, step):
        alive = lax.broadcasted_iota(jnp.int32, (step, width), 0) + at < live
        keys = jnp.where(alive, k_ref[at : at + step, :].astype(F32), first)
        ka_ref[at : at + step, :] = keys.astype(BF)
        vals = jnp.where(alive, v_ref[at : at + step, :].astype(F32), 0.0)
        vt_ref[0:width, at : at + step] = vals.T.astype(BF)
        flags = lax.broadcasted_iota(jnp.int32, (16, step), 1) + at < live
        vt_ref[width:, at : at + step] = flags.astype(F32).astype(BF)
    keys = jnp.concatenate([fk_ref[...].astype(F32), jnp.zeros((16 - fresh, width), F32)], 0)
    ka_ref[slots:, :] = keys.astype(BF)
    vals = jnp.concatenate([fv_ref[...].astype(F32), jnp.zeros((128 - fresh, width), F32)], 0)
    vt_ref[0:width, slots:] = vals.T.astype(BF)
    flags = lax.broadcasted_iota(jnp.int32, (16, 128), 1) < fresh
    vt_ref[width:, slots:] = flags.astype(F32).astype(BF)


def prepare(live, keys, vals, fresh_k, fresh_v):
    slots, width = keys.shape
    out = [
        jax.ShapeDtypeStruct((slots + 16, width), BF),
        jax.ShapeDtypeStruct((width + 16, slots + 128), BF),
    ]
    return call(prepare_body, out, smem=1, args=(live, keys, vals, fresh_k, fresh_v))


def three(value):
    parts = []
    for _ in range(3):
        top = value.astype(BF).astype(F32)
        parts.append(top)
        value = value - top
    return parts


def attend_body(me_ref, seg_ref, ka_ref, vt_ref, q_ref, o_ref, worst_ref):
    keys, width = ka_ref.shape
    slots = keys - 16
    rows = 256
    heads = 16
    fresh = 4
    pieces = q_ref.shape[0] // rows
    factor = LOG2E / width**0.5
    first = fresh * me_ref[0]
    line = lax.broadcasted_iota(jnp.int32, (16, rows), 0)
    never = 1 << 30
    opens = jnp.where(line < fresh, line + first, never)
    ends = jnp.full((16, rows), never, jnp.int32)
    seg = seg_ref[...]
    spot = lax.broadcasted_iota(jnp.int32, seg.shape, 0) * 128 + lax.broadcasted_iota(
        jnp.int32, seg.shape, 1
    )
    for j in range(fresh):
        own = jnp.sum(jnp.where(spot == first + j, seg, 0))
        ends = jnp.where(line == j, jnp.sum((seg <= own).astype(jnp.int32)), ends)
    token0 = lax.broadcasted_iota(jnp.int32, (16, rows), 1) // heads
    cuts = [(at, 256) for at in range(0, slots, 256)] + [(slots, 16)]

    def score(query, cut, i):
        at, deep = cut
        part = jnp.dot(ka_ref[at : at + deep, :], query, preferred_element_type=F32)
        if deep == 16:
            token = token0 + i * (rows // heads)
            part = jnp.where((token >= opens) & (token < ends), part, -jnp.inf)
        return part

    def most(part):
        return jnp.max(part, axis=0, keepdims=True)

    def piece(i, exact):
        at = pl.multiple_of(i * rows, rows)
        query = q_ref[pl.ds(at, rows), :].astype(F32).T.astype(BF)
        start = score(query, cuts[0], i)
        peak = most(start)
        if exact:
            for cut in cuts[1:]:
                peak = jnp.maximum(peak, most(score(query, cut, i)))
        total = None
        for n, cut in enumerate(cuts):
            part = start if n == 0 else score(query, cut, i)
            weight = jnp.exp2((part - peak) * factor).astype(BF)
            wide = cut[1]
            if wide == 16:
                weight = jnp.concatenate([weight, jnp.zeros((112, rows), BF)], 0)
                wide = 128
            add = jnp.dot(vt_ref[:, cut[0] : cut[0] + wide], weight, preferred_element_type=F32)
            total = add if total is None else total + add
        count = total[width : width + 1, :]
        out = (total[0:width, :] * (1.0 / count)).T.astype(BF)
        parts = three(peak * factor + jnp.log(count) * LOG2E)
        empty = jnp.zeros((5, 128), F32)
        for j in range(rows // 64):
            to = i * (rows // 64) + j
            lanes = slice(128 * (j // 2), 128 * (j // 2) + 128)
            o_ref[to, 0:64, :] = out[64 * j : 64 * j + 64, :]
            tail = jnp.concatenate([p[:, lanes] for p in parts] + [empty], 0)
            o_ref[to, 64:72, :] = tail.astype(BF)
        return count

    worst_ref[...] = jnp.zeros(worst_ref.shape, F32)

    def quick(i, carry):
        counts = jnp.maximum(piece(2 * i, False), piece(2 * i + 1, False))
        worst_ref[0:1, :] = jnp.maximum(worst_ref[0:1, :], counts)
        return carry

    lax.fori_loop(0, pieces // 2, quick, 0)

    @pl.when(jnp.logical_not(jnp.max(worst_ref[0:1, :]) < HUGE))
    def _():
        def slow(i, carry):
            piece(i, True)
            return carry

        lax.fori_loop(0, pieces, slow, 0)


def attend(me, seg, ka, vt, query):
    rows, width = query.shape
    return call(
        attend_body,
        jax.ShapeDtypeStruct((rows // 64, 72, width), BF),
        flops=8 * rows * ka.shape[0] * 256,
        moved=(ka.size + vt.size + 2 * query.size) * 2,
        scratch=[pltpu.VMEM((8, 256), F32)],
        smem=1,
        args=(me, seg, ka, vt, query),
    )


def merge_body(me_ref, got_ref, out_ref, logs):
    parts = got_ref.shape[0]
    for c in range(parts):
        tail = got_ref[c, 64:72, :].astype(F32)
        logs[c : c + 1, :] = tail[0:1] + tail[1:2] + tail[2:3]
    lse = logs[...]
    lse = jnp.where(lax.rem(me_ref[0], 2) == 1, pltpu.roll(lse, 64, 1), lse)
    weight = jnp.exp2(lse - jnp.max(lse, axis=0, keepdims=True))
    weight = weight / jnp.sum(weight, axis=0, keepdims=True)
    eye = lax.broadcasted_iota(jnp.int32, (64, 128), 0) == lax.broadcasted_iota(
        jnp.int32, (64, 128), 1
    )
    total = None
    for c in range(parts):
        column = jnp.sum(jnp.where(eye, weight[c : c + 1, :], 0.0), axis=1, keepdims=True)
        term = got_ref[c, 0:64, :].astype(F32) * column
        total = term if total is None else total + term
    out_ref[...] = total.astype(BF)


def merge(me, got):
    return call(
        merge_body,
        jax.ShapeDtypeStruct((64, got.shape[2]), BF),
        scratch=[pltpu.VMEM((got.shape[0], 128), F32)],
        smem=1,
        args=(me, got),
    )


def project_body(w_ref, in_ref, out_ref, rows):
    heads = w_ref.shape[0] // in_ref.shape[1]
    tokens = in_ref.shape[0] // heads
    rows[...] = in_ref[...].astype(F32)
    left = [rows[pl.ds(h, tokens, stride=heads), :].astype(BF) for h in range(heads)]
    mixed = jnp.dot(jnp.concatenate(left, 1), w_ref[...], preferred_element_type=F32)
    out_ref[...] = mixed.astype(BF)


def project(weight, value):
    deep, cols = weight.shape
    tokens = value.size // deep
    return call(
        project_body,
        jax.ShapeDtypeStruct((tokens, cols), BF),
        flops=2 * tokens * deep * cols,
        scratch=[pltpu.VMEM(value.shape, F32)],
        args=(weight, value),
    )


def final_body(got_ref, out_ref):
    total = got_ref[0].astype(F32)
    for i in range(1, got_ref.shape[0]):
        total = total + got_ref[i].astype(F32)
    out_ref[...] = total.astype(BF)


def local(queries, cache_keys, cache_values, new_keys, new_values, cache_len, segment, out_weight):
    me = lax.axis_index("ctx").reshape(1).astype(jnp.int32)
    ring = lax.axis_size("ctx")
    block, heads, width = queries.shape
    own = copies(queries.reshape(block * heads, width), ring)
    asked = lax.all_to_all(own, "ctx", 0, 0, tiled=True).reshape(-1, width)
    ka, vt = prepare(
        cache_len,
        cache_keys[:, 0, :],
        cache_values[:, 0, :],
        new_keys[:, 0, :],
        new_values[:, 0, :],
    )
    partial = attend(me, segment.reshape(-1, 128), ka, vt, asked)
    own = merge(me, lax.all_to_all(partial, "ctx", 0, 0, tiled=True))
    every = lax.all_to_all(copies(own, ring), "ctx", 0, 0, tiled=True).reshape(-1, width)
    mixed = project(out_weight, every)
    mixed = mixed.reshape(lax.axis_size("kvh"), -1, mixed.shape[1])
    got = lax.all_to_all(mixed, "kvh", 0, 0, tiled=True)
    return call(final_body, jax.ShapeDtypeStruct(got.shape[1:], BF), args=(got,))


def solution(mesh):
    in_specs = (
        P("ctx", "kvh", None),
        P("ctx", "kvh", None),
        P("ctx", "kvh", None),
        P("ctx", "kvh", None),
        P("ctx", "kvh", None),
        P("ctx"),
        P(),
        P("kvh", "ctx"),
    )
    out_specs = P("kvh", "ctx")
    return jax.shard_map(local, mesh=mesh, in_specs=in_specs, out_specs=out_specs, check_vma=False)
```

time: 516 us -> 155 us (0.30)
  waiting for transfers between devices: 265 us -> 25.7 us
  local copies, waits for them, and re-layouts: 96.3 us -> 2.21 us
  blocking collectives: 0 us -> 87.4 us
  matrix products: 70.9 us -> 0 us
  loops' own time: 27.1 us -> 0 us
  other arithmetic: 21 us -> 0 us
  Pallas kernels: 0 us -> 20.8 us
  between operations: 13.2 us -> 0.74 us
    all_gather x2 -> x0, waiting for transfers between devices: 170 us -> none  [the longest x1 85.4 us: local(): everyone = lax.all_gather(queries, 'ctx', axis=0, tiled=True)]
    all_to_all x0 -> x3, blocking collectives: none -> 87.4 us  [the longest x1 38.1 us: local(): own = merge(me, lax.all_to_all(partial, 'ctx', 0, 0, tiled=True))]
    dynamic_update_slice x48 -> x0, local copies, waits for them, and re-layouts: 76.2 us -> none  [shard_part(): lax.map(one_head, jnp.arange(count_heads, dtype=jnp.int32))]
    dot_general x65 -> x0, matrix products: 70.9 us -> none  [the longest x16 25.6 us: one_head(): lax.dot_general(query, keys_c, dims, preferred_element_type=jnp.float32)]
    reduce_scatter x1 -> x0, waiting for transfers between devices: 35.8 us -> none  [local(): lax.psum_scatter(jnp.dot(every_row, out_weight, preferred_element_type=jn...]
    all_to_all x3 -> x1, waiting for transfers between devices: 59.3 us -> 25.7 us  [local(): asked = lax.all_to_all(own, 'ctx', 0, 0, tiled=True).reshape(-1, width)]
    another operation x1 -> x0, loops' own time: 27.1 us -> none  [shard_part(): lax.map(one_head, jnp.arange(count_heads, dtype=jnp.int32))]
    pallas_call x0 -> x5, Pallas kernels: none -> 20.8 us  [call(): pl.pallas_call(body, out_shape=out_shape, in_specs=specs, out_specs=jax.t...]
  transfers between devices with their start and end apart: 6 -> 1, of which waited for: 6 -> 1; matrix products, arithmetic and copies ran while one was open for 1% -> 0% of each run, Pallas kernels for 0% -> 0%
where the time goes in v2:
time: 155 us; the launch traced here: 154 us
  blocking collectives  87.4 us (56%)
  waiting for transfers between devices  25.7 us (17%)
  Pallas kernels  20.8 us (13%)
  starting transfers between devices  17.3 us (11%)
  local copies, waits for them, and re-layouts  2.21 us (1%)
    all_to_all x1, blocking collectives, local(): own = merge(me, lax.all_to_all(partial, 'ctx', 0, 0, tiled=True))  38.1 us
    all_to_all x1, blocking collectives, local(): lax.all_to_all(copies(own, ring), 'ctx', 0, 0, tiled=True)  35.9 us
    all_to_all x1, waiting for transfers between devices, local(): asked = lax.all_to_all(own, 'ctx', 0, 0, tiled=True).reshape(-1, width)  25.7 us
    pallas_call x5, Pallas kernels, call(): pl.pallas_call(body, out_shape=out_shape, in_specs=specs, out_specs=jax.t...  20.8 us
    all_to_all x1, starting transfers between devices, local(): asked = lax.all_to_all(own, 'ctx', 0, 0, tiled=True).reshape(-1, width)  17.3 us
    all_to_all x1, blocking collectives, local(): got = lax.all_to_all(mixed, 'kvh', 0, 0, tiled=True)  13.3 us
  transfers between devices with their start and end apart: 1, of which 1 were waited for; matrix products, arithmetic and copies ran while one was open for 0% of the time, Pallas kernels for 0%

profile of v2, /device:TPU:1, one launch (start us, length us, event | category | flops | bytes accessed | tf_op | source)
XLA Modules:
  0.0 154.1 jit_solution(2289726403290328515)
XLA Ops:
  0.0 1.9 %broadcast_in_dim.14 = bf16[64,64,128]{2,1,0:T(8,128)(2,1)} broadcast(bf16[64,128]{1,0:T(8,128)(2,1)} %bitcast.18), dimensions={1,2} | broadcast | bytes 1064960 | tf_op jit(solution)/shard_map/broadcast_in_dim | solution.py:31
  1.9 0.0 copy-start.1
  1.9 0.0 copy-start.2
  1.9 0.0 copy-start.3
  1.9 0.0 copy-start.4
  1.9 0.0 copy-start.5
  2.0 17.3 %all-to-all-start = ((bf16[64,64,128]{2,1,0:T(8,128)(2,1)}), bf16[64,64,128]{2,1,0:T(8,128)(2,1)S(1)}, u32[]{:S(2)}, u32[]{:S(2)}) async-start(bf16[64,64,128]{2,1,0:T(8,128)(2,1)} %broadcast_in_dim.14), calls=%async_computation | async-start | bytes 2097152 | tf_op jit(solution)/shard_map/all_to_all | solution.py:232
  19.9 0.0 copy-done.1
  19.9 0.0 copy-done.2
  19.9 0.0 copy-done.3
  19.9 0.0 copy-done.4
  19.9 0.4 shard_map.82
  20.3 25.7 %all-to-all-done = bf16[64,64,128]{2,1,0:T(8,128)(2,1)S(1)} async-done(((bf16[64,64,128]{2,1,0:T(8,128)(2,1)}), bf16[64,64,128]{2,1,0:T(8,128)(2,1)S(1)}, u32[]{:S(2)}, u32[]{:S(2)}) %all-to-all-start) | async-done | bytes 1048608 | tf_op jit(solution)/shard_map/all_to_all | solution.py:232
  46.0 0.0 copy-done.5
  46.0 18.2 %shard_map.83 = bf16[64,72,128]{2,1,0:T(8,128)(2,1)S(1)} custom-call(s32[1]{0:T(128)} %bitcast.me_ref, s32[2,128]{1,0:T(2,128)S(1)} %bitcast.17, bf16[2064,128]{1,0:T(8,128)(2,1)S(1)} %get-tuple-element.7.ka_ref, bf16[144,2176]{1,0:T(8,128)(2,1)S(1)} %get-tuple-element.8.vt_ref, bf16[4096,128]{1,0:T(8,128)(2,1)S(1)} %bitcast.11), custom_call_target="tpu_custom_call" | custom-call | flops 17314086912 | bytes 3252224 | tf_op jit(solution)/shard_map/pallas_call | solution.py:19
  64.2 38.1 %all_to_all.20.got_ref = bf16[64,72,128]{2,1,0:T(8,128)(2,1)S(1)} all-to-all(bf16[64,72,128]{2,1,0:T(8,128)(2,1)S(1)} %shard_map.83), channel_id=1, replica_groups=mesh['ctx'=64,'kvh'=8] {'ctx'}, dimensions={0} | all-to-all | bytes 2359296 | tf_op jit(solution)/shard_map/all_to_all | solution.py:241
  102.3 0.8 shard_map.84
  103.1 0.2 broadcast_in_dim.15
  103.4 0.0 copy-start
  103.4 35.9 %all_to_all.21 = bf16[64,64,128]{2,1,0:T(8,128)(2,1)S(1)} all-to-all(bf16[64,64,128]{2,1,0:T(8,128)(2,1)S(1)} %broadcast_in_dim.15), channel_id=1, replica_groups=mesh['ctx'=64,'kvh'=8] {'ctx'}, dimensions={0} | all-to-all | bytes 2097152 | tf_op jit(solution)/shard_map/all_to_all | solution.py:242
  139.3 0.0 copy-done
  139.3 0.8 shard_map.85
  140.1 13.3 %all_to_all.22.got_ref = bf16[8,32,256]{2,1,0:T(8,128)(2,1)S(1)} all-to-all(bf16[8,32,256]{2,1,0:T(8,128)(2,1)S(1)} %bitcast.12), channel_id=1, replica_groups=mesh['ctx'=64,'kvh'=8] {'kvh'}, dimensions={0} | all-to-all | bytes 262144 | tf_op jit(solution)/shard_map/all_to_all | solution.py:245
  153.4 0.6 shard_map.86
Async XLA Ops:
  1.9 18.0 %copy-start.1 = (bf16[2048,1,128]{2,0,1:T(8,128)(2,1)S(1)}, bf16[2048,1,128]{2,0,1:T(8,128)(2,1)}, u32[]{:S(2)}) copy-start(bf16[2048,1,128]{2,0,1:T(8,128)(2,1)} %param.9) | copy-start | bytes 1572868
  1.9 18.0 %copy-start.2 = (bf16[2048,1,128]{2,0,1:T(8,128)(2,1)S(1)}, bf16[2048,1,128]{2,0,1:T(8,128)(2,1)}, u32[]{:S(2)}) copy-start(bf16[2048,1,128]{2,0,1:T(8,128)(2,1)} %param.10) | copy-start | bytes 1572868
  1.9 18.0 %copy-start.3 = (bf16[4,1,128]{2,0,1:T(4,128)(2,1)S(1)}, bf16[4,1,128]{2,0,1:T(4,128)(2,1)}, u32[]{:S(2)}) copy-start(bf16[4,1,128]{2,0,1:T(4,128)(2,1)} %param.11) | copy-start | bytes 3076
  1.9 18.0 %copy-start.4 = (bf16[4,1,128]{2,0,1:T(4,128)(2,1)S(1)}, bf16[4,1,128]{2,0,1:T(4,128)(2,1)}, u32[]{:S(2)}) copy-start(bf16[4,1,128]{2,0,1:T(4,128)(2,1)} %param.12) | copy-start | bytes 3076
  1.9 44.0 %copy-start.5 = (s32[256]{0:T(256)S(1)}, s32[256]{0:T(256)}, u32[]{:S(2)}) copy-start(s32[256]{0:T(256)} %param.14) | copy-start | bytes 3076
  2.0 44.0 %all-to-all-start = ((bf16[64,64,128]{2,1,0:T(8,128)(2,1)}), bf16[64,64,128]{2,1,0:T(8,128)(2,1)S(1)}, u32[]{:S(2)}, u32[]{:S(2)}) async-start(bf16[64,64,128]{2,1,0:T(8,128)(2,1)} %broadcast_in_dim.14), calls=%async_computation | async-start | bytes 2097152 | tf_op jit(solution)/shard_map/all_to_all | solution.py:232
  103.4 35.9 %copy-start = (bf16[2048,256]{1,0:T(8,128)(2,1)S(1)}, bf16[2048,256]{1,0:T(8,128)(2,1)}, u32[]{:S(2)}) copy-start(bf16[2048,256]{1,0:T(8,128)(2,1)} %w_ref.1) | copy-start | bytes 3145732

commit v3 on v2

v3 whole, which is shorter than its diff:
```python
import jax
import jax.numpy as jnp
from jax import lax
from jax.experimental import pallas as pl
from jax.experimental.pallas import tpu as pltpu
from jax.sharding import PartitionSpec as P

BF = jnp.bfloat16
F32 = jnp.float32
LOG2E = 1.4426950408889634
LIMIT = 48 * 1024 * 1024
HUGE = 2.0**100
SIDE = 8
STEPS = ((0, 0), (1, 0), (-1, 0), (0, 1))
BLOCK = 512


def shift(value, step):
    pairs = []
    for y in range(SIDE):
        for z in range(SIDE):
            to = ((y + step[0]) % SIDE) * SIDE + (z + step[1]) % SIDE
            pairs.append((y * SIDE + z, to))
    return lax.ppermute(value, "ctx", pairs)


def coset(y, z):
    return lax.rem(y + 2 * z + 4 * SIDE, 4)


def member_y(which, i):
    return lax.rem(which + 2 * (i // 2), 4) + 4 * (i % 2)


def cosets():
    return [
        [((v + 2 * z) % 4 + 4 * b) * SIDE + z for z in range(SIDE) for b in range(2)]
        for v in range(4)
    ]


def exchange(value):
    return lax.all_to_all(value, "ctx", 0, 0, axis_index_groups=cosets(), tiled=True)


def share(value):
    copies = jnp.broadcast_to(value[None], (16,) + value.shape)
    return exchange(copies).reshape(16 * value.shape[0], value.shape[1])


def call(body, out_shape, flops=0, moved=0, scratch=(), smem=0, args=()):
    vmem = pl.BlockSpec(memory_space=pltpu.VMEM)
    scalars = pl.BlockSpec(memory_space=pltpu.SMEM)
    specs = [scalars] * smem + [vmem] * (len(args) - smem)
    return pl.pallas_call(
        body,
        out_shape=out_shape,
        in_specs=specs,
        out_specs=jax.tree.map(lambda _: vmem, out_shape),
        scratch_shapes=list(scratch),
        compiler_params=pltpu.CompilerParams(vmem_limit_bytes=LIMIT),
        cost_estimate=pl.CostEstimate(flops=flops, bytes_accessed=moved, transcendentals=0),
    )(*args)


def pack_body(live_ref, k_ref, v_ref, fk_ref, fv_ref, out_ref):
    live = live_ref[0]
    slots, width = k_ref.shape
    fresh = fk_ref.shape[0]
    span = slots + 16
    step = 256
    first = k_ref[0:16, :].astype(F32)[0:1, :]
    for at in range(0, slots, step):
        alive = lax.broadcasted_iota(jnp.int32, (step, width), 0) + at < live
        keys = jnp.where(alive, k_ref[at : at + step, :].astype(F32), first)
        out_ref[at : at + step, :] = keys.astype(BF)
        vals = jnp.where(alive, v_ref[at : at + step, :].astype(F32), 0.0)
        out_ref[span + at : span + at + step, :] = vals.astype(BF)
    pad = jnp.zeros((16 - fresh, width), F32)
    for at, ref in ((slots, fk_ref), (span + slots, fv_ref)):
        out_ref[at : at + 16, :] = jnp.concatenate([ref[...].astype(F32), pad], 0).astype(BF)
    line = lax.broadcasted_iota(jnp.int32, (16, width), 0)
    size = jnp.where(line == 0, live // 64, jnp.where(line == 1, lax.rem(live, 64), 0))
    out_ref[2 * span :, :] = size.astype(F32).astype(BF)


def pack(live, keys, vals, fresh_k, fresh_v):
    slots, width = keys.shape
    out = jax.ShapeDtypeStruct((2 * (slots + 16) + 16, width), BF)
    return call(pack_body, out, smem=1, args=(live, keys, vals, fresh_k, fresh_v))


def three(value):
    parts = []
    for _ in range(3):
        top = value.astype(BF).astype(F32)
        parts.append(top)
        value = value - top
    return parts


def attend_body(place_ref, seg_ref, q_ref, *refs):
    shards, (o_ref, peak_ref, sum_ref) = refs[:4], refs[4:]
    rows, width = q_ref.shape
    span = (shards[0].shape[0] - 16) // 2
    slots = span - 16
    heads = 16
    fresh = 4
    factor = LOG2E / width**0.5
    y, z = place_ref[0], place_ref[1]
    dims = (((1,), (1,)), ((), ()))
    lives = []
    for ref in shards:
        size = ref[2 * span :, :].astype(F32)
        lives.append(jnp.max(64.0 * size[0:1] + size[1:2]).astype(jnp.int32))

    def score(keys):
        return lax.dot_general(q_ref[...], keys, dims, preferred_element_type=F32)

    def weigh(part):
        peak = peak_ref[...]
        lanes = [part[:, at : at + 128] - peak for at in range(0, part.shape[1], 128)]
        lanes = [jnp.exp2(lane * factor).astype(BF) for lane in lanes]
        return jnp.concatenate(lanes, 1) if len(lanes) > 1 else lanes[0]

    def beside(vals, ones):
        return jnp.concatenate([vals, ones.astype(F32).astype(BF)], 1)

    def most(part):
        return jnp.broadcast_to(jnp.max(part, axis=1, keepdims=True), (rows, 128))

    seg = seg_ref[...]
    spot = lax.broadcasted_iota(jnp.int32, seg.shape, 0) * 128 + lax.broadcasted_iota(
        jnp.int32, seg.shape, 1
    )
    lane = lax.broadcasted_iota(jnp.int32, (8, 128), 1)
    never = 1 << 30
    opens = jnp.full((8, 128), never, jnp.int32)
    ends = jnp.full((8, 128), never, jnp.int32)
    for s, step in enumerate(STEPS):
        from_y = lax.rem(y + SIDE - step[0], SIDE)
        from_z = lax.rem(z + SIDE - step[1], SIDE)
        for j in range(fresh):
            token = fresh * (SIDE * from_y + from_z) + j
            own = jnp.sum(jnp.where(spot == token, seg, 0))
            here = lane == 16 * s + j
            opens = jnp.where(here, token, opens)
            ends = jnp.where(here, jnp.sum((seg <= own).astype(jnp.int32)), ends)
    opens, ends = opens[0:1], ends[0:1]

    def fresh_score():
        pad = jnp.zeros((64, width), BF)
        part = score(jnp.concatenate([r[slots:span, :] for r in shards] + [pad], 0))
        line = lax.broadcasted_iota(jnp.int32, (rows, 128), 0)
        member = line // 64
        token = 32 * member_y(coset(y, z), member) + 4 * (member // 2)
        token = token + lax.rem(line // heads, 4)
        return jnp.where((token >= opens) & (token < ends), part, -jnp.inf)

    def gather():
        pad = jnp.zeros((64, width), BF)
        vals = jnp.concatenate([r[span + slots : 2 * span, :] for r in shards] + [pad], 0)
        ones = lax.broadcasted_iota(jnp.int32, (128, 128), 0)
        ones = (lax.rem(ones, 16) < fresh) & (ones < 64)
        sum_ref[...] = jnp.dot(
            weigh(fresh_score()), beside(vals, ones), preferred_element_type=F32
        )
        for ref, live in zip(shards, lives):

            def step(n, carry, ref=ref, live=live):
                at = pl.multiple_of(n * BLOCK, BLOCK)
                keys = ref[pl.ds(at, BLOCK), :]
                vals = ref[pl.ds(pl.multiple_of(span + at, 16), BLOCK), :]
                ones = lax.broadcasted_iota(jnp.int32, (BLOCK, 128), 0) + at < live
                sum_ref[...] += jnp.dot(
                    weigh(score(keys)), beside(vals, ones), preferred_element_type=F32
                )
                return carry

            lax.fori_loop(0, (live + BLOCK - 1) // BLOCK, step, 0)

    peak_ref[...] = most(score(shards[0][0:256, :]))
    gather()

    @pl.when(jnp.logical_not(jnp.max(sum_ref[:, width:]) < HUGE))
    def _():
        peak_ref[...] = jnp.maximum(peak_ref[...], most(fresh_score()))
        for ref, live in zip(shards, lives):

            def step(n, carry, ref=ref):
                at = pl.multiple_of(n * BLOCK, BLOCK)
                part = score(ref[pl.ds(at, BLOCK), :])
                peak_ref[...] = jnp.maximum(peak_ref[...], most(part))
                return carry

            lax.fori_loop(0, (live + BLOCK - 1) // BLOCK, step, 0)
        gather()

    eye = lax.broadcasted_iota(jnp.int32, (128, 128), 0) == lax.broadcasted_iota(
        jnp.int32, (128, 128), 1
    )
    empty = jnp.zeros((5, 128), F32)
    for b in range(rows // 128):
        at = slice(128 * b, 128 * b + 128)
        count = sum_ref[at, width:]
        out = (sum_ref[at, 0:width] / count).astype(BF)
        lse = peak_ref[at, :] * factor + jnp.log(count) * LOG2E
        row = jnp.sum(jnp.where(eye, lse, 0.0), axis=0, keepdims=True)
        tail = jnp.concatenate(three(row) + [empty], 0).astype(BF)
        for j in range(2):
            o_ref[2 * b + j, 0:64, :] = out[64 * j : 64 * j + 64, :]
            o_ref[2 * b + j, 64:72, :] = tail


def attend(place, seg, query, shards):
    rows, width = query.shape
    keys = 4 * shards[0].shape[0] // 2
    return call(
        attend_body,
        jax.ShapeDtypeStruct((rows // 64, 72, width), BF),
        flops=8 * rows * keys * 256,
        moved=(4 * shards[0].size + 2 * query.size) * 2,
        scratch=[pltpu.VMEM((rows, 128), F32), pltpu.VMEM((rows, 2 * width), F32)],
        smem=1,
        args=(place, seg, query, *shards),
    )


def merge_body(place_ref, got_ref, out_ref, logs):
    parts = got_ref.shape[0]
    for c in range(parts):
        tail = got_ref[c, 64:72, :].astype(F32)
        logs[c : c + 1, :] = tail[0:1] + tail[1:2] + tail[2:3]
    lse = logs[...]
    lse = jnp.where(place_ref[0] // 4 == 1, pltpu.roll(lse, 64, 1), lse)
    weight = jnp.exp2(lse - jnp.max(lse, axis=0, keepdims=True))
    weight = weight / jnp.sum(weight, axis=0, keepdims=True)
    eye = lax.broadcasted_iota(jnp.int32, (64, 128), 0) == lax.broadcasted_iota(
        jnp.int32, (64, 128), 1
    )
    total = None
    for c in range(parts):
        column = jnp.sum(jnp.where(eye, weight[c : c + 1, :], 0.0), axis=1, keepdims=True)
        term = got_ref[c, 0:64, :].astype(F32) * column
        total = term if total is None else total + term
    out_ref[...] = total.astype(BF)


def merge(place, got):
    return call(
        merge_body,
        jax.ShapeDtypeStruct((64, got.shape[2]), BF),
        scratch=[pltpu.VMEM((got.shape[0], 128), F32)],
        smem=1,
        args=(place, got),
    )


def project_body(place_ref, w_ref, *refs):
    ins, out_ref, rows, placed = refs[:4], refs[4], refs[5], refs[6]
    heads = w_ref.shape[0] // ins[0].shape[1]
    tokens = ins[0].shape[0] // heads
    left = []
    for ref in ins:
        rows[...] = ref[...].astype(F32)
        parts = [rows[pl.ds(h, tokens, stride=heads), :].astype(BF) for h in range(heads)]
        left.append(jnp.concatenate(parts, 1))
    mixed = jnp.dot(jnp.concatenate(left, 0), w_ref[...], preferred_element_type=F32)
    for i, step in enumerate(STEPS):
        which = coset(place_ref[0] - step[0], place_ref[1] - step[1])
        for n in range(tokens // 4):
            to = SIDE * member_y(which, n) + n // 2
            placed[to] = mixed[i * tokens + 4 * n : i * tokens + 4 * n + 4, :]
    for k in range(out_ref.shape[0]):
        out_ref[k] = jnp.concatenate([placed[8 * k + n] for n in range(8)], 0).astype(BF)


def project(place, weight, ins):
    deep, cols = weight.shape
    rows, width = ins[0].shape
    tokens = 4 * rows * width // deep
    return call(
        project_body,
        jax.ShapeDtypeStruct((8, tokens // 8, cols), BF),
        flops=2 * tokens * deep * cols,
        scratch=[pltpu.VMEM((rows, width), F32), pltpu.VMEM((tokens // 4, 4, cols), F32)],
        smem=1,
        args=(place, weight, *ins),
    )


def final_body(got_ref, out_ref):
    total = got_ref[0].astype(F32)
    for i in range(1, got_ref.shape[0]):
        total = total + got_ref[i].astype(F32)
    out_ref[...] = total.astype(BF)


def local(queries, cache_keys, cache_values, new_keys, new_values, cache_len, segment, out_weight):
    me = lax.axis_index("ctx").astype(jnp.int32)
    place = jnp.stack([me // SIDE, me % SIDE])
    block, heads, width = queries.shape
    shard = pack(
        cache_len,
        cache_keys[:, 0, :],
        cache_values[:, 0, :],
        new_keys[:, 0, :],
        new_values[:, 0, :],
    )
    shards = [shard] + [shift(shard, step) for step in STEPS[1:]]
    asked = share(queries.reshape(block * heads, width))
    partial = attend(place, segment.reshape(-1, 128), asked, shards)
    own = merge(place, exchange(partial))
    mine = share(own)
    every = [mine] + [shift(mine, step) for step in STEPS[1:]]
    mixed = project(place, out_weight, every)
    got = lax.all_to_all(mixed, "kvh", 0, 0, tiled=True)
    return call(final_body, jax.ShapeDtypeStruct(got.shape[1:], BF), args=(got,))


def solution(mesh):
    in_specs = (
        P("ctx", "kvh", None),
        P("ctx", "kvh", None),
        P("ctx", "kvh", None),
        P("ctx", "kvh", None),
        P("ctx", "kvh", None),
        P("ctx"),
        P(),
        P("kvh", "ctx"),
    )
    out_specs = P("kvh", "ctx")
    return jax.shard_map(local, mesh=mesh, in_specs=in_specs, out_specs=out_specs, check_vma=False)
```

time: 155 us -> 135 us (0.87)
  blocking collectives: 87.4 us -> 53 us
  starting transfers between devices: 17.3 us -> 32.3 us
  Pallas kernels: 20.8 us -> 17.3 us
  local copies, waits for them, and re-layouts: 2.21 us -> 4.26 us
    all_to_all x2, blocking collectives: 74 us -> 35.8 us  [exchange(): lax.all_to_all(value, 'ctx', 0, 0, axis_index_groups=cosets(), tiled=True)]
    ppermute x0 -> x6, starting transfers between devices: none -> 19.5 us  [shift(): return lax.ppermute(value, 'ctx', pairs)]
    ppermute x0 -> x6, waiting for transfers between devices: none -> 4.96 us  [shift(): return lax.ppermute(value, 'ctx', pairs)]
    all_to_all x1, starting transfers between devices: 17.3 us -> 12.8 us  [exchange(): lax.all_to_all(value, 'ctx', 0, 0, axis_index_groups=cosets(), tiled=True)]
    all_to_all x1, blocking collectives: 13.3 us -> 17.2 us  [local(): got = lax.all_to_all(mixed, 'kvh', 0, 0, tiled=True)]
    all_to_all x1, waiting for transfers between devices: 25.7 us -> 22.1 us  [exchange(): lax.all_to_all(value, 'ctx', 0, 0, axis_index_groups=cosets(), tiled=True)]
    pallas_call x5, Pallas kernels: 20.8 us -> 17.3 us  [call(): pl.pallas_call(body, out_shape=out_shape, in_specs=specs, out_specs=jax.t...]
    unnamed x12 -> x14, local copies, waits for them, and re-layouts: 0.03 us -> 3.45 us
  transfers between devices with their start and end apart: 1 -> 7, of which waited for: 1 -> 4; matrix products, arithmetic and copies ran while one was open for 0% -> 1% of each run, Pallas kernels for 0% -> 0%
where the time goes in v3:
time: 135 us
  blocking collectives  53 us (39%)
  starting transfers between devices  32.3 us (24%)
  waiting for transfers between devices  27.1 us (20%)
  Pallas kernels  17.3 us (13%)
  local copies, waits for them, and re-layouts  4.26 us (3%)
    all_to_all x2, blocking collectives, exchange(): lax.all_to_all(value, 'ctx', 0, 0, axis_index_groups=cosets(), tiled=True)  35.8 us
    all_to_all x1, waiting for transfers between devices, exchange(): lax.all_to_all(value, 'ctx', 0, 0, axis_index_groups=cosets(), tiled=True)  22.1 us
    ppermute x6, starting transfers between devices, shift(): return lax.ppermute(value, 'ctx', pairs)  19.5 us
    pallas_call x5, Pallas kernels, call(): pl.pallas_call(body, out_shape=out_shape, in_specs=specs, out_specs=jax.t...  17.3 us
    all_to_all x1, blocking collectives, local(): got = lax.all_to_all(mixed, 'kvh', 0, 0, tiled=True)  17.2 us
    all_to_all x1, starting transfers between devices, exchange(): lax.all_to_all(value, 'ctx', 0, 0, axis_index_groups=cosets(), tiled=True)  12.8 us
    ppermute x6, waiting for transfers between devices, shift(): return lax.ppermute(value, 'ctx', pairs)  4.96 us
    unnamed x14, local copies, waits for them, and re-layouts  3.45 us
  transfers between devices with their start and end apart: 7, of which 4 were waited for; matrix products, arithmetic and copies ran while one was open for 1% of the time, Pallas kernels for 0%

profile of v3, /device:TPU:1, one launch (start us, length us, event | category | flops | bytes accessed | tf_op | source)
XLA Modules:
  0.0 134.8 jit_solution(14622587299043061493)
XLA Ops:
  0.7 1.0 copy-done.1
  1.7 1.0 copy-done.2
  2.7 0.7 copy-done.3
  3.4 0.7 copy-done.4
  4.1 0.3 shard_map.82.refs_0_
  4.4 4.8 %collective-permute-start.2 = (bf16[4144,128]{1,0:T(8,128)(2,1)S(1)}, bf16[4144,128]{1,0:T(8,128)(2,1)S(1)}, u32[]{:S(2)}, u32[]{:S(2)}) collective-permute-start(bf16[4144,128]{1,0:T(8,128)(2,1)S(1)} %shard_map.82.refs_0_), channel_id=1, source_target_pairs={{0,8},{8,16},{16,24},{24,32},{32,40},{40,48},{48,56},{56,0},{64,72... | collective-permute-start | bytes 3182600 | tf_op jit(solution)/shard_map/ppermute | solution.py:24
  9.2 5.1 %collective-permute-start.1 = (bf16[4144,128]{1,0:T(8,128)(2,1)S(1)}, bf16[4144,128]{1,0:T(8,128)(2,1)S(1)}, u32[]{:S(2)}, u32[]{:S(2)}) collective-permute-start(bf16[4144,128]{1,0:T(8,128)(2,1)S(1)} %shard_map.82.refs_0_), channel_id=1, source_target_pairs={{0,448},{8,456},{16,464},{24,472},{32,480},{40,488},{48,496},{56,5... | collective-permute-start | bytes 3182600 | tf_op jit(solution)/shard_map/ppermute | solution.py:24
  14.3 1.9 %collective-permute-start = (bf16[4144,128]{1,0:T(8,128)(2,1)S(1)}, bf16[4144,128]{1,0:T(8,128)(2,1)}, u32[]{:S(2)}, u32[]{:S(2)}) collective-permute-start(bf16[4144,128]{1,0:T(8,128)(2,1)S(1)} %shard_map.82.refs_0_), channel_id=1, source_target_pairs={{0,64},{8,72},{16,80},{24,88},{32,96},{40,104},{48,112},{56,120},{... | collective-permute-start | bytes 3182600 | tf_op jit(solution)/shard_map/ppermute | solution.py:24
  16.3 0.8 broadcast_in_dim.14
  17.0 12.8 %all-to-all-start = ((bf16[16,64,128]{2,1,0:T(8,128)(2,1)}), bf16[16,64,128]{2,1,0:T(8,128)(2,1)S(1)}, u32[]{:S(2)}, u32[]{:S(2)}) async-start(bf16[16,64,128]{2,1,0:T(8,128)(2,1)} %broadcast_in_dim.14), calls=%async_computation | async-start | bytes 524288 | tf_op jit(solution)/shard_map/all_to_all | solution.py:43
  29.9 22.1 %all-to-all-done = bf16[16,64,128]{2,1,0:T(8,128)(2,1)S(1)} async-done(((bf16[16,64,128]{2,1,0:T(8,128)(2,1)}), bf16[16,64,128]{2,1,0:T(8,128)(2,1)S(1)}, u32[]{:S(2)}, u32[]{:S(2)}) %all-to-all-start) | async-done | bytes 262176 | tf_op jit(solution)/shard_map/all_to_all | solution.py:43
  52.0 13.7 %shard_map.83 = bf16[16,72,128]{2,1,0:T(8,128)(2,1)S(1)} custom-call(s32[2]{0:T(128)S(1)} %pad_add_fusion.place_ref, s32[2,128]{1,0:T(2,128)S(1)} %bitcast.19, bf16[1024,128]{1,0:T(8,128)(2,1)S(1)} %bitcast.16, bf16[4144,128]{1,0:T(8,128)(2,1)S(1)} %shard_map.82.refs_0_, bf16[4144,128]{1,0:T(8,128)(2,1)} %collective-permute-done.refs_1_, ...), custom_call_target="tpu_custom_call" | custom-call | flops 17381195776 | bytes 4767744 | tf_op jit(solution)/shard_map/pallas_call | solution.py:55
  65.7 20.5 %all_to_all.20.got_ref = bf16[16,72,128]{2,1,0:T(8,128)(2,1)S(1)} all-to-all(bf16[16,72,128]{2,1,0:T(8,128)(2,1)S(1)} %shard_map.83), channel_id=1, replica_groups={{0,256,136,392,16,272,152,408,32,288,168,424,48,304,184,440},{64,320,20..., dimensions={0} | all-to-all | bytes 589824 | tf_op jit(solution)/shard_map/all_to_all | solution.py:43
  86.2 0.9 shard_map.84
  87.2 15.3 %all_to_all.21 = bf16[16,64,128]{2,1,0:T(8,128)(2,1)S(1)} all-to-all(bf16[16,64,128]{2,1,0:T(8,128)(2,1)S(1)} %broadcast_in_dim.15), channel_id=1, replica_groups={{0,256,136,392,16,272,152,408,32,288,168,424,48,304,184,440},{64,320,20..., dimensions={0} | all-to-all | bytes 524288 | tf_op jit(solution)/shard_map/all_to_all | solution.py:43
  102.5 2.4 %collective-permute-start.5 = (bf16[1024,128]{1,0:T(8,128)(2,1)S(1)}, bf16[1024,128]{1,0:T(8,128)(2,1)S(1)}, u32[]{:S(2)}, u32[]{:S(2)}) collective-permute-start(bf16[1024,128]{1,0:T(8,128)(2,1)S(1)} %bitcast.10), channel_id=1, source_target_pairs={{0,8},{8,16},{16,24},{24,32},{32,40},{40,48},{48,56},{56,0},{64,72... | collective-permute-start | bytes 786440 | tf_op jit(solution)/shard_map/ppermute | solution.py:24
  104.9 1.9 %collective-permute-start.4 = (bf16[1024,128]{1,0:T(8,128)(2,1)S(1)}, bf16[1024,128]{1,0:T(8,128)(2,1)S(1)}, u32[]{:S(2)}, u32[]{:S(2)}) collective-permute-start(bf16[1024,128]{1,0:T(8,128)(2,1)S(1)} %bitcast.11), channel_id=1, source_target_pairs={{0,448},{8,456},{16,464},{24,472},{32,480},{40,488},{48,496},{56,5... | collective-permute-start | bytes 786440 | tf_op jit(solution)/shard_map/ppermute | solution.py:24
  106.8 3.4 %collective-permute-start.3 = (bf16[1024,128]{1,0:T(8,128)(2,1)S(1)}, bf16[1024,128]{1,0:T(8,128)(2,1)S(1)}, u32[]{:S(2)}, u32[]{:S(2)}) collective-permute-start(bf16[1024,128]{1,0:T(8,128)(2,1)S(1)} %bitcast.12), channel_id=1, source_target_pairs={{0,64},{8,72},{16,80},{24,88},{32,96},{40,104},{48,112},{56,120},{... | collective-permute-start | bytes 786440 | tf_op jit(solution)/shard_map/ppermute | solution.py:24
  110.2 0.8 collective-permute-done.5.refs_3_
  111.0 1.0 collective-permute-done.4.refs_2_
  112.0 3.1 %collective-permute-done.3.refs_1_ = bf16[1024,128]{1,0:T(8,128)(2,1)S(1)} collective-permute-done((bf16[1024,128]{1,0:T(8,128)(2,1)S(1)}, bf16[1024,128]{1,0:T(8,128)(2,1)S(1)}, u32[]{:S(2)}, u32[]{:S(2)}) %collective-permute-start.3) | collective-permute-done | bytes 262176 | tf_op jit(solution)/shard_map/ppermute | solution.py:24
  115.1 1.8 %shard_map.85 = bf16[8,32,256]{2,1,0:T(8,128)(2,1)S(1)} custom-call(s32[2]{0:T(128)S(1)} %pad_add_fusion.place_ref, bf16[2048,256]{1,0:T(8,128)(2,1)S(1)} %copy-done, bf16[1024,128]{1,0:T(8,128)(2,1)S(1)} %bitcast.13, bf16[1024,128]{1,0:T(8,128)(2,1)S(1)} %collective-permute-done.3.refs_1_, bf16[1024,128]{1,0:T(8,128)(2,1)S(1)} %collective-permute-done.4.refs_2_, ...), custom_call_target="tpu_custom_call" | custom-call | flops 268435456 | tf_op jit(solution)/shard_map/pallas_call | solution.py:55
  117.0 17.2 %all_to_all.22.got_ref = bf16[8,32,256]{2,1,0:T(8,128)(2,1)S(1)} all-to-all(bf16[8,32,256]{2,1,0:T(8,128)(2,1)S(1)} %shard_map.85), channel_id=1, replica_groups=mesh['ctx'=64,'kvh'=8] {'kvh'}, dimensions={0} | all-to-all | bytes 262144 | tf_op jit(solution)/shard_map/all_to_all | solution.py:317
  134.2 0.6 shard_map.86
  (15 shorter events, 0.1 us)
Async XLA Ops:
  0.7 1.0 copy-start.1
  1.7 1.0 copy-start.2
  2.7 0.7 copy-start.3
  3.4 0.7 copy-start.4
  4.1 12.2 %copy-start.6 = (bf16[4,16,128]{2,1,0:T(8,128)(2,1)S(1)}, bf16[4,16,128]{2,1,0:T(8,128)(2,1)}, u32[]{:S(2)}) copy-start(bf16[4,16,128]{2,1,0:T(8,128)(2,1)} %param.8) | copy-start | bytes 49156
  4.1 47.9 %copy-start.5 = (s32[256]{0:T(256)S(1)}, s32[256]{0:T(256)}, u32[]{:S(2)}) copy-start(s32[256]{0:T(256)} %param.14) | copy-start | bytes 3076
  4.4 47.6 %collective-permute-start.2 = (bf16[4144,128]{1,0:T(8,128)(2,1)S(1)}, bf16[4144,128]{1,0:T(8,128)(2,1)S(1)}, u32[]{:S(2)}, u32[]{:S(2)}) collective-permute-start(bf16[4144,128]{1,0:T(8,128)(2,1)S(1)} %shard_map.82.refs_0_), channel_id=1, source_target_pairs={{0,8},{8,16},{16,24},{24,32},{32,40},{40,48},{48,56},{56,0},{64,72... | collective-permute-start | bytes 3182600 | tf_op jit(solution)/shard_map/ppermute | solution.py:24
  9.2 42.8 %collective-permute-start.1 = (bf16[4144,128]{1,0:T(8,128)(2,1)S(1)}, bf16[4144,128]{1,0:T(8,128)(2,1)S(1)}, u32[]{:S(2)}, u32[]{:S(2)}) collective-permute-start(bf16[4144,128]{1,0:T(8,128)(2,1)S(1)} %shard_map.82.refs_0_), channel_id=1, source_target_pairs={{0,448},{8,456},{16,464},{24,472},{32,480},{40,488},{48,496},{56,5... | collective-permute-start | bytes 3182600 | tf_op jit(solution)/shard_map/ppermute | solution.py:24
  14.3 37.7 %collective-permute-start = (bf16[4144,128]{1,0:T(8,128)(2,1)S(1)}, bf16[4144,128]{1,0:T(8,128)(2,1)}, u32[]{:S(2)}, u32[]{:S(2)}) collective-permute-start(bf16[4144,128]{1,0:T(8,128)(2,1)S(1)} %shard_map.82.refs_0_), channel_id=1, source_target_pairs={{0,64},{8,72},{16,80},{24,88},{32,96},{40,104},{48,112},{56,120},{... | collective-permute-start | bytes 3182600 | tf_op jit(solution)/shard_map/ppermute | solution.py:24
  17.0 35.0 %all-to-all-start = ((bf16[16,64,128]{2,1,0:T(8,128)(2,1)}), bf16[16,64,128]{2,1,0:T(8,128)(2,1)S(1)}, u32[]{:S(2)}, u32[]{:S(2)}) async-start(bf16[16,64,128]{2,1,0:T(8,128)(2,1)} %broadcast_in_dim.14), calls=%async_computation | async-start | bytes 524288 | tf_op jit(solution)/shard_map/all_to_all | solution.py:43
  65.7 49.4 %copy-start = (bf16[2048,256]{1,0:T(8,128)(2,1)S(1)}, bf16[2048,256]{1,0:T(8,128)(2,1)}, u32[]{:S(2)}) copy-start(bf16[2048,256]{1,0:T(8,128)(2,1)} %w_ref.1) | copy-start | bytes 3145732
  102.5 8.5 %collective-permute-start.5 = (bf16[1024,128]{1,0:T(8,128)(2,1)S(1)}, bf16[1024,128]{1,0:T(8,128)(2,1)S(1)}, u32[]{:S(2)}, u32[]{:S(2)}) collective-permute-start(bf16[1024,128]{1,0:T(8,128)(2,1)S(1)} %bitcast.10), channel_id=1, source_target_pairs={{0,8},{8,16},{16,24},{24,32},{32,40},{40,48},{48,56},{56,0},{64,72... | collective-permute-start | bytes 786440 | tf_op jit(solution)/shard_map/ppermute | solution.py:24
  104.9 7.1 %collective-permute-start.4 = (bf16[1024,128]{1,0:T(8,128)(2,1)S(1)}, bf16[1024,128]{1,0:T(8,128)(2,1)S(1)}, u32[]{:S(2)}, u32[]{:S(2)}) collective-permute-start(bf16[1024,128]{1,0:T(8,128)(2,1)S(1)} %bitcast.11), channel_id=1, source_target_pairs={{0,448},{8,456},{16,464},{24,472},{32,480},{40,488},{48,496},{56,5... | collective-permute-start | bytes 786440 | tf_op jit(solution)/shard_map/ppermute | solution.py:24
  106.8 8.3 %collective-permute-start.3 = (bf16[1024,128]{1,0:T(8,128)(2,1)S(1)}, bf16[1024,128]{1,0:T(8,128)(2,1)S(1)}, u32[]{:S(2)}, u32[]{:S(2)}) collective-permute-start(bf16[1024,128]{1,0:T(8,128)(2,1)S(1)} %bitcast.12), channel_id=1, source_target_pairs={{0,64},{8,72},{16,80},{24,88},{32,96},{40,104},{48,112},{56,120},{... | collective-permute-start | bytes 786440 | tf_op jit(solution)/shard_map/ppermute | solution.py:24

commit v4 on v1

v4 whole, which is shorter than its diff:
```python
import functools

import jax
import jax.numpy as jnp
from jax import lax
from jax.experimental import pallas as pl
from jax.experimental.pallas import tpu as pltpu
from jax.sharding import PartitionSpec as P

BF = jnp.bfloat16
F32 = jnp.float32
LOG2E = 1.4426950408889634
LIMIT = 48 * 1024 * 1024
HUGE = 2.0**100
SIDE = 8
STEPS = ((0, 0), (1, 0), (-1, 0), (0, 1))
TAIL = 32


def shift(value, step):
    pairs = []
    for y in range(SIDE):
        for z in range(SIDE):
            to = ((y + step[0]) % SIDE) * SIDE + (z + step[1]) % SIDE
            pairs.append((y * SIDE + z, to))
    return lax.ppermute(value, "ctx", pairs)


def coset(y, z):
    return lax.rem(y + 2 * z + 4 * SIDE, 4)


def member_y(which, i):
    return lax.rem(which + 2 * (i // 2), 4) + 4 * (i % 2)


def cosets():
    return [
        [((v + 2 * z) % 4 + 4 * b) * SIDE + z for z in range(SIDE) for b in range(2)]
        for v in range(4)
    ]


def exchange(value):
    return lax.all_to_all(value, "ctx", 0, 0, axis_index_groups=cosets(), tiled=True)


def share(value):
    copies = jnp.broadcast_to(value[None], (16,) + value.shape)
    return exchange(copies).reshape(16 * value.shape[0], value.shape[1])


def call(body, out_shape, flops=0, moved=0, scratch=(), smem=0, args=()):
    vmem = pl.BlockSpec(memory_space=pltpu.VMEM)
    scalars = pl.BlockSpec(memory_space=pltpu.SMEM)
    specs = [scalars] * smem + [vmem] * (len(args) - smem)
    return pl.pallas_call(
        body,
        out_shape=out_shape,
        in_specs=specs,
        out_specs=jax.tree.map(lambda _: vmem, out_shape),
        scratch_shapes=list(scratch),
        compiler_params=pltpu.CompilerParams(vmem_limit_bytes=LIMIT),
        cost_estimate=pl.CostEstimate(flops=flops, bytes_accessed=moved, transcendentals=0),
    )(*args)


def prepare_body(live_ref, k_ref, v_ref, fk_ref, fv_ref, ka_ref, vt_ref):
    live = live_ref[0]
    slots, width = k_ref.shape
    fresh = fk_ref.shape[0]
    step = 256
    first = k_ref[0:16, :].astype(F32)[0:1, :]
    for at in range(0, slots, step):
        alive = lax.broadcasted_iota(jnp.int32, (step, width), 0) + at < live
        keys = jnp.where(alive, k_ref[at : at + step, :].astype(F32), first)
        ka_ref[at : at + step, :] = keys.astype(BF)
        vals = jnp.where(alive, v_ref[at : at + step, :].astype(F32), 0.0)
        vt_ref[0:width, at : at + step] = vals.T.astype(BF)
        flags = lax.broadcasted_iota(jnp.int32, (16, step), 1) + at < live
        vt_ref[width:, at : at + step] = flags.astype(F32).astype(BF)
    keys = jnp.concatenate([fk_ref[...].astype(F32), jnp.zeros((16 - fresh, width), F32)], 0)
    ka_ref[slots:, :] = keys.astype(BF)
    vals = jnp.concatenate([fv_ref[...].astype(F32), jnp.zeros((128 - fresh, width), F32)], 0)
    vt_ref[0:width, slots:] = vals.T.astype(BF)
    flags = lax.broadcasted_iota(jnp.int32, (16, 128), 1) < fresh
    vt_ref[width:, slots:] = flags.astype(F32).astype(BF)


def prepare(live, keys, vals, fresh_k, fresh_v):
    slots, width = keys.shape
    out = [
        jax.ShapeDtypeStruct((slots + 16, width), BF),
        jax.ShapeDtypeStruct((width + 16, slots + 128), BF),
    ]
    return call(prepare_body, out, smem=1, args=(live, keys, vals, fresh_k, fresh_v))


def three(value):
    parts = []
    for _ in range(3):
        top = value.astype(BF).astype(F32)
        parts.append(top)
        value = value - top
    return parts


def attend_body(step, place_ref, seg_ref, ka_ref, vt_ref, q_ref, o_ref, qt_ref, lse_ref, worst_ref):
    keys, width = ka_ref.shape
    slots = keys - 16
    rows = 256
    heads = 16
    fresh = 4
    pieces = q_ref.shape[0] // rows
    factor = LOG2E / width**0.5
    y, z = place_ref[0], place_ref[1]
    first = fresh * (SIDE * y + z)
    line = lax.broadcasted_iota(jnp.int32, (16, rows), 0)
    never = 1 << 30
    opens = jnp.where(line < fresh, line + first, never)
    ends = jnp.full((16, rows), never, jnp.int32)
    seg = seg_ref[...]
    spot = lax.broadcasted_iota(jnp.int32, seg.shape, 0) * 128 + lax.broadcasted_iota(
        jnp.int32, seg.shape, 1
    )
    for j in range(fresh):
        own = jnp.sum(jnp.where(spot == first + j, seg, 0))
        ends = jnp.where(line == j, jnp.sum((seg <= own).astype(jnp.int32)), ends)
    lane = lax.broadcasted_iota(jnp.int32, (16, rows), 1)
    which = coset(y - step[0], z - step[1])
    cuts = [(at, 256) for at in range(0, slots, 256)] + [(slots, 16)]

    for i in range(pieces):
        at = slice(i * rows, (i + 1) * rows)
        qt_ref[:, at] = q_ref[at, :].astype(F32).T.astype(BF)

    def score(query, cut, i):
        at, deep = cut
        part = jnp.dot(ka_ref[at : at + deep, :], query, preferred_element_type=F32)
        if deep == 16:
            member = 4 * i + lane // 64
            token = 32 * member_y(which, member) + 4 * (member // 2)
            token = token + lax.rem(lane // heads, 4)
            part = jnp.where((token >= opens) & (token < ends), part, -jnp.inf)
        return part

    def most(part):
        return jnp.max(part, axis=0, keepdims=True)

    def weigh(part, cut, peak, total):
        weight = jnp.exp2((part - peak) * factor).astype(BF)
        at, wide = cut
        if wide == 16:
            weight = jnp.concatenate([weight, jnp.zeros((112, rows), BF)], 0)
            wide = 128
        add = jnp.dot(vt_ref[:, at : at + wide], weight, preferred_element_type=F32)
        return add if total is None else total + add

    def finish(i, peak, total):
        count = total[width : width + 1, :]
        out = total[0:width, :] * (1.0 / count)
        at = i * rows
        if not isinstance(i, int):
            at = pl.multiple_of(at, rows)
        o_ref[pl.ds(at, rows), :] = out.T.astype(BF)
        lse = peak * factor + jnp.log(count) * LOG2E
        lse_ref[i] = jnp.concatenate([lse[:, 0:128], lse[:, 128:256]], 0)
        return count

    def query_of(i):
        return qt_ref[:, i * rows : (i + 1) * rows]

    worst = None
    todo = [(i, cut) for i in range(pieces) for cut in cuts]
    ahead = score(query_of(0), cuts[0], 0)
    peak_ahead = most(ahead)
    for n, (i, cut) in enumerate(todo):
        part, peak = ahead, peak_ahead
        if n + 1 < len(todo):
            j, later = todo[n + 1]
            ahead = score(query_of(j), later, j)
            if later == cuts[0]:
                peak_ahead = most(ahead)
        total = weigh(part, cut, peak, None if cut == cuts[0] else total)
        if cut == cuts[-1]:
            count = finish(i, peak, total)
            worst = count if worst is None else jnp.maximum(worst, count)
    worst_ref[...] = jnp.broadcast_to(worst, worst_ref.shape)

    @pl.when(jnp.logical_not(jnp.max(worst_ref[0:1, :]) < HUGE))
    def _():
        def slow(i, carry):
            at = pl.multiple_of(i * rows, rows)
            query = qt_ref[:, pl.ds(at, rows)]
            peak = None
            for cut in cuts:
                top = most(score(query, cut, i))
                peak = top if peak is None else jnp.maximum(peak, top)
            total = None
            for cut in cuts:
                total = weigh(score(query, cut, i), cut, peak, total)
            finish(i, peak, total)
            return carry

        lax.fori_loop(0, pieces, slow, 0)

    lse = jnp.concatenate([lse_ref[i] for i in range(pieces)], 0)
    parts = three(lse) + [jnp.zeros((8, 128), F32)]
    o_ref[pieces * rows :, :] = jnp.concatenate(parts, 0).astype(BF)


def attend(place, seg, ka, vt, query, step):
    rows, width = query.shape
    return call(
        functools.partial(attend_body, step),
        jax.ShapeDtypeStruct((rows + TAIL, width), BF),
        flops=8 * rows * ka.shape[0] * 256,
        moved=(ka.size + vt.size + 2 * query.size) * 2,
        scratch=[
            pltpu.VMEM((width, rows), BF),
            pltpu.VMEM((4, 2, 128), F32),
            pltpu.VMEM((8, 256), F32),
        ],
        smem=1,
        args=(place, seg, ka, vt, query),
    )


def diagonal(rows):
    return lax.broadcasted_iota(jnp.int32, (rows, 128), 0) == lax.broadcasted_iota(
        jnp.int32, (rows, 128), 1
    )


def spread(row, eye):
    return jnp.sum(jnp.where(eye, row, 0.0), axis=1, keepdims=True)


def first_body(*refs):
    ins, out_ref = refs[:-1], refs[-1]
    rows = ins[0].shape[0] - TAIL
    eye = diagonal(128)
    logs = []
    for ref in ins:
        tail = ref[rows:, :].astype(F32)
        logs.append(tail[0:8] + tail[8:16] + tail[16:24])
    top = functools.reduce(jnp.maximum, logs)
    weights = [jnp.exp2(log - top) for log in logs]
    total = functools.reduce(jnp.add, weights)
    lse = top + jnp.log(total) * LOG2E
    weights = [w / total for w in weights]
    parts = []
    for _ in range(3):
        high = lse.astype(BF).astype(F32)
        parts.append(high)
        lse = lse - high
    empty = jnp.zeros((5, 128), F32)
    for b in range(rows // 128):
        merged = None
        for ref, weight in zip(ins, weights):
            term = ref[b * 128 : (b + 1) * 128, :].astype(F32) * spread(weight[b : b + 1], eye)
            merged = term if merged is None else merged + term
        merged = merged.astype(BF)
        tail = jnp.concatenate([p[b : b + 1] for p in parts] + [empty], 0).astype(BF)
        for j in range(2):
            out_ref[2 * b + j, 0:64, :] = merged[64 * j : 64 * j + 64, :]
            out_ref[2 * b + j, 64:72, :] = tail


def first_merge(ins):
    rows, width = ins[0].shape
    out = jax.ShapeDtypeStruct(((rows - TAIL) // 64, 72, width), BF)
    return call(first_body, out, args=tuple(ins))


def second_body(place_ref, got_ref, out_ref, logs):
    parts = got_ref.shape[0]
    for c in range(parts):
        tail = got_ref[c, 64:72, :].astype(F32)
        logs[c : c + 1, :] = tail[0:1] + tail[1:2] + tail[2:3]
    lse = logs[...]
    lse = jnp.where(place_ref[0] // 4 == 1, pltpu.roll(lse, 64, 1), lse)
    weight = jnp.exp2(lse - jnp.max(lse, axis=0, keepdims=True))
    weight = weight / jnp.sum(weight, axis=0, keepdims=True)
    eye = diagonal(64)
    total = None
    for c in range(parts):
        term = got_ref[c, 0:64, :].astype(F32) * spread(weight[c : c + 1, :], eye)
        total = term if total is None else total + term
    out_ref[...] = total.astype(BF)


def second_merge(place, got):
    return call(
        second_body,
        jax.ShapeDtypeStruct((64, got.shape[2]), BF),
        scratch=[pltpu.VMEM((got.shape[0], 128), F32)],
        smem=1,
        args=(place, got),
    )


def project_body(w_ref, *refs):
    ins, out_ref, rows = refs[:2], refs[2], refs[3]
    heads = w_ref.shape[0] // ins[0].shape[1]
    tokens = ins[0].shape[0] // heads
    left = []
    for ref in ins:
        rows[...] = ref[...].astype(F32)
        parts = [rows[pl.ds(h, tokens, stride=heads), :].astype(BF) for h in range(heads)]
        left.append(jnp.concatenate(parts, 1))
    mixed = jnp.dot(jnp.concatenate(left, 0), w_ref[...], preferred_element_type=F32)
    for k in range(out_ref.shape[0]):
        for i in range(2):
            at = i * tokens + 16 * k
            out_ref[k, 16 * i : 16 * i + 16, :] = mixed[at : at + 16, :].astype(BF)


def project(weight, ins):
    deep, cols = weight.shape
    rows, width = ins[0].shape
    tokens = 2 * rows * width // deep
    return call(
        project_body,
        jax.ShapeDtypeStruct((8, tokens // 8, cols), BF),
        flops=2 * tokens * deep * cols,
        scratch=[pltpu.VMEM((rows, width), F32)],
        args=(weight, *ins),
    )


def final_body(got_ref, out_ref):
    total = got_ref[0].astype(F32)
    for i in range(1, got_ref.shape[0]):
        total = total + got_ref[i].astype(F32)
    out_ref[...] = total.astype(BF)


def along(value, axis):
    lines = [[y * SIDE + z for z in range(SIDE)] for y in range(SIDE)]
    if axis == "y":
        lines = [list(line) for line in zip(*lines)]
    return lax.all_gather(value, "ctx", axis=0, tiled=True, axis_index_groups=lines)


def local(queries, cache_keys, cache_values, new_keys, new_values, cache_len, segment, out_weight):
    me = lax.axis_index("ctx").astype(jnp.int32)
    place = jnp.stack([me // SIDE, me % SIDE])
    block, heads, width = queries.shape
    ka, vt = prepare(
        cache_len,
        cache_keys[:, 0, :],
        cache_values[:, 0, :],
        new_keys[:, 0, :],
        new_values[:, 0, :],
    )
    mine = share(queries.reshape(block * heads, width))
    asked = [mine] + [shift(mine, step) for step in STEPS[1:]]
    seg = segment.reshape(-1, 128)
    partial = [attend(place, seg, ka, vt, q, step) for q, step in zip(asked, STEPS)]
    back = [shift(p, (-s[0], -s[1])) for p, s in zip(partial[1:], STEPS[1:])]
    own = second_merge(place, exchange(first_merge([partial[0]] + back)))
    line = along(own, "z")
    half = line.shape[0] // 2
    mixed = project(out_weight, [along(line[:half], "y"), along(line[half:], "y")])
    got = lax.all_to_all(mixed, "kvh", 0, 0, tiled=True)
    return call(final_body, jax.ShapeDtypeStruct(got.shape[1:], BF), args=(got,))


def solution(mesh):
    in_specs = (
        P("ctx", "kvh", None),
        P("ctx", "kvh", None),
        P("ctx", "kvh", None),
        P("ctx", "kvh", None),
        P("ctx", "kvh", None),
        P("ctx"),
        P(),
        P("kvh", "ctx"),
    )
    out_specs = P("kvh", "ctx")
    return jax.shard_map(local, mesh=mesh, in_specs=in_specs, out_specs=out_specs, check_vma=False)
```

time: 143 us -> 179 us (1.25)
  blocking collectives: 81.2 us -> 137 us
  starting transfers between devices: 26.5 us -> 18.2 us
  waiting for transfers between devices: 7.7 us -> 0.02 us
  Pallas kernels: 21.8 us -> 19.4 us
    all_gather x0 -> x3, blocking collectives: none -> 57.4 us  [along(): lax.all_gather(value, 'ctx', axis=0, tiled=True, axis_index_groups=lines)]
    ppermute x9 -> x6, starting transfers between devices: 26.5 us -> 18.2 us  [shift(): return lax.ppermute(value, 'ctx', pairs)]
    ppermute x9 -> x6, waiting for transfers between devices: 7.7 us -> 0.02 us  [shift(): return lax.ppermute(value, 'ctx', pairs)]
    pallas_call x9, Pallas kernels: 21.8 us -> 19.4 us  [call(): pl.pallas_call(body, out_shape=out_shape, in_specs=specs, out_specs=jax.t...]
    all_to_all x4 -> x3, blocking collectives: 81.2 us -> 79.4 us  [the longest x2 46.5 us: exchange(): lax.all_to_all(value, 'ctx', 0, 0, axis_index_groups=cosets(), tiled=True)]
  transfers between devices with their start and end apart: 9 -> 6, of which waited for: 3 -> 0; matrix products, arithmetic and copies ran while one was open for 0% -> 0% of each run, Pallas kernels for 12% -> 9%
where the time goes in v4:
time: 179 us
  blocking collectives  137 us (77%)
  Pallas kernels  19.4 us (11%)
  starting transfers between devices  18.2 us (10%)
  local copies, waits for them, and re-layouts  3.22 us (2%)
    all_gather x3, blocking collectives, along(): lax.all_gather(value, 'ctx', axis=0, tiled=True, axis_index_groups=lines)  57.4 us
    all_to_all x2, blocking collectives, exchange(): lax.all_to_all(value, 'ctx', 0, 0, axis_index_groups=cosets(), tiled=True)  46.5 us
    all_to_all x1, blocking collectives, local(): got = lax.all_to_all(mixed, 'kvh', 0, 0, tiled=True)  32.9 us
    pallas_call x9, Pallas kernels, call(): pl.pallas_call(body, out_shape=out_shape, in_specs=specs, out_specs=jax.t...  19.4 us
    ppermute x6, starting transfers between devices, shift(): return lax.ppermute(value, 'ctx', pairs)  18.2 us
  transfers between devices with their start and end apart: 6, of which 0 were waited for; matrix products, arithmetic and copies ran while one was open for 0% of the time, Pallas kernels for 9%

profile of v4, /device:TPU:1, one launch (start us, length us, event | category | flops | bytes accessed | tf_op | source)
XLA Modules:
  0.0 178.5 jit_solution(18233112971098682915)
XLA Ops:
  0.0 0.8 broadcast_in_dim.8
  0.8 28.9 %all_to_all.15 = bf16[16,64,128]{2,1,0:T(8,128)(2,1)S(1)} all-to-all(bf16[16,64,128]{2,1,0:T(8,128)(2,1)S(1)} %broadcast_in_dim.8), channel_id=1, replica_groups={{0,256,136,392,16,272,152,408,32,288,168,424,48,304,184,440},{64,320,20..., dimensions={0} | all-to-all | bytes 524288 | tf_op jit(solution)/shard_map/all_to_all | solution.py:45
  29.7 2.0 %collective-permute-start = (bf16[1024,128]{1,0:T(8,128)(2,1)S(1)}, bf16[1024,128]{1,0:T(8,128)(2,1)S(1)}, u32[]{:S(2)}, u32[]{:S(2)}) collective-permute-start(bf16[1024,128]{1,0:T(8,128)(2,1)S(1)} %bitcast.11), channel_id=1, source_target_pairs={{0,64},{8,72},{16,80},{24,88},{32,96},{40,104},{48,112},{56,120},{... | collective-permute-start | bytes 786440 | tf_op jit(solution)/shard_map/ppermute | solution.py:26
  32.5 0.6 copy-done.4
  33.2 1.0 copy-done.2
  34.6 1.9 %collective-permute-start.4 = (bf16[1024,128]{1,0:T(8,128)(2,1)S(1)}, bf16[1024,128]{1,0:T(8,128)(2,1)S(1)}, u32[]{:S(2)}, u32[]{:S(2)}) collective-permute-start(bf16[1024,128]{1,0:T(8,128)(2,1)S(1)} %bitcast.12), channel_id=1, source_target_pairs={{0,8},{8,16},{16,24},{24,32},{32,40},{40,48},{48,56},{56,0},{64,72... | collective-permute-start | bytes 786440 | tf_op jit(solution)/shard_map/ppermute | solution.py:26
  36.5 4.4 %collective-permute-start.2 = (bf16[1024,128]{1,0:T(8,128)(2,1)S(1)}, bf16[1024,128]{1,0:T(8,128)(2,1)S(1)}, u32[]{:S(2)}, u32[]{:S(2)}) collective-permute-start(bf16[1024,128]{1,0:T(8,128)(2,1)S(1)} %bitcast.13), channel_id=1, source_target_pairs={{0,448},{8,456},{16,464},{24,472},{32,480},{40,488},{48,496},{56,5... | collective-permute-start | bytes 786440 | tf_op jit(solution)/shard_map/ppermute | solution.py:26
  41.0 0.7 copy-done.5
  41.7 3.9 %shard_map.84 = bf16[1056,128]{1,0:T(8,128)(2,1)S(1)} custom-call(s32[2]{0:T(128)S(1)} %pad_add_fusion.place_ref, s32[2,128]{1,0:T(2,128)S(1)} %bitcast.17, bf16[2064,128]{1,0:T(8,128)(2,1)S(1)} %get-tuple-element.7.ka_ref, bf16[144,2176]{1,0:T(8,128)(2,1)S(1)} %get-tuple-element.8.vt_ref, bf16[1024,128]{1,0:T(8,128)(2,1)S(1)} %collective-permute-done.q_ref), custom_call_target="tpu_custom_call" | custom-call | flops 4328521728 | bytes 1679360 | tf_op jit(solution)/shard_map/pallas_call | solution.py:57
  45.6 1.9 %collective-permute-start.1 = (bf16[1056,128]{1,0:T(8,128)(2,1)S(1)}, bf16[1056,128]{1,0:T(8,128)(2,1)S(1)}, u32[]{:S(2)}, u32[]{:S(2)}) collective-permute-start(bf16[1056,128]{1,0:T(8,128)(2,1)S(1)} %shard_map.84), channel_id=1, source_target_pairs={{0,448},{8,456},{16,464},{24,472},{32,480},{40,488},{48,496},{56,5... | collective-permute-start | bytes 811016 | tf_op jit(solution)/shard_map/ppermute | solution.py:26
  47.5 3.9 %shard_map.85 = bf16[1056,128]{1,0:T(8,128)(2,1)S(1)} custom-call(s32[2]{0:T(128)S(1)} %pad_add_fusion.place_ref, s32[2,128]{1,0:T(2,128)S(1)} %bitcast.18, bf16[2064,128]{1,0:T(8,128)(2,1)S(1)} %get-tuple-element.7.ka_ref, bf16[144,2176]{1,0:T(8,128)(2,1)S(1)} %get-tuple-element.8.vt_ref, bf16[1024,128]{1,0:T(8,128)(2,1)S(1)} %collective-permute-done.2.q_ref), custom_call_target="tpu_custom_call" | custom-call | flops 4328521728 | bytes 1679360 | tf_op jit(solution)/shard_map/pallas_call | solution.py:57
  51.4 3.4 %collective-permute-start.3 = (bf16[1056,128]{1,0:T(8,128)(2,1)S(1)}, bf16[1056,128]{1,0:T(8,128)(2,1)S(1)}, u32[]{:S(2)}, u32[]{:S(2)}) collective-permute-start(bf16[1056,128]{1,0:T(8,128)(2,1)S(1)} %shard_map.85), channel_id=1, source_target_pairs={{0,64},{8,72},{16,80},{24,88},{32,96},{40,104},{48,112},{56,120},{... | collective-permute-start | bytes 811016 | tf_op jit(solution)/shard_map/ppermute | solution.py:26
  54.8 4.1 %shard_map.86 = bf16[1056,128]{1,0:T(8,128)(2,1)S(1)} custom-call(s32[2]{0:T(128)S(1)} %pad_add_fusion.place_ref, s32[2,128]{1,0:T(2,128)S(1)} %bitcast.19, bf16[2064,128]{1,0:T(8,128)(2,1)S(1)} %get-tuple-element.7.ka_ref, bf16[144,2176]{1,0:T(8,128)(2,1)S(1)} %get-tuple-element.8.vt_ref, bf16[1024,128]{1,0:T(8,128)(2,1)S(1)} %collective-permute-done.4.q_ref), custom_call_target="tpu_custom_call" | custom-call | flops 4328521728 | bytes 1679360 | tf_op jit(solution)/shard_map/pallas_call | solution.py:57
  58.8 4.6 %collective-permute-start.5 = (bf16[1056,128]{1,0:T(8,128)(2,1)S(1)}, bf16[1056,128]{1,0:T(8,128)(2,1)S(1)}, u32[]{:S(2)}, u32[]{:S(2)}) collective-permute-start(bf16[1056,128]{1,0:T(8,128)(2,1)S(1)} %shard_map.86), channel_id=1, source_target_pairs={{0,56},{8,0},{16,8},{24,16},{32,24},{40,32},{48,40},{56,48},{64,12... | collective-permute-start | bytes 811016 | tf_op jit(solution)/shard_map/ppermute | solution.py:26
  63.4 3.9 %shard_map.83.refs_0_ = bf16[1056,128]{1,0:T(8,128)(2,1)S(1)} custom-call(s32[2]{0:T(128)S(1)} %pad_add_fusion.place_ref, s32[2,128]{1,0:T(2,128)S(1)} %bitcast.20, bf16[2064,128]{1,0:T(8,128)(2,1)S(1)} %get-tuple-element.7.ka_ref, bf16[144,2176]{1,0:T(8,128)(2,1)S(1)} %get-tuple-element.8.vt_ref, bf16[1024,128]{1,0:T(8,128)(2,1)S(1)} %bitcast.14), custom_call_target="tpu_custom_call" | custom-call | flops 4328521728 | bytes 1679360 | tf_op jit(solution)/shard_map/pallas_call | solution.py:57
  67.3 0.7 shard_map.87
  68.0 17.6 %all_to_all.16.got_ref = bf16[16,72,128]{2,1,0:T(8,128)(2,1)S(1)} all-to-all(bf16[16,72,128]{2,1,0:T(8,128)(2,1)S(1)} %shard_map.87), channel_id=1, replica_groups={{0,256,136,392,16,272,152,408,32,288,168,424,48,304,184,440},{64,320,20..., dimensions={0} | all-to-all | bytes 589824 | tf_op jit(solution)/shard_map/all_to_all | solution.py:45
  85.6 0.9 shard_map.88
  86.5 18.2 %all_gather.9 = bf16[512,128]{1,0:T(8,128)(2,1)S(1)} all-gather(bf16[64,128]{1,0:T(8,128)(2,1)S(1)} %shard_map.88), channel_id=1, replica_groups={{0,8,16,24,32,40,48,56},{64,72,80,88,96,104,112,120},{128,136,144,152,1..., dimensions={0}, use_global_device_ids=true | all-gather | bytes 147456 | tf_op jit(solution)/shard_map/all_gather | solution.py:343
  104.7 19.5 %all_gather.11.refs_1_ = bf16[2048,128]{1,0:T(8,128)(2,1)S(1)} all-gather(bf16[256,128]{1,0:T(8,128)(2,1)S(1)} %get-tuple-element.9), channel_id=1, replica_groups={{0,64,128,192,256,320,384,448},{8,72,136,200,264,328,392,456},{16,80,14..., dimensions={0}, use_global_device_ids=true | all-gather | bytes 589824 | tf_op jit(solution)/shard_map/all_gather | solution.py:343
  124.2 19.6 %all_gather.10.refs_0_ = bf16[2048,128]{1,0:T(8,128)(2,1)S(1)} all-gather(bf16[256,128]{1,0:T(8,128)(2,1)S(1)} %get-tuple-element.10), channel_id=1, replica_groups={{0,64,128,192,256,320,384,448},{8,72,136,200,264,328,392,456},{16,80,14..., dimensions={0}, use_global_device_ids=true | all-gather | bytes 589824 | tf_op jit(solution)/shard_map/all_gather | solution.py:343
  143.8 1.2 shard_map.89
  145.0 32.9 %all_to_all.17.got_ref = bf16[8,32,256]{2,1,0:T(8,128)(2,1)S(1)} all-to-all(bf16[8,32,256]{2,1,0:T(8,128)(2,1)S(1)} %shard_map.89), channel_id=1, replica_groups=mesh['ctx'=64,'kvh'=8] {'kvh'}, dimensions={0} | all-to-all | bytes 262144 | tf_op jit(solution)/shard_map/all_to_all | solution.py:366
  177.9 0.6 shard_map.90
  (18 shorter events, 0.5 us)
Async XLA Ops:
  0.0 32.5 %copy-start.1 = (bf16[2048,1,128]{2,0,1:T(8,128)(2,1)S(1)}, bf16[2048,1,128]{2,0,1:T(8,128)(2,1)}, u32[]{:S(2)}) copy-start(bf16[2048,1,128]{2,0,1:T(8,128)(2,1)} %param.9) | copy-start | bytes 1572868
  29.7 11.2 %collective-permute-start = (bf16[1024,128]{1,0:T(8,128)(2,1)S(1)}, bf16[1024,128]{1,0:T(8,128)(2,1)S(1)}, u32[]{:S(2)}, u32[]{:S(2)}) collective-permute-start(bf16[1024,128]{1,0:T(8,128)(2,1)S(1)} %bitcast.11), channel_id=1, source_target_pairs={{0,64},{8,72},{16,80},{24,88},{32,96},{40,104},{48,112},{56,120},{... | collective-permute-start | bytes 786440 | tf_op jit(solution)/shard_map/ppermute | solution.py:26
  32.5 0.7 copy-start.4
  32.5 0.7 copy-start.3
  33.2 1.0 copy-start.2
  34.6 20.1 %collective-permute-start.4 = (bf16[1024,128]{1,0:T(8,128)(2,1)S(1)}, bf16[1024,128]{1,0:T(8,128)(2,1)S(1)}, u32[]{:S(2)}, u32[]{:S(2)}) collective-permute-start(bf16[1024,128]{1,0:T(8,128)(2,1)S(1)} %bitcast.12), channel_id=1, source_target_pairs={{0,8},{8,16},{16,24},{24,32},{32,40},{40,48},{48,56},{56,0},{64,72... | collective-permute-start | bytes 786440 | tf_op jit(solution)/shard_map/ppermute | solution.py:26
  36.5 10.9 %collective-permute-start.2 = (bf16[1024,128]{1,0:T(8,128)(2,1)S(1)}, bf16[1024,128]{1,0:T(8,128)(2,1)S(1)}, u32[]{:S(2)}, u32[]{:S(2)}) collective-permute-start(bf16[1024,128]{1,0:T(8,128)(2,1)S(1)} %bitcast.13), channel_id=1, source_target_pairs={{0,448},{8,456},{16,464},{24,472},{32,480},{40,488},{48,496},{56,5... | collective-permute-start | bytes 786440 | tf_op jit(solution)/shard_map/ppermute | solution.py:26
  41.0 0.7 copy-start.5
  45.6 21.7 %collective-permute-start.1 = (bf16[1056,128]{1,0:T(8,128)(2,1)S(1)}, bf16[1056,128]{1,0:T(8,128)(2,1)S(1)}, u32[]{:S(2)}, u32[]{:S(2)}) collective-permute-start(bf16[1056,128]{1,0:T(8,128)(2,1)S(1)} %shard_map.84), channel_id=1, source_target_pairs={{0,448},{8,456},{16,464},{24,472},{32,480},{40,488},{48,496},{56,5... | collective-permute-start | bytes 811016 | tf_op jit(solution)/shard_map/ppermute | solution.py:26
  51.4 15.9 %collective-permute-start.3 = (bf16[1056,128]{1,0:T(8,128)(2,1)S(1)}, bf16[1056,128]{1,0:T(8,128)(2,1)S(1)}, u32[]{:S(2)}, u32[]{:S(2)}) collective-permute-start(bf16[1056,128]{1,0:T(8,128)(2,1)S(1)} %shard_map.85), channel_id=1, source_target_pairs={{0,64},{8,72},{16,80},{24,88},{32,96},{40,104},{48,112},{56,120},{... | collective-permute-start | bytes 811016 | tf_op jit(solution)/shard_map/ppermute | solution.py:26
  58.8 8.5 %collective-permute-start.5 = (bf16[1056,128]{1,0:T(8,128)(2,1)S(1)}, bf16[1056,128]{1,0:T(8,128)(2,1)S(1)}, u32[]{:S(2)}, u32[]{:S(2)}) collective-permute-start(bf16[1056,128]{1,0:T(8,128)(2,1)S(1)} %shard_map.86), channel_id=1, source_target_pairs={{0,56},{8,0},{16,8},{24,16},{32,24},{40,32},{48,40},{56,48},{64,12... | collective-permute-start | bytes 811016 | tf_op jit(solution)/shard_map/ppermute | solution.py:26
  85.6 58.3 %copy-start = (bf16[2048,256]{1,0:T(8,128)(2,1)S(1)}, bf16[2048,256]{1,0:T(8,128)(2,1)}, u32[]{:S(2)}) copy-start(bf16[2048,256]{1,0:T(8,128)(2,1)} %w_ref.1) | copy-start | bytes 3145732

commit v5 on v4

--- a/solution.py
+++ b/solution.py
@@ -65,7 +65,7 @@
     )(*args)
 
 
-def prepare_body(live_ref, k_ref, v_ref, fk_ref, fv_ref, ka_ref, vt_ref):
+def prepare_body(live_ref, place_ref, seg_ref, k_ref, v_ref, fk_ref, fv_ref, ka_ref, vt_ref, b_ref):
     live = live_ref[0]
     slots, width = k_ref.shape
     fresh = fk_ref.shape[0]
@@ -85,15 +85,40 @@
     vt_ref[0:width, slots:] = vals.T.astype(BF)
     flags = lax.broadcasted_iota(jnp.int32, (16, 128), 1) < fresh
     vt_ref[width:, slots:] = flags.astype(F32).astype(BF)
-
-
-def prepare(live, keys, vals, fresh_k, fresh_v):
+    mine = fresh * (SIDE * place_ref[0] + place_ref[1])
+    line = lax.broadcasted_iota(jnp.int32, (16, 128), 0)
+    never = 1 << 30
+    ends = jnp.full((16, 128), never, jnp.int32)
+    seg = seg_ref[...]
+    spot = lax.broadcasted_iota(jnp.int32, seg.shape, 0) * 128 + lax.broadcasted_iota(
+        jnp.int32, seg.shape, 1
+    )
+    for j in range(fresh):
+        own = jnp.sum(jnp.where(spot == mine + j, seg, 0))
+        ends = jnp.where(line == j, jnp.sum((seg <= own).astype(jnp.int32)), ends)
+    b_ref[0:16, :] = jnp.where(line < fresh, line + mine, never)
+    b_ref[16:32, :] = ends
+
+
+def prepare(live, place, seg, keys, vals, fresh_k, fresh_v):
     slots, width = keys.shape
     out = [
         jax.ShapeDtypeStruct((slots + 16, width), BF),
         jax.ShapeDtypeStruct((width + 16, slots + 128), BF),
+        jax.ShapeDtypeStruct((32, 128), jnp.int32),
     ]
-    return call(prepare_body, out, smem=1, args=(live, keys, vals, fresh_k, fresh_v))
+    args = (live, place, seg, keys, vals, fresh_k, fresh_v)
+    return call(prepare_body, out, smem=2, args=args)
+
+
+def turn_body(bound_ref, q_ref, out_ref):
+    for at in range(0, q_ref.shape[0], 256):
+        out_ref[:, at : at + 256] = q_ref[at : at + 256, :].astype(F32).T.astype(BF)
+
+
+def turn(bounds, query):
+    out = jax.ShapeDtypeStruct(query.shape[::-1], BF)
+    return call(turn_body, out, args=(bounds, query))
 
 
 def three(value):
@@ -105,34 +130,18 @@
     return parts
 
 
-def attend_body(step, place_ref, seg_ref, ka_ref, vt_ref, q_ref, o_ref, qt_ref, lse_ref, worst_ref):
+def attend_body(step, place_ref, bound_ref, ka_ref, vt_ref, qt_ref, o_ref, lse_ref, worst_ref):
     keys, width = ka_ref.shape
     slots = keys - 16
     rows = 256
     heads = 16
-    fresh = 4
-    pieces = q_ref.shape[0] // rows
+    pieces = qt_ref.shape[1] // rows
     factor = LOG2E / width**0.5
-    y, z = place_ref[0], place_ref[1]
-    first = fresh * (SIDE * y + z)
-    line = lax.broadcasted_iota(jnp.int32, (16, rows), 0)
-    never = 1 << 30
-    opens = jnp.where(line < fresh, line + first, never)
-    ends = jnp.full((16, rows), never, jnp.int32)
-    seg = seg_ref[...]
-    spot = lax.broadcasted_iota(jnp.int32, seg.shape, 0) * 128 + lax.broadcasted_iota(
-        jnp.int32, seg.shape, 1
-    )
-    for j in range(fresh):
-        own = jnp.sum(jnp.where(spot == first + j, seg, 0))
-        ends = jnp.where(line == j, jnp.sum((seg <= own).astype(jnp.int32)), ends)
+    opens = jnp.concatenate([bound_ref[0:16, :]] * 2, 1)
+    ends = jnp.concatenate([bound_ref[16:32, :]] * 2, 1)
     lane = lax.broadcasted_iota(jnp.int32, (16, rows), 1)
-    which = coset(y - step[0], z - step[1])
+    which = coset(place_ref[0] - step[0], place_ref[1] - step[1])
     cuts = [(at, 256) for at in range(0, slots, 256)] + [(slots, 16)]
-
-    for i in range(pieces):
-        at = slice(i * rows, (i + 1) * rows)
-        qt_ref[:, at] = q_ref[at, :].astype(F32).T.astype(BF)
 
     def score(query, cut, i):
         at, deep = cut
@@ -209,20 +218,16 @@
     o_ref[pieces * rows :, :] = jnp.concatenate(parts, 0).astype(BF)
 
 
-def attend(place, seg, ka, vt, query, step):
-    rows, width = query.shape
+def attend(place, bounds, ka, vt, query, step):
+    width, rows = query.shape
     return call(
         functools.partial(attend_body, step),
         jax.ShapeDtypeStruct((rows + TAIL, width), BF),
         flops=8 * rows * ka.shape[0] * 256,
         moved=(ka.size + vt.size + 2 * query.size) * 2,
-        scratch=[
-            pltpu.VMEM((width, rows), BF),
-            pltpu.VMEM((4, 2, 128), F32),
-            pltpu.VMEM((8, 256), F32),
-        ],
+        scratch=[pltpu.VMEM((4, 2, 128), F32), pltpu.VMEM((8, 256), F32)],
         smem=1,
-        args=(place, seg, ka, vt, query),
+        args=(place, bounds, ka, vt, query),
     )
 
 
@@ -300,32 +305,31 @@
     )
 
 
-def project_body(w_ref, *refs):
-    ins, out_ref, rows = refs[:2], refs[2], refs[3]
+def project_body(place_ref, w_ref, *refs):
+    ins, out_ref, rows = refs[:4], refs[4], refs[5]
     heads = w_ref.shape[0] // ins[0].shape[1]
-    tokens = ins[0].shape[0] // heads
-    left = []
-    for ref in ins:
-        rows[...] = ref[...].astype(F32)
-        parts = [rows[pl.ds(h, tokens, stride=heads), :].astype(BF) for h in range(heads)]
-        left.append(jnp.concatenate(parts, 1))
-    mixed = jnp.dot(jnp.concatenate(left, 0), w_ref[...], preferred_element_type=F32)
-    for k in range(out_ref.shape[0]):
-        for i in range(2):
-            at = i * tokens + 16 * k
-            out_ref[k, 16 * i : 16 * i + 16, :] = mixed[at : at + 16, :].astype(BF)
-
-
-def project(weight, ins):
+    tokens = rows.shape[0] // heads
+    for ref, step in zip(ins, STEPS):
+        which = coset(place_ref[0] - step[0], place_ref[1] - step[1])
+        for n in range(ref.shape[0] // 64):
+            to = pl.multiple_of(64 * (SIDE * member_y(which, n) + n // 2), 64)
+            rows[pl.ds(to, 64), :] = ref[64 * n : 64 * n + 64, :].astype(F32)
+    left = [rows[pl.ds(h, tokens, stride=heads), :].astype(BF) for h in range(heads)]
+    mixed = jnp.dot(jnp.concatenate(left, 1), w_ref[...], preferred_element_type=F32)
+    out_ref[...] = mixed.astype(BF)
+
+
+def project(place, weight, ins):
     deep, cols = weight.shape
     rows, width = ins[0].shape
-    tokens = 2 * rows * width // deep
+    tokens = 4 * rows * width // deep
     return call(
         project_body,
-        jax.ShapeDtypeStruct((8, tokens // 8, cols), BF),
+        jax.ShapeDtypeStruct((tokens, cols), BF),
         flops=2 * tokens * deep * cols,
-        scratch=[pltpu.VMEM((rows, width), F32)],
-        args=(weight, *ins),
+        scratch=[pltpu.VMEM((4 * rows, width), F32)],
+        smem=1,
+        args=(place, weight, *ins),
     )
 
 
@@ -336,33 +340,28 @@
     out_ref[...] = total.astype(BF)
 
 
-def along(value, axis):
-    lines = [[y * SIDE + z for z in range(SIDE)] for y in range(SIDE)]
-    if axis == "y":
-        lines = [list(line) for line in zip(*lines)]
-    return lax.all_gather(value, "ctx", axis=0, tiled=True, axis_index_groups=lines)
-
-
 def local(queries, cache_keys, cache_values, new_keys, new_values, cache_len, segment, out_weight):
     me = lax.axis_index("ctx").astype(jnp.int32)
     place = jnp.stack([me // SIDE, me % SIDE])
     block, heads, width = queries.shape
-    ka, vt = prepare(
+    ka, vt, bounds = prepare(
         cache_len,
+        place,
+        segment.reshape(-1, 128),
         cache_keys[:, 0, :],
         cache_values[:, 0, :],
         new_keys[:, 0, :],
         new_values[:, 0, :],
     )
-    mine = share(queries.reshape(block * heads, width))
+    mine = turn(bounds, share(queries.reshape(block * heads, width)))
     asked = [mine] + [shift(mine, step) for step in STEPS[1:]]
-    seg = segment.reshape(-1, 128)
-    partial = [attend(place, seg, ka, vt, q, step) for q, step in zip(asked, STEPS)]
+    partial = [attend(place, bounds, ka, vt, q, step) for q, step in zip(asked, STEPS)]
     back = [shift(p, (-s[0], -s[1])) for p, s in zip(partial[1:], STEPS[1:])]
     own = second_merge(place, exchange(first_merge([partial[0]] + back)))
-    line = along(own, "z")
-    half = line.shape[0] // 2
-    mixed = project(out_weight, [along(line[:half], "y"), along(line[half:], "y")])
+    mine = share(own)
+    every = [mine] + [shift(mine, step) for step in STEPS[1:]]
+    mixed = project(place, out_weight, every)
+    mixed = mixed.reshape(lax.axis_size("kvh"), -1, mixed.shape[1])
     got = lax.all_to_all(mixed, "kvh", 0, 0, tiled=True)
     return call(final_body, jax.ShapeDtypeStruct(got.shape[1:], BF), args=(got,))
 

time: 179 us -> 134 us (0.75)
  blocking collectives: 137 us -> 52.8 us
  starting transfers between devices: 18.2 us -> 41.6 us
  waiting for transfers between devices: 0.02 us -> 14.8 us
    all_gather x3 -> x0, blocking collectives: 57.4 us -> none  [along(): lax.all_gather(value, 'ctx', axis=0, tiled=True, axis_index_groups=lines)]
    all_to_all x0 -> x1, starting transfers between devices: none -> 16.2 us  [exchange(): lax.all_to_all(value, 'ctx', 0, 0, axis_index_groups=cosets(), tiled=True)]
    all_to_all x1, blocking collectives: 32.9 us -> 17.4 us  [local(): got = lax.all_to_all(mixed, 'kvh', 0, 0, tiled=True)]
    all_to_all x2, blocking collectives: 46.5 us -> 35.4 us  [exchange(): lax.all_to_all(value, 'ctx', 0, 0, axis_index_groups=cosets(), tiled=True)]
    all_to_all x0 -> x1, waiting for transfers between devices: none -> 9.2 us  [exchange(): lax.all_to_all(value, 'ctx', 0, 0, axis_index_groups=cosets(), tiled=True)]
    ppermute x6 -> x9, starting transfers between devices: 18.2 us -> 25.3 us  [shift(): return lax.ppermute(value, 'ctx', pairs)]
    ppermute x6 -> x9, waiting for transfers between devices: 0.02 us -> 5.57 us  [shift(): return lax.ppermute(value, 'ctx', pairs)]
    pallas_call x9 -> x10, Pallas kernels: 19.4 us -> 20.1 us  [call(): pl.pallas_call(body, out_shape=out_shape, in_specs=specs, out_specs=jax.t...]
  transfers between devices with their start and end apart: 6 -> 10, of which waited for: 0 -> 5; matrix products, arithmetic and copies ran while one was open for 0% -> 0% of each run, Pallas kernels for 9% -> 12%
where the time goes in v5:
time: 134 us; the launch traced here: 133 us
  blocking collectives  52.8 us (39%)
  starting transfers between devices  41.6 us (31%)
  Pallas kernels  20.1 us (15%)
  waiting for transfers between devices  14.8 us (11%)
  local copies, waits for them, and re-layouts  3.29 us (2%)
    all_to_all x2, blocking collectives, exchange(): lax.all_to_all(value, 'ctx', 0, 0, axis_index_groups=cosets(), tiled=True)  35.4 us
    ppermute x9, starting transfers between devices, shift(): return lax.ppermute(value, 'ctx', pairs)  25.3 us
    pallas_call x10, Pallas kernels, call(): pl.pallas_call(body, out_shape=out_shape, in_specs=specs, out_specs=jax.t...  20.1 us
    all_to_all x1, blocking collectives, local(): got = lax.all_to_all(mixed, 'kvh', 0, 0, tiled=True)  17.4 us
    all_to_all x1, starting transfers between devices, exchange(): lax.all_to_all(value, 'ctx', 0, 0, axis_index_groups=cosets(), tiled=True)  16.2 us
    all_to_all x1, waiting for transfers between devices, exchange(): lax.all_to_all(value, 'ctx', 0, 0, axis_index_groups=cosets(), tiled=True)  9.2 us
    ppermute x9, waiting for transfers between devices, shift(): return lax.ppermute(value, 'ctx', pairs)  5.57 us
  transfers between devices with their start and end apart: 10, of which 5 were waited for; matrix products, arithmetic and copies ran while one was open for 0% of the time, Pallas kernels for 12%

profile of v5, /device:TPU:1, one launch (start us, length us, event | category | flops | bytes accessed | tf_op | source)
XLA Modules:
  0.0 133.5 jit_solution(7893915258782646273)
XLA Ops:
  0.0 1.5 %broadcast_in_dim.14 = bf16[16,64,128]{2,1,0:T(8,128)(2,1)} broadcast(bf16[64,128]{1,0:T(8,128)(2,1)} %bitcast.22), dimensions={1,2} | broadcast | bytes 278528 | tf_op jit(solution)/shard_map/broadcast_in_dim | solution.py:49
  1.5 16.2 %all-to-all-start = ((bf16[16,64,128]{2,1,0:T(8,128)(2,1)}), bf16[16,64,128]{2,1,0:T(8,128)(2,1)S(1)}, u32[]{:S(2)}, u32[]{:S(2)}) async-start(bf16[16,64,128]{2,1,0:T(8,128)(2,1)} %broadcast_in_dim.14), calls=%async_computation | async-start | bytes 524288 | tf_op jit(solution)/shard_map/all_to_all | solution.py:45
  19.2 1.0 copy-done.2
  20.2 1.2 shard_map.82
  21.4 9.2 %all-to-all-done = bf16[16,64,128]{2,1,0:T(8,128)(2,1)S(1)} async-done(((bf16[16,64,128]{2,1,0:T(8,128)(2,1)}), bf16[16,64,128]{2,1,0:T(8,128)(2,1)S(1)}, u32[]{:S(2)}, u32[]{:S(2)}) %all-to-all-start) | async-done | bytes 262176 | tf_op jit(solution)/shard_map/all_to_all | solution.py:45
  30.8 2.1 %collective-permute-start = (bf16[128,1024]{1,0:T(8,128)(2,1)S(1)}, bf16[128,1024]{1,0:T(8,128)(2,1)S(1)}, u32[]{:S(2)}, u32[]{:S(2)}) collective-permute-start(bf16[128,1024]{1,0:T(8,128)(2,1)S(1)} %shard_map.83.qt_ref), channel_id=1, source_target_pairs={{0,64},{8,72},{16,80},{24,88},{32,96},{40,104},{48,112},{56,120},{... | collective-permute-start | bytes 786440 | tf_op jit(solution)/shard_map/ppermute | solution.py:26
  32.9 1.9 %collective-permute-start.4 = (bf16[128,1024]{1,0:T(8,128)(2,1)S(1)}, bf16[128,1024]{1,0:T(8,128)(2,1)S(1)}, u32[]{:S(2)}, u32[]{:S(2)}) collective-permute-start(bf16[128,1024]{1,0:T(8,128)(2,1)S(1)} %shard_map.83.qt_ref), channel_id=1, source_target_pairs={{0,8},{8,16},{16,24},{24,32},{32,40},{40,48},{48,56},{56,0},{64,72... | collective-permute-start | bytes 786440 | tf_op jit(solution)/shard_map/ppermute | solution.py:26
  34.8 4.4 %collective-permute-start.2 = (bf16[128,1024]{1,0:T(8,128)(2,1)S(1)}, bf16[128,1024]{1,0:T(8,128)(2,1)S(1)}, u32[]{:S(2)}, u32[]{:S(2)}) collective-permute-start(bf16[128,1024]{1,0:T(8,128)(2,1)S(1)} %shard_map.83.qt_ref), channel_id=1, source_target_pairs={{0,448},{8,456},{16,464},{24,472},{32,480},{40,488},{48,496},{56,5... | collective-permute-start | bytes 786440 | tf_op jit(solution)/shard_map/ppermute | solution.py:26
  39.5 3.8 %shard_map.85 = bf16[1056,128]{1,0:T(8,128)(2,1)S(1)} custom-call(s32[2]{0:T(128)S(1)} %pad_add_fusion.place_ref, s32[32,128]{1,0:T(8,128)S(1)} %get-tuple-element.8.bound_ref, bf16[2064,128]{1,0:T(8,128)(2,1)S(1)} %get-tuple-element.9.ka_ref, bf16[144,2176]{1,0:T(8,128)(2,1)S(1)} %get-tuple-element.10.vt_ref, bf16[128,1024]{1,0:T(8,128)(2,1)S(1)} %collective-permute-done.qt_ref), custom_call_target="tpu_custom_call" | custom-call | flops 4328521728 | bytes 1679360 | tf_op jit(solution)/shard_map/pallas_call | solution.py:57
  43.3 1.9 %collective-permute-start.1 = (bf16[1056,128]{1,0:T(8,128)(2,1)S(1)}, bf16[1056,128]{1,0:T(8,128)(2,1)S(1)}, u32[]{:S(2)}, u32[]{:S(2)}) collective-permute-start(bf16[1056,128]{1,0:T(8,128)(2,1)S(1)} %shard_map.85), channel_id=1, source_target_pairs={{0,448},{8,456},{16,464},{24,472},{32,480},{40,488},{48,496},{56,5... | collective-permute-start | bytes 811016 | tf_op jit(solution)/shard_map/ppermute | solution.py:26
  45.3 3.8 %shard_map.86 = bf16[1056,128]{1,0:T(8,128)(2,1)S(1)} custom-call(s32[2]{0:T(128)S(1)} %pad_add_fusion.place_ref, s32[32,128]{1,0:T(8,128)S(1)} %get-tuple-element.8.bound_ref, bf16[2064,128]{1,0:T(8,128)(2,1)S(1)} %get-tuple-element.9.ka_ref, bf16[144,2176]{1,0:T(8,128)(2,1)S(1)} %get-tuple-element.10.vt_ref, ...), custom_call_target="tpu_custom_call" | custom-call | flops 4328521728 | bytes 1679360 | tf_op jit(solution)/shard_map/pallas_call | solution.py:57
  49.1 3.5 %collective-permute-start.3 = (bf16[1056,128]{1,0:T(8,128)(2,1)S(1)}, bf16[1056,128]{1,0:T(8,128)(2,1)S(1)}, u32[]{:S(2)}, u32[]{:S(2)}) collective-permute-start(bf16[1056,128]{1,0:T(8,128)(2,1)S(1)} %shard_map.86), channel_id=1, source_target_pairs={{0,64},{8,72},{16,80},{24,88},{32,96},{40,104},{48,112},{56,120},{... | collective-permute-start | bytes 811016 | tf_op jit(solution)/shard_map/ppermute | solution.py:26
  52.6 3.8 %shard_map.87 = bf16[1056,128]{1,0:T(8,128)(2,1)S(1)} custom-call(s32[2]{0:T(128)S(1)} %pad_add_fusion.place_ref, s32[32,128]{1,0:T(8,128)S(1)} %get-tuple-element.8.bound_ref, bf16[2064,128]{1,0:T(8,128)(2,1)S(1)} %get-tuple-element.9.ka_ref, bf16[144,2176]{1,0:T(8,128)(2,1)S(1)} %get-tuple-element.10.vt_ref, ...), custom_call_target="tpu_custom_call" | custom-call | flops 4328521728 | bytes 1679360 | tf_op jit(solution)/shard_map/pallas_call | solution.py:57
  56.4 4.3 %collective-permute-start.5 = (bf16[1056,128]{1,0:T(8,128)(2,1)S(1)}, bf16[1056,128]{1,0:T(8,128)(2,1)S(1)}, u32[]{:S(2)}, u32[]{:S(2)}) collective-permute-start(bf16[1056,128]{1,0:T(8,128)(2,1)S(1)} %shard_map.87), channel_id=1, source_target_pairs={{0,56},{8,0},{16,8},{24,16},{32,24},{40,32},{48,40},{56,48},{64,12... | collective-permute-start | bytes 811016 | tf_op jit(solution)/shard_map/ppermute | solution.py:26
  60.7 3.8 %shard_map.84.refs_0_ = bf16[1056,128]{1,0:T(8,128)(2,1)S(1)} custom-call(s32[2]{0:T(128)S(1)} %pad_add_fusion.place_ref, s32[32,128]{1,0:T(8,128)S(1)} %get-tuple-element.8.bound_ref, bf16[2064,128]{1,0:T(8,128)(2,1)S(1)} %get-tuple-element.9.ka_ref, bf16[144,2176]{1,0:T(8,128)(2,1)S(1)} %get-tuple-element.10.vt_ref, bf16[128,1024]{1,0:T(8,128)(2,1)S(1)} %shard_map.83.qt_ref), custom_call_target="tpu_custom_call" | custom-call | flops 4328521728 | bytes 1679360 | tf_op jit(solution)/shard_map/pallas_call | solution.py:57
  65.2 19.6 %all_to_all.20.got_ref = bf16[16,72,128]{2,1,0:T(8,128)(2,1)S(1)} all-to-all(bf16[16,72,128]{2,1,0:T(8,128)(2,1)S(1)} %shard_map.88), channel_id=1, replica_groups={{0,256,136,392,16,272,152,408,32,288,168,424,48,304,184,440},{64,320,20..., dimensions={0} | all-to-all | bytes 589824 | tf_op jit(solution)/shard_map/all_to_all | solution.py:45
  85.8 15.8 %all_to_all.21 = bf16[16,64,128]{2,1,0:T(8,128)(2,1)S(1)} all-to-all(bf16[16,64,128]{2,1,0:T(8,128)(2,1)S(1)} %broadcast_in_dim.15), channel_id=1, replica_groups={{0,256,136,392,16,272,152,408,32,288,168,424,48,304,184,440},{64,320,20..., dimensions={0} | all-to-all | bytes 524288 | tf_op jit(solution)/shard_map/all_to_all | solution.py:45
  101.5 1.9 %collective-permute-start.8 = (bf16[1024,128]{1,0:T(8,128)(2,1)S(1)}, bf16[1024,128]{1,0:T(8,128)(2,1)S(1)}, u32[]{:S(2)}, u32[]{:S(2)}) collective-permute-start(bf16[1024,128]{1,0:T(8,128)(2,1)S(1)} %bitcast.11), channel_id=1, source_target_pairs={{0,8},{8,16},{16,24},{24,32},{32,40},{40,48},{48,56},{56,0},{64,72... | collective-permute-start | bytes 786440 | tf_op jit(solution)/shard_map/ppermute | solution.py:26
  103.5 1.9 %collective-permute-start.7 = (bf16[1024,128]{1,0:T(8,128)(2,1)S(1)}, bf16[1024,128]{1,0:T(8,128)(2,1)S(1)}, u32[]{:S(2)}, u32[]{:S(2)}) collective-permute-start(bf16[1024,128]{1,0:T(8,128)(2,1)S(1)} %bitcast.12), channel_id=1, source_target_pairs={{0,448},{8,456},{16,464},{24,472},{32,480},{40,488},{48,496},{56,5... | collective-permute-start | bytes 786440 | tf_op jit(solution)/shard_map/ppermute | solution.py:26
  105.4 3.4 %collective-permute-start.6 = (bf16[1024,128]{1,0:T(8,128)(2,1)S(1)}, bf16[1024,128]{1,0:T(8,128)(2,1)S(1)}, u32[]{:S(2)}, u32[]{:S(2)}) collective-permute-start(bf16[1024,128]{1,0:T(8,128)(2,1)S(1)} %bitcast.13), channel_id=1, source_target_pairs={{0,64},{8,72},{16,80},{24,88},{32,96},{40,104},{48,112},{56,120},{... | collective-permute-start | bytes 786440 | tf_op jit(solution)/shard_map/ppermute | solution.py:26
  108.8 1.1 collective-permute-done.8.refs_3_
  110.6 3.4 %collective-permute-done.6.refs_1_ = bf16[1024,128]{1,0:T(8,128)(2,1)S(1)} collective-permute-done((bf16[1024,128]{1,0:T(8,128)(2,1)S(1)}, bf16[1024,128]{1,0:T(8,128)(2,1)S(1)}, u32[]{:S(2)}, u32[]{:S(2)}) %collective-permute-start.6) | collective-permute-done | bytes 262176 | tf_op jit(solution)/shard_map/ppermute | solution.py:26
  114.0 1.4 %shard_map.90 = bf16[256,256]{1,0:T(8,128)(2,1)S(1)} custom-call(s32[2]{0:T(128)S(1)} %pad_add_fusion.place_ref, bf16[2048,256]{1,0:T(8,128)(2,1)S(1)} %copy-done, bf16[1024,128]{1,0:T(8,128)(2,1)S(1)} %bitcast.14, bf16[1024,128]{1,0:T(8,128)(2,1)S(1)} %collective-permute-done.6.refs_1_, bf16[1024,128]{1,0:T(8,128)(2,1)S(1)} %collective-permute-done.7.refs_2_, ...), custom_call_target="tpu_custom_call" | custom-call | flops 268435456 | tf_op jit(solution)/shard_map/pallas_call | solution.py:57
  115.4 17.4 %all_to_all.22.got_ref = bf16[8,32,256]{2,1,0:T(8,128)(2,1)S(1)} all-to-all(bf16[8,32,256]{2,1,0:T(8,128)(2,1)S(1)} %bitcast.16), channel_id=1, replica_groups=mesh['ctx'=64,'kvh'=8] {'kvh'}, dimensions={0} | all-to-all | bytes 262144 | tf_op jit(solution)/shard_map/all_to_all | solution.py:365
  (24 shorter events, 4.2 us)
Async XLA Ops:
  0.0 18.5 %copy-start.1 = (bf16[2048,1,128]{2,0,1:T(8,128)(2,1)S(1)}, bf16[2048,1,128]{2,0,1:T(8,128)(2,1)}, u32[]{:S(2)}) copy-start(bf16[2048,1,128]{2,0,1:T(8,128)(2,1)} %param.9) | copy-start | bytes 1572868
  1.5 29.1 %all-to-all-start = ((bf16[16,64,128]{2,1,0:T(8,128)(2,1)}), bf16[16,64,128]{2,1,0:T(8,128)(2,1)S(1)}, u32[]{:S(2)}, u32[]{:S(2)}) async-start(bf16[16,64,128]{2,1,0:T(8,128)(2,1)} %broadcast_in_dim.14), calls=%async_computation | async-start | bytes 524288 | tf_op jit(solution)/shard_map/all_to_all | solution.py:45
  18.4 0.7 copy-start.4
  18.4 0.7 copy-start.5
  18.5 0.7 copy-start.3
  19.2 1.0 copy-start.2
  30.8 8.7 %collective-permute-start = (bf16[128,1024]{1,0:T(8,128)(2,1)S(1)}, bf16[128,1024]{1,0:T(8,128)(2,1)S(1)}, u32[]{:S(2)}, u32[]{:S(2)}) collective-permute-start(bf16[128,1024]{1,0:T(8,128)(2,1)S(1)} %shard_map.83.qt_ref), channel_id=1, source_target_pairs={{0,64},{8,72},{16,80},{24,88},{32,96},{40,104},{48,112},{56,120},{... | collective-permute-start | bytes 786440 | tf_op jit(solution)/shard_map/ppermute | solution.py:26
  32.9 19.8 %collective-permute-start.4 = (bf16[128,1024]{1,0:T(8,128)(2,1)S(1)}, bf16[128,1024]{1,0:T(8,128)(2,1)S(1)}, u32[]{:S(2)}, u32[]{:S(2)}) collective-permute-start(bf16[128,1024]{1,0:T(8,128)(2,1)S(1)} %shard_map.83.qt_ref), channel_id=1, source_target_pairs={{0,8},{8,16},{16,24},{24,32},{32,40},{40,48},{48,56},{56,0},{64,72... | collective-permute-start | bytes 786440 | tf_op jit(solution)/shard_map/ppermute | solution.py:26
  34.8 10.5 %collective-permute-start.2 = (bf16[128,1024]{1,0:T(8,128)(2,1)S(1)}, bf16[128,1024]{1,0:T(8,128)(2,1)S(1)}, u32[]{:S(2)}, u32[]{:S(2)}) collective-permute-start(bf16[128,1024]{1,0:T(8,128)(2,1)S(1)} %shard_map.83.qt_ref), channel_id=1, source_target_pairs={{0,448},{8,456},{16,464},{24,472},{32,480},{40,488},{48,496},{56,5... | collective-permute-start | bytes 786440 | tf_op jit(solution)/shard_map/ppermute | solution.py:26
  43.3 21.2 %collective-permute-start.1 = (bf16[1056,128]{1,0:T(8,128)(2,1)S(1)}, bf16[1056,128]{1,0:T(8,128)(2,1)S(1)}, u32[]{:S(2)}, u32[]{:S(2)}) collective-permute-start(bf16[1056,128]{1,0:T(8,128)(2,1)S(1)} %shard_map.85), channel_id=1, source_target_pairs={{0,448},{8,456},{16,464},{24,472},{32,480},{40,488},{48,496},{56,5... | collective-permute-start | bytes 811016 | tf_op jit(solution)/shard_map/ppermute | solution.py:26
  49.1 15.5 %collective-permute-start.3 = (bf16[1056,128]{1,0:T(8,128)(2,1)S(1)}, bf16[1056,128]{1,0:T(8,128)(2,1)S(1)}, u32[]{:S(2)}, u32[]{:S(2)}) collective-permute-start(bf16[1056,128]{1,0:T(8,128)(2,1)S(1)} %shard_map.86), channel_id=1, source_target_pairs={{0,64},{8,72},{16,80},{24,88},{32,96},{40,104},{48,112},{56,120},{... | collective-permute-start | bytes 811016 | tf_op jit(solution)/shard_map/ppermute | solution.py:26
  56.4 8.1 %collective-permute-start.5 = (bf16[1056,128]{1,0:T(8,128)(2,1)S(1)}, bf16[1056,128]{1,0:T(8,128)(2,1)S(1)}, u32[]{:S(2)}, u32[]{:S(2)}) collective-permute-start(bf16[1056,128]{1,0:T(8,128)(2,1)S(1)} %shard_map.87), channel_id=1, source_target_pairs={{0,56},{8,0},{16,8},{24,16},{32,24},{40,32},{48,40},{56,48},{64,12... | collective-permute-start | bytes 811016 | tf_op jit(solution)/shard_map/ppermute | solution.py:26
  65.2 48.8 %copy-start = (bf16[2048,256]{1,0:T(8,128)(2,1)S(1)}, bf16[2048,256]{1,0:T(8,128)(2,1)}, u32[]{:S(2)}) copy-start(bf16[2048,256]{1,0:T(8,128)(2,1)} %w_ref.1) | copy-start | bytes 3145732
  101.5 8.3 %collective-permute-start.8 = (bf16[1024,128]{1,0:T(8,128)(2,1)S(1)}, bf16[1024,128]{1,0:T(8,128)(2,1)S(1)}, u32[]{:S(2)}, u32[]{:S(2)}) collective-permute-start(bf16[1024,128]{1,0:T(8,128)(2,1)S(1)} %bitcast.11), channel_id=1, source_target_pairs={{0,8},{8,16},{16,24},{24,32},{32,40},{40,48},{48,56},{56,0},{64,72... | collective-permute-start | bytes 786440 | tf_op jit(solution)/shard_map/ppermute | solution.py:26
  103.5 7.1 %collective-permute-start.7 = (bf16[1024,128]{1,0:T(8,128)(2,1)S(1)}, bf16[1024,128]{1,0:T(8,128)(2,1)S(1)}, u32[]{:S(2)}, u32[]{:S(2)}) collective-permute-start(bf16[1024,128]{1,0:T(8,128)(2,1)S(1)} %bitcast.12), channel_id=1, source_target_pairs={{0,448},{8,456},{16,464},{24,472},{32,480},{40,488},{48,496},{56,5... | collective-permute-start | bytes 786440 | tf_op jit(solution)/shard_map/ppermute | solution.py:26
  105.4 8.6 %collective-permute-start.6 = (bf16[1024,128]{1,0:T(8,128)(2,1)S(1)}, bf16[1024,128]{1,0:T(8,128)(2,1)S(1)}, u32[]{:S(2)}, u32[]{:S(2)}) collective-permute-start(bf16[1024,128]{1,0:T(8,128)(2,1)S(1)} %bitcast.13), channel_id=1, source_target_pairs={{0,64},{8,72},{16,80},{24,88},{32,96},{40,104},{48,112},{56,120},{... | collective-permute-start | bytes 786440 | tf_op jit(solution)/shard_map/ppermute | solution.py:26

commit v6 on v5

--- a/solution.py
+++ b/solution.py
@@ -65,50 +65,105 @@
     )(*args)
 
 
-def prepare_body(live_ref, place_ref, seg_ref, k_ref, v_ref, fk_ref, fv_ref, ka_ref, vt_ref, b_ref):
-    live = live_ref[0]
-    slots, width = k_ref.shape
-    fresh = fk_ref.shape[0]
+def turned(kv_ref, span, fresh, live, vt_ref):
+    width = kv_ref.shape[1]
+    slots = span - fresh
     step = 256
-    first = k_ref[0:16, :].astype(F32)[0:1, :]
     for at in range(0, slots, step):
-        alive = lax.broadcasted_iota(jnp.int32, (step, width), 0) + at < live
-        keys = jnp.where(alive, k_ref[at : at + step, :].astype(F32), first)
-        ka_ref[at : at + step, :] = keys.astype(BF)
-        vals = jnp.where(alive, v_ref[at : at + step, :].astype(F32), 0.0)
+        vals = kv_ref[span + at : span + at + step, :].astype(F32)
         vt_ref[0:width, at : at + step] = vals.T.astype(BF)
         flags = lax.broadcasted_iota(jnp.int32, (16, step), 1) + at < live
         vt_ref[width:, at : at + step] = flags.astype(F32).astype(BF)
-    keys = jnp.concatenate([fk_ref[...].astype(F32), jnp.zeros((16 - fresh, width), F32)], 0)
-    ka_ref[slots:, :] = keys.astype(BF)
-    vals = jnp.concatenate([fv_ref[...].astype(F32), jnp.zeros((128 - fresh, width), F32)], 0)
-    vt_ref[0:width, slots:] = vals.T.astype(BF)
-    flags = lax.broadcasted_iota(jnp.int32, (16, 128), 1) < fresh
-    vt_ref[width:, slots:] = flags.astype(F32).astype(BF)
-    mine = fresh * (SIDE * place_ref[0] + place_ref[1])
+    if fresh:
+        vals = kv_ref[span + slots : 2 * span, :].astype(F32)
+        vals = jnp.concatenate([vals, jnp.zeros((128 - fresh, width), F32)], 0)
+        vt_ref[0:width, slots:] = vals.T.astype(BF)
+        flags = lax.broadcasted_iota(jnp.int32, (16, 128), 1) < 4
+        vt_ref[width:, slots:] = flags.astype(F32).astype(BF)
+
+
+def bounds_of(first, seg, live, b_ref):
     line = lax.broadcasted_iota(jnp.int32, (16, 128), 0)
     never = 1 << 30
     ends = jnp.full((16, 128), never, jnp.int32)
-    seg = seg_ref[...]
     spot = lax.broadcasted_iota(jnp.int32, seg.shape, 0) * 128 + lax.broadcasted_iota(
         jnp.int32, seg.shape, 1
     )
-    for j in range(fresh):
-        own = jnp.sum(jnp.where(spot == mine + j, seg, 0))
+    for j in range(4):
+        own = jnp.sum(jnp.where(spot == first + j, seg, 0))
         ends = jnp.where(line == j, jnp.sum((seg <= own).astype(jnp.int32)), ends)
-    b_ref[0:16, :] = jnp.where(line < fresh, line + mine, never)
+    b_ref[0:16, :] = jnp.where(line < 4, line + first, never)
     b_ref[16:32, :] = ends
+    b_ref[32:40, :] = jnp.zeros((8, 128), jnp.int32) + live
+
+
+def prepare_body(live_ref, place_ref, seg_ref, k_ref, v_ref, fk_ref, fv_ref, *outs):
+    live = live_ref[0]
+    slots, width = k_ref.shape
+    half = slots // 2
+    step = 256
+    first = k_ref[0:16, :].astype(F32)[0:1, :]
+    line = lax.broadcasted_iota(jnp.int32, (16, width), 0)
+    size = jnp.where(line == 0, live // 64, jnp.where(line == 1, lax.rem(live, 64), 0))
+    pad = jnp.zeros((16 - fk_ref.shape[0], width), F32)
+    for n in range(2):
+        kv_ref, vt_ref, b_ref = outs[3 * n : 3 * n + 3]
+        fresh = 16 * n
+        span = half + fresh
+        for at in range(0, half, step):
+            rows = slice(n * half + at, n * half + at + step)
+            alive = lax.broadcasted_iota(jnp.int32, (step, width), 0) + n * half + at < live
+            keys = jnp.where(alive, k_ref[rows, :].astype(F32), first)
+            kv_ref[at : at + step, :] = keys.astype(BF)
+            vals = jnp.where(alive, v_ref[rows, :].astype(F32), 0.0)
+            kv_ref[span + at : span + at + step, :] = vals.astype(BF)
+        if fresh:
+            for at, ref in ((half, fk_ref), (span + half, fv_ref)):
+                new = jnp.concatenate([ref[...].astype(F32), pad], 0)
+                kv_ref[at : at + 16, :] = new.astype(BF)
+        kv_ref[2 * span :, :] = size.astype(F32).astype(BF)
+        turned(kv_ref, span, fresh, live - n * half, vt_ref)
+        first_token = 4 * (SIDE * place_ref[0] + place_ref[1])
+        bounds_of(first_token, seg_ref[...], live - n * half, b_ref)
+
+
+def ready_shapes(half, n, width):
+    return [
+        jax.ShapeDtypeStruct((width + 16, half + 128 * n), BF),
+        jax.ShapeDtypeStruct((40, 128), jnp.int32),
+    ]
 
 
 def prepare(live, place, seg, keys, vals, fresh_k, fresh_v):
     slots, width = keys.shape
-    out = [
-        jax.ShapeDtypeStruct((slots + 16, width), BF),
-        jax.ShapeDtypeStruct((width + 16, slots + 128), BF),
-        jax.ShapeDtypeStruct((32, 128), jnp.int32),
-    ]
+    half = slots // 2
+    out = []
+    for n in range(2):
+        out.append(jax.ShapeDtypeStruct((2 * (half + 16 * n) + 16, width), BF))
+        out += ready_shapes(half, n, width)
     args = (live, place, seg, keys, vals, fresh_k, fresh_v)
-    return call(prepare_body, out, smem=2, args=args)
+    got = call(prepare_body, out, smem=2, args=args)
+    return tuple(got[:3]), tuple(got[3:])
+
+
+def unpack_body(place_ref, seg_ref, lower_ref, upper_ref, *outs):
+    for n, kv_ref in enumerate((lower_ref, upper_ref)):
+        vt_ref, b_ref = outs[2 * n : 2 * n + 2]
+        span = (kv_ref.shape[0] - 16) // 2
+        fresh = 16 * n
+        size = kv_ref[2 * span :, :].astype(F32)
+        live = jnp.max(64.0 * size[0:1] + size[1:2]).astype(jnp.int32)
+        live = live - n * (span - fresh)
+        turned(kv_ref, span, fresh, live, vt_ref)
+        from_z = lax.rem(place_ref[1] + SIDE - 1 + 2 * n, SIDE)
+        bounds_of(4 * (SIDE * place_ref[0] + from_z), seg_ref[...], live, b_ref)
+
+
+def unpack(place, seg, lower, upper):
+    half, width = (lower.shape[0] - 16) // 2, lower.shape[1]
+    out = ready_shapes(half, 0, width) + ready_shapes(half, 1, width)
+    got = call(unpack_body, out, smem=1, args=(place, seg, lower, upper))
+    return (lower, *got[:2]), (upper, *got[2:])
 
 
 def turn_body(bound_ref, q_ref, out_ref):
@@ -130,27 +185,40 @@
     return parts
 
 
-def attend_body(step, place_ref, bound_ref, ka_ref, vt_ref, qt_ref, o_ref, lse_ref, worst_ref):
-    keys, width = ka_ref.shape
-    slots = keys - 16
+def attend_body(step, begin, place_ref, qt_ref, *refs):
+    count = 2 if begin else 4
+    shards = [refs[3 * n : 3 * n + 3] for n in range(count)]
+    if begin:
+        acc_out, peak_out = refs[6:]
+    else:
+        acc_in, peak_in, o_ref, lse_ref, worst_ref = refs[12:]
+    width = qt_ref.shape[0]
+    slots = shards[0][1].shape[1]
     rows = 256
     heads = 16
     pieces = qt_ref.shape[1] // rows
     factor = LOG2E / width**0.5
-    opens = jnp.concatenate([bound_ref[0:16, :]] * 2, 1)
-    ends = jnp.concatenate([bound_ref[16:32, :]] * 2, 1)
     lane = lax.broadcasted_iota(jnp.int32, (16, rows), 1)
     which = coset(place_ref[0] - step[0], place_ref[1] - step[1])
-    cuts = [(at, 256) for at in range(0, slots, 256)] + [(slots, 16)]
-
-    def score(query, cut, i):
-        at, deep = cut
-        part = jnp.dot(ka_ref[at : at + deep, :], query, preferred_element_type=F32)
+
+    def cuts_of(n):
+        return [(n, at, 256) for at in range(0, slots, 256)] + [(n, slots, 16)] * (n % 2)
+
+    def score(query, cut, i, exact=False):
+        n, at, deep = cut
+        kv_ref, vt_ref, b_ref = shards[n]
+        part = jnp.dot(kv_ref[at : at + deep, :], query, preferred_element_type=F32)
         if deep == 16:
+            opens = jnp.concatenate([b_ref[0:16, :]] * 2, 1)
+            ends = jnp.concatenate([b_ref[16:32, :]] * 2, 1)
             member = 4 * i + lane // 64
             token = 32 * member_y(which, member) + 4 * (member // 2)
             token = token + lax.rem(lane // heads, 4)
             part = jnp.where((token >= opens) & (token < ends), part, -jnp.inf)
+        elif exact:
+            live = jnp.concatenate([b_ref[32:33, :]] * 2, 1)
+            alive = lax.broadcasted_iota(jnp.int32, (deep, rows), 0) + at < live
+            part = jnp.where(alive, part, -jnp.inf)
         return part
 
     def most(part):
@@ -158,11 +226,11 @@
 
     def weigh(part, cut, peak, total):
         weight = jnp.exp2((part - peak) * factor).astype(BF)
-        at, wide = cut
+        n, at, wide = cut
         if wide == 16:
             weight = jnp.concatenate([weight, jnp.zeros((112, rows), BF)], 0)
             wide = 128
-        add = jnp.dot(vt_ref[:, at : at + wide], weight, preferred_element_type=F32)
+        add = jnp.dot(shards[n][1][:, at : at + wide], weight, preferred_element_type=F32)
         return add if total is None else total + add
 
     def finish(i, peak, total):
@@ -179,35 +247,44 @@
     def query_of(i):
         return qt_ref[:, i * rows : (i + 1) * rows]
 
+    cuts = cuts_of(count - 2) + cuts_of(count - 1)
     worst = None
     todo = [(i, cut) for i in range(pieces) for cut in cuts]
     ahead = score(query_of(0), cuts[0], 0)
     peak_ahead = most(ahead)
-    for n, (i, cut) in enumerate(todo):
-        part, peak = ahead, peak_ahead
-        if n + 1 < len(todo):
-            j, later = todo[n + 1]
+    for at_todo, (i, cut) in enumerate(todo):
+        part, at = ahead, slice(i * rows, (i + 1) * rows)
+        if cut == cuts[0]:
+            peak = peak_ahead if begin else peak_in[0:1, at]
+            total = None if begin else acc_in[:, at]
+        if at_todo + 1 < len(todo):
+            j, later = todo[at_todo + 1]
             ahead = score(query_of(j), later, j)
-            if later == cuts[0]:
+            if begin and later == cuts[0]:
                 peak_ahead = most(ahead)
-        total = weigh(part, cut, peak, None if cut == cuts[0] else total)
+        total = weigh(part, cut, peak, total)
         if cut == cuts[-1]:
-            count = finish(i, peak, total)
-            worst = count if worst is None else jnp.maximum(worst, count)
+            if begin:
+                acc_out[:, at] = total
+                peak_out[:, at] = jnp.broadcast_to(peak, (8, rows))
+            else:
+                counts = finish(i, peak, total)
+                worst = counts if worst is None else jnp.maximum(worst, counts)
+    if begin:
+        return
     worst_ref[...] = jnp.broadcast_to(worst, worst_ref.shape)
 
     @pl.when(jnp.logical_not(jnp.max(worst_ref[0:1, :]) < HUGE))
     def _():
         def slow(i, carry):
-            at = pl.multiple_of(i * rows, rows)
-            query = qt_ref[:, pl.ds(at, rows)]
-            peak = None
-            for cut in cuts:
-                top = most(score(query, cut, i))
+            query = qt_ref[:, pl.ds(pl.multiple_of(i * rows, rows), rows)]
+            peak, total = None, None
+            every = sum((cuts_of(n) for n in range(count)), [])
+            for cut in every:
+                top = most(score(query, cut, i, True))
                 peak = top if peak is None else jnp.maximum(peak, top)
-            total = None
-            for cut in cuts:
-                total = weigh(score(query, cut, i), cut, peak, total)
+            for cut in every:
+                total = weigh(score(query, cut, i, True), cut, peak, total)
             finish(i, peak, total)
             return carry
 
@@ -218,16 +295,31 @@
     o_ref[pieces * rows :, :] = jnp.concatenate(parts, 0).astype(BF)
 
 
-def attend(place, bounds, ka, vt, query, step):
+def attend(place, query, near, step):
     width, rows = query.shape
     return call(
-        functools.partial(attend_body, step),
+        functools.partial(attend_body, step, True),
+        [
+            jax.ShapeDtypeStruct((width + 16, rows), F32),
+            jax.ShapeDtypeStruct((8, rows), F32),
+        ],
+        flops=8 * rows * near[0][1].shape[1] * 256,
+        moved=8 * near[0][0].size,
+        smem=1,
+        args=(place, query, *near[0], *near[1]),
+    )
+
+
+def attend_on(place, query, near, far, sums, step):
+    width, rows = query.shape
+    return call(
+        functools.partial(attend_body, step, False),
         jax.ShapeDtypeStruct((rows + TAIL, width), BF),
-        flops=8 * rows * ka.shape[0] * 256,
-        moved=(ka.size + vt.size + 2 * query.size) * 2,
+        flops=8 * rows * far[0][1].shape[1] * 256,
+        moved=8 * far[0][0].size,
         scratch=[pltpu.VMEM((4, 2, 128), F32), pltpu.VMEM((8, 256), F32)],
         smem=1,
-        args=(place, bounds, ka, vt, query),
+        args=(place, query, *near[0], *near[1], *far[0], *far[1], *sums),
     )
 
 
@@ -344,20 +436,25 @@
     me = lax.axis_index("ctx").astype(jnp.int32)
     place = jnp.stack([me // SIDE, me % SIDE])
     block, heads, width = queries.shape
-    ka, vt, bounds = prepare(
+    seg = segment.reshape(-1, 128)
+    near = prepare(
         cache_len,
         place,
-        segment.reshape(-1, 128),
+        seg,
         cache_keys[:, 0, :],
         cache_values[:, 0, :],
         new_keys[:, 0, :],
         new_values[:, 0, :],
     )
-    mine = turn(bounds, share(queries.reshape(block * heads, width)))
-    asked = [mine] + [shift(mine, step) for step in STEPS[1:]]
-    partial = [attend(place, bounds, ka, vt, q, step) for q, step in zip(asked, STEPS)]
-    back = [shift(p, (-s[0], -s[1])) for p, s in zip(partial[1:], STEPS[1:])]
-    own = second_merge(place, exchange(first_merge([partial[0]] + back)))
+    far = unpack(place, seg, shift(near[0][0], (0, 1)), shift(near[1][0], (0, -1)))
+    mine = turn(near[0][2], share(queries.reshape(block * heads, width)))
+    theirs = shift(mine, (1, 0))
+    sums = attend(place, mine, near, (0, 0))
+    their_sums = attend(place, theirs, near, (1, 0))
+    their_part = attend_on(place, theirs, near, far, their_sums, (1, 0))
+    part = attend_on(place, mine, near, far, sums, (0, 0))
+    part = first_merge([part, shift(their_part, (-1, 0))])
+    own = second_merge(place, exchange(part))
     mine = share(own)
     every = [mine] + [shift(mine, step) for step in STEPS[1:]]
     mixed = project(place, out_weight, every)

time: 134 us -> 133 us (level)
  starting transfers between devices: 41.6 us -> 37.7 us
  waiting for transfers between devices: 14.8 us -> 17.4 us
  Pallas kernels: 20.1 us -> 21.6 us
    ppermute x9 -> x7, waiting for transfers between devices: 5.57 us -> 15.3 us  [shift(): return lax.ppermute(value, 'ctx', pairs)]
    all_to_all x1, waiting for transfers between devices: 9.2 us -> 2.06 us  [exchange(): lax.all_to_all(value, 'ctx', 0, 0, axis_index_groups=cosets(), tiled=True)]
    ppermute x9 -> x7, starting transfers between devices: 25.3 us -> 21.5 us  [shift(): return lax.ppermute(value, 'ctx', pairs)]
    all_to_all x1, blocking collectives: 17.4 us -> 15.5 us  [local(): got = lax.all_to_all(mixed, 'kvh', 0, 0, tiled=True)]
    pallas_call x10 -> x11, Pallas kernels: 20.1 us -> 21.6 us  [call(): pl.pallas_call(body, out_shape=out_shape, in_specs=specs, out_specs=jax.t...]
  transfers between devices with their start and end apart: 10 -> 8, of which waited for: 5 -> 4; matrix products, arithmetic and copies ran while one was open for 0% -> 0% of each run, Pallas kernels for 12% -> 8%
where the time goes in v6:
time: 133 us; the launch traced here: 132 us
  blocking collectives  51.6 us (39%)
  starting transfers between devices  37.7 us (28%)
  Pallas kernels  21.6 us (16%)
  waiting for transfers between devices  17.4 us (13%)
  local copies, waits for them, and re-layouts  3.31 us (2%)
    all_to_all x2, blocking collectives, exchange(): lax.all_to_all(value, 'ctx', 0, 0, axis_index_groups=cosets(), tiled=True)  36 us
    pallas_call x11, Pallas kernels, call(): pl.pallas_call(body, out_shape=out_shape, in_specs=specs, out_specs=jax.t...  21.6 us
    ppermute x7, starting transfers between devices, shift(): return lax.ppermute(value, 'ctx', pairs)  21.5 us
    all_to_all x1, starting transfers between devices, exchange(): lax.all_to_all(value, 'ctx', 0, 0, axis_index_groups=cosets(), tiled=True)  16.2 us
    all_to_all x1, blocking collectives, local(): got = lax.all_to_all(mixed, 'kvh', 0, 0, tiled=True)  15.5 us
    ppermute x7, waiting for transfers between devices, shift(): return lax.ppermute(value, 'ctx', pairs)  15.3 us
  transfers between devices with their start and end apart: 8, of which 4 were waited for; matrix products, arithmetic and copies ran while one was open for 0% of the time, Pallas kernels for 8%

profile of v6, /device:TPU:1, one launch (start us, length us, event | category | flops | bytes accessed | tf_op | source)
XLA Modules:
  0.0 132.4 jit_solution(4299024421825359720)
XLA Ops:
  0.0 1.5 %broadcast_in_dim.14 = bf16[16,64,128]{2,1,0:T(8,128)(2,1)} broadcast(bf16[64,128]{1,0:T(8,128)(2,1)} %bitcast.23), dimensions={1,2} | broadcast | bytes 278528 | tf_op jit(solution)/shard_map/broadcast_in_dim | solution.py:49
  1.5 16.2 %all-to-all-start = ((bf16[16,64,128]{2,1,0:T(8,128)(2,1)}), bf16[16,64,128]{2,1,0:T(8,128)(2,1)S(1)}, u32[]{:S(2)}, u32[]{:S(2)}) async-start(bf16[16,64,128]{2,1,0:T(8,128)(2,1)} %broadcast_in_dim.14), calls=%async_computation | async-start | bytes 524288 | tf_op jit(solution)/shard_map/all_to_all | solution.py:45
  19.2 1.0 copy-done.2
  20.3 1.7 %shard_map.82 = (bf16[2064,128]{1,0:T(8,128)(2,1)S(1)}, bf16[144,1024]{1,0:T(8,128)(2,1)S(1)}, s32[40,128]{1,0:T(8,128)S(1)}, bf16[2096,128]{1,0:T(8,128)(2,1)S(...) custom-call(s32[1]{0:T(128)S(6)} %copy.9.live_ref, s32[2]{0:T(128)S(1)} %pad_add_fusion.place_ref, ...), custom_call_target="tpu_custom_call" | custom-call | tf_op jit(solution)/shard_map/pallas_call | solution.py:57
  22.0 4.7 %collective-permute-start.1 = (bf16[2096,128]{1,0:T(8,128)(2,1)S(1)}, bf16[2096,128]{1,0:T(8,128)(2,1)S(1)}, u32[]{:S(2)}, u32[]{:S(2)}) collective-permute-start(bf16[2096,128]{1,0:T(8,128)(2,1)S(1)} %get-tuple-element.22.refs_3_), channel_id=1, source_target_pairs={{0,56},{8,0},{16,8},{24,16},{32,24},{40,32},{48,40},{56,48},{64,12... | collective-permute-start | bytes 1609736 | tf_op jit(solution)/shard_map/ppermute | solution.py:26
  26.7 1.9 %collective-permute-start = (bf16[2064,128]{1,0:T(8,128)(2,1)S(1)}, bf16[2064,128]{1,0:T(8,128)(2,1)S(1)}, u32[]{:S(2)}, u32[]{:S(2)}) collective-permute-start(bf16[2064,128]{1,0:T(8,128)(2,1)S(1)} %get-tuple-element.20.refs_0_), channel_id=1, source_target_pairs={{0,8},{8,16},{16,24},{24,32},{32,40},{40,48},{48,56},{56,0},{64,72... | collective-permute-start | bytes 1585160 | tf_op jit(solution)/shard_map/ppermute | solution.py:26
  28.6 2.1 %all-to-all-done = bf16[16,64,128]{2,1,0:T(8,128)(2,1)S(1)} async-done(((bf16[16,64,128]{2,1,0:T(8,128)(2,1)}), bf16[16,64,128]{2,1,0:T(8,128)(2,1)S(1)}, u32[]{:S(2)}, u32[]{:S(2)}) %all-to-all-start) | async-done | bytes 262176 | tf_op jit(solution)/shard_map/all_to_all | solution.py:45
  30.8 2.1 %collective-permute-start.2 = (bf16[128,1024]{1,0:T(8,128)(2,1)S(1)}, bf16[128,1024]{1,0:T(8,128)(2,1)S(1)}, u32[]{:S(2)}, u32[]{:S(2)}) collective-permute-start(bf16[128,1024]{1,0:T(8,128)(2,1)S(1)} %shard_map.83.qt_ref), channel_id=1, source_target_pairs={{0,64},{8,72},{16,80},{24,88},{32,96},{40,104},{48,112},{56,120},{... | collective-permute-start | bytes 786440 | tf_op jit(solution)/shard_map/ppermute | solution.py:26
  32.9 8.9 %collective-permute-done.lower_ref.refs_6_ = bf16[2064,128]{1,0:T(8,128)(2,1)S(1)} collective-permute-done((bf16[2064,128]{1,0:T(8,128)(2,1)S(1)}, bf16[2064,128]{1,0:T(8,128)(2,1)S(1)}, u32[]{:S(2)}, u32[]{:S(2)}) %collective-permute-start) | collective-permute-done | bytes 528416 | tf_op jit(solution)/shard_map/ppermute | solution.py:26
  41.8 1.7 %shard_map.84 = (bf16[144,1024]{1,0:T(8,128)(2,1)S(1)}, s32[40,128]{1,0:T(8,128)S(1)}, bf16[144,1152]{1,0:T(8,128)(2,1)S(1)}, s32[40,128]{1,0:T(8,128)S(1)}) custom-call(s32[2]{0:T(128)S(1)} %pad_add_fusion.place_ref, s32[2,128]{1,0:T(2,128)S(1)} %bitcast.20, bf16[2064,128]{1,0:T(8,128)(2,1)S(1)} %collective-permute-done.lower_ref.refs_6_, ...), custom_call_target="tpu_custom_call" | custom-call | tf_op jit(solution)/shard_map/pallas_call | solution.py:57
  43.5 3.6 %shard_map.87 = (f32[144,1024]{1,0:T(8,128)S(1)}, f32[8,1024]{1,0:T(8,128)S(1)}) custom-call(s32[2]{0:T(128)S(1)} %pad_add_fusion.place_ref, bf16[128,1024]{1,0:T(8,128)(2,1)S(1)} %collective-permute-done.2.qt_ref, bf16[2064,128]{1,0:T(8,128)(2,1)S(1)} %get-tuple-element.20.refs_0_, bf16[144,1024]{1,0:T(8,128)(2,1)S(1)} %get-tuple-element.21.refs_1_, ...), custom_call_target="tpu_custom_call" | custom-call | flops 2147483648 | bytes 2113536 | tf_op jit(solution)/shard_map/pallas_call | solution.py:57
  47.1 3.8 %shard_map.88 = bf16[1056,128]{1,0:T(8,128)(2,1)S(1)} custom-call(s32[2]{0:T(128)S(1)} %pad_add_fusion.place_ref, bf16[128,1024]{1,0:T(8,128)(2,1)S(1)} %collective-permute-done.2.qt_ref, bf16[2064,128]{1,0:T(8,128)(2,1)S(1)} %get-tuple-element.20.refs_0_, bf16[144,1024]{1,0:T(8,128)(2,1)S(1)} %get-tuple-element.21.refs_1_, ...), custom_call_target="tpu_custom_call" | custom-call | flops 2147483648 | bytes 2113536 | tf_op jit(solution)/shard_map/pallas_call | solution.py:57
  50.9 4.4 %collective-permute-start.3 = (bf16[1056,128]{1,0:T(8,128)(2,1)S(1)}, bf16[1056,128]{1,0:T(8,128)(2,1)S(1)}, u32[]{:S(2)}, u32[]{:S(2)}) collective-permute-start(bf16[1056,128]{1,0:T(8,128)(2,1)S(1)} %shard_map.88), channel_id=1, source_target_pairs={{0,448},{8,456},{16,464},{24,472},{32,480},{40,488},{48,496},{56,5... | collective-permute-start | bytes 811016 | tf_op jit(solution)/shard_map/ppermute | solution.py:26
  55.3 3.6 %shard_map.85 = (f32[144,1024]{1,0:T(8,128)S(1)}, f32[8,1024]{1,0:T(8,128)S(1)}) custom-call(s32[2]{0:T(128)S(1)} %pad_add_fusion.place_ref, bf16[128,1024]{1,0:T(8,128)(2,1)S(1)} %shard_map.83.qt_ref, bf16[2064,128]{1,0:T(8,128)(2,1)S(1)} %get-tuple-element.20.refs_0_, bf16[144,1024]{1,0:T(8,128)(2,1)S(1)} %get-tuple-element.21.refs_1_, ...), custom_call_target="tpu_custom_call" | custom-call | flops 2147483648 | bytes 2113536 | tf_op jit(solution)/shard_map/pallas_call | solution.py:57
  58.9 3.8 %shard_map.86.refs_0_ = bf16[1056,128]{1,0:T(8,128)(2,1)S(1)} custom-call(s32[2]{0:T(128)S(1)} %pad_add_fusion.place_ref, bf16[128,1024]{1,0:T(8,128)(2,1)S(1)} %shard_map.83.qt_ref, bf16[2064,128]{1,0:T(8,128)(2,1)S(1)} %get-tuple-element.20.refs_0_, bf16[144,1024]{1,0:T(8,128)(2,1)S(1)} %get-tuple-element.21.refs_1_, ...), custom_call_target="tpu_custom_call" | custom-call | flops 2147483648 | bytes 2113536 | tf_op jit(solution)/shard_map/pallas_call | solution.py:57
  63.0 19.7 %all_to_all.20.got_ref = bf16[16,72,128]{2,1,0:T(8,128)(2,1)S(1)} all-to-all(bf16[16,72,128]{2,1,0:T(8,128)(2,1)S(1)} %shard_map.89), channel_id=1, replica_groups={{0,256,136,392,16,272,152,408,32,288,168,424,48,304,184,440},{64,320,20..., dimensions={0} | all-to-all | bytes 589824 | tf_op jit(solution)/shard_map/all_to_all | solution.py:45
  83.7 16.3 %all_to_all.21 = bf16[16,64,128]{2,1,0:T(8,128)(2,1)S(1)} all-to-all(bf16[16,64,128]{2,1,0:T(8,128)(2,1)S(1)} %broadcast_in_dim.15), channel_id=1, replica_groups={{0,256,136,392,16,272,152,408,32,288,168,424,48,304,184,440},{64,320,20..., dimensions={0} | all-to-all | bytes 524288 | tf_op jit(solution)/shard_map/all_to_all | solution.py:45
  100.0 4.1 %collective-permute-start.4 = (bf16[1024,128]{1,0:T(8,128)(2,1)S(1)}, bf16[1024,128]{1,0:T(8,128)(2,1)S(1)}, u32[]{:S(2)}, u32[]{:S(2)}) collective-permute-start(bf16[1024,128]{1,0:T(8,128)(2,1)S(1)} %bitcast.11), channel_id=1, source_target_pairs={{0,64},{8,72},{16,80},{24,88},{32,96},{40,104},{48,112},{56,120},{... | collective-permute-start | bytes 786440 | tf_op jit(solution)/shard_map/ppermute | solution.py:26
  104.2 2.3 %collective-permute-start.5 = (bf16[1024,128]{1,0:T(8,128)(2,1)S(1)}, bf16[1024,128]{1,0:T(8,128)(2,1)S(1)}, u32[]{:S(2)}, u32[]{:S(2)}) collective-permute-start(bf16[1024,128]{1,0:T(8,128)(2,1)S(1)} %bitcast.12), channel_id=1, source_target_pairs={{0,448},{8,456},{16,464},{24,472},{32,480},{40,488},{48,496},{56,5... | collective-permute-start | bytes 786440 | tf_op jit(solution)/shard_map/ppermute | solution.py:26
  106.5 1.9 %collective-permute-start.6 = (bf16[1024,128]{1,0:T(8,128)(2,1)S(1)}, bf16[1024,128]{1,0:T(8,128)(2,1)S(1)}, u32[]{:S(2)}, u32[]{:S(2)}) collective-permute-start(bf16[1024,128]{1,0:T(8,128)(2,1)S(1)} %bitcast.13), channel_id=1, source_target_pairs={{0,8},{8,16},{16,24},{24,32},{32,40},{40,48},{48,56},{56,0},{64,72... | collective-permute-start | bytes 786440 | tf_op jit(solution)/shard_map/ppermute | solution.py:26
  108.5 3.1 %collective-permute-done.5.refs_2_ = bf16[1024,128]{1,0:T(8,128)(2,1)S(1)} collective-permute-done((bf16[1024,128]{1,0:T(8,128)(2,1)S(1)}, bf16[1024,128]{1,0:T(8,128)(2,1)S(1)}, u32[]{:S(2)}, u32[]{:S(2)}) %collective-permute-start.5) | collective-permute-done | bytes 262176 | tf_op jit(solution)/shard_map/ppermute | solution.py:26
  111.6 3.3 %collective-permute-done.6.refs_3_ = bf16[1024,128]{1,0:T(8,128)(2,1)S(1)} collective-permute-done((bf16[1024,128]{1,0:T(8,128)(2,1)S(1)}, bf16[1024,128]{1,0:T(8,128)(2,1)S(1)}, u32[]{:S(2)}, u32[]{:S(2)}) %collective-permute-start.6) | collective-permute-done | bytes 262176 | tf_op jit(solution)/shard_map/ppermute | solution.py:26
  114.8 1.4 %shard_map.91 = bf16[256,256]{1,0:T(8,128)(2,1)S(1)} custom-call(s32[2]{0:T(128)S(1)} %pad_add_fusion.place_ref, bf16[2048,256]{1,0:T(8,128)(2,1)S(1)} %copy-done, bf16[1024,128]{1,0:T(8,128)(2,1)S(1)} %bitcast.14, bf16[1024,128]{1,0:T(8,128)(2,1)S(1)} %collective-permute-done.4.refs_1_, bf16[1024,128]{1,0:T(8,128)(2,1)S(1)} %collective-permute-done.5.refs_2_, ...), custom_call_target="tpu_custom_call" | custom-call | flops 268435456 | tf_op jit(solution)/shard_map/pallas_call | solution.py:57
  116.3 15.5 %all_to_all.22.got_ref = bf16[8,32,256]{2,1,0:T(8,128)(2,1)S(1)} all-to-all(bf16[8,32,256]{2,1,0:T(8,128)(2,1)S(1)} %bitcast.16), channel_id=1, replica_groups=mesh['ctx'=64,'kvh'=8] {'kvh'}, dimensions={0} | all-to-all | bytes 262144 | tf_op jit(solution)/shard_map/all_to_all | solution.py:462
  (21 shorter events, 2.8 us)
Async XLA Ops:
  0.0 18.5 %copy-start.1 = (bf16[2048,1,128]{2,0,1:T(8,128)(2,1)S(1)}, bf16[2048,1,128]{2,0,1:T(8,128)(2,1)}, u32[]{:S(2)}) copy-start(bf16[2048,1,128]{2,0,1:T(8,128)(2,1)} %param.9) | copy-start | bytes 1572868
  1.5 29.1 %all-to-all-start = ((bf16[16,64,128]{2,1,0:T(8,128)(2,1)}), bf16[16,64,128]{2,1,0:T(8,128)(2,1)S(1)}, u32[]{:S(2)}, u32[]{:S(2)}) async-start(bf16[16,64,128]{2,1,0:T(8,128)(2,1)} %broadcast_in_dim.14), calls=%async_computation | async-start | bytes 524288 | tf_op jit(solution)/shard_map/all_to_all | solution.py:45
  18.4 0.7 copy-start.4
  18.4 0.7 copy-start.5
  18.5 0.7 copy-start.3
  19.2 1.0 copy-start.2
  22.0 19.8 %collective-permute-start.1 = (bf16[2096,128]{1,0:T(8,128)(2,1)S(1)}, bf16[2096,128]{1,0:T(8,128)(2,1)S(1)}, u32[]{:S(2)}, u32[]{:S(2)}) collective-permute-start(bf16[2096,128]{1,0:T(8,128)(2,1)S(1)} %get-tuple-element.22.refs_3_), channel_id=1, source_target_pairs={{0,56},{8,0},{16,8},{24,16},{32,24},{40,32},{48,40},{56,48},{64,12... | collective-permute-start | bytes 1609736 | tf_op jit(solution)/shard_map/ppermute | solution.py:26
  26.7 15.1 %collective-permute-start = (bf16[2064,128]{1,0:T(8,128)(2,1)S(1)}, bf16[2064,128]{1,0:T(8,128)(2,1)S(1)}, u32[]{:S(2)}, u32[]{:S(2)}) collective-permute-start(bf16[2064,128]{1,0:T(8,128)(2,1)S(1)} %get-tuple-element.20.refs_0_), channel_id=1, source_target_pairs={{0,8},{8,16},{16,24},{24,32},{32,40},{40,48},{48,56},{56,0},{64,72... | collective-permute-start | bytes 1585160 | tf_op jit(solution)/shard_map/ppermute | solution.py:26
  30.8 12.7 %collective-permute-start.2 = (bf16[128,1024]{1,0:T(8,128)(2,1)S(1)}, bf16[128,1024]{1,0:T(8,128)(2,1)S(1)}, u32[]{:S(2)}, u32[]{:S(2)}) collective-permute-start(bf16[128,1024]{1,0:T(8,128)(2,1)S(1)} %shard_map.83.qt_ref), channel_id=1, source_target_pairs={{0,64},{8,72},{16,80},{24,88},{32,96},{40,104},{48,112},{56,120},{... | collective-permute-start | bytes 786440 | tf_op jit(solution)/shard_map/ppermute | solution.py:26
  50.9 11.8 %collective-permute-start.3 = (bf16[1056,128]{1,0:T(8,128)(2,1)S(1)}, bf16[1056,128]{1,0:T(8,128)(2,1)S(1)}, u32[]{:S(2)}, u32[]{:S(2)}) collective-permute-start(bf16[1056,128]{1,0:T(8,128)(2,1)S(1)} %shard_map.88), channel_id=1, source_target_pairs={{0,448},{8,456},{16,464},{24,472},{32,480},{40,488},{48,496},{56,5... | collective-permute-start | bytes 811016 | tf_op jit(solution)/shard_map/ppermute | solution.py:26
  63.0 51.8 %copy-start = (bf16[2048,256]{1,0:T(8,128)(2,1)S(1)}, bf16[2048,256]{1,0:T(8,128)(2,1)}, u32[]{:S(2)}) copy-start(bf16[2048,256]{1,0:T(8,128)(2,1)} %w_ref.1) | copy-start | bytes 3145732
  100.0 8.4 %collective-permute-start.4 = (bf16[1024,128]{1,0:T(8,128)(2,1)S(1)}, bf16[1024,128]{1,0:T(8,128)(2,1)S(1)}, u32[]{:S(2)}, u32[]{:S(2)}) collective-permute-start(bf16[1024,128]{1,0:T(8,128)(2,1)S(1)} %bitcast.11), channel_id=1, source_target_pairs={{0,64},{8,72},{16,80},{24,88},{32,96},{40,104},{48,112},{56,120},{... | collective-permute-start | bytes 786440 | tf_op jit(solution)/shard_map/ppermute | solution.py:26
  104.2 7.4 %collective-permute-start.5 = (bf16[1024,128]{1,0:T(8,128)(2,1)S(1)}, bf16[1024,128]{1,0:T(8,128)(2,1)S(1)}, u32[]{:S(2)}, u32[]{:S(2)}) collective-permute-start(bf16[1024,128]{1,0:T(8,128)(2,1)S(1)} %bitcast.12), channel_id=1, source_target_pairs={{0,448},{8,456},{16,464},{24,472},{32,480},{40,488},{48,496},{56,5... | collective-permute-start | bytes 786440 | tf_op jit(solution)/shard_map/ppermute | solution.py:26
  106.5 8.3 %collective-permute-start.6 = (bf16[1024,128]{1,0:T(8,128)(2,1)S(1)}, bf16[1024,128]{1,0:T(8,128)(2,1)S(1)}, u32[]{:S(2)}, u32[]{:S(2)}) collective-permute-start(bf16[1024,128]{1,0:T(8,128)(2,1)S(1)} %bitcast.13), channel_id=1, source_target_pairs={{0,8},{8,16},{16,24},{24,32},{32,40},{40,48},{48,56},{56,0},{64,72... | collective-permute-start | bytes 786440 | tf_op jit(solution)/shard_map/ppermute | solution.py:26

commit v7 on v6

--- a/solution.py
+++ b/solution.py
@@ -86,12 +86,18 @@
     line = lax.broadcasted_iota(jnp.int32, (16, 128), 0)
     never = 1 << 30
     ends = jnp.full((16, 128), never, jnp.int32)
+    seg = seg.astype(F32)
     spot = lax.broadcasted_iota(jnp.int32, seg.shape, 0) * 128 + lax.broadcasted_iota(
         jnp.int32, seg.shape, 1
     )
+
+    def whole(part):
+        return jnp.sum(jnp.sum(part, axis=0, keepdims=True), axis=1, keepdims=True)
+
     for j in range(4):
-        own = jnp.sum(jnp.where(spot == first + j, seg, 0))
-        ends = jnp.where(line == j, jnp.sum((seg <= own).astype(jnp.int32)), ends)
+        own = whole(jnp.where(spot == first + j, seg, 0.0))
+        count = whole(jnp.where(seg <= own, 1.0, 0.0))
+        ends = jnp.where(line == j, count.astype(jnp.int32), ends)
     b_ref[0:16, :] = jnp.where(line < 4, line + first, never)
     b_ref[16:32, :] = ends
     b_ref[32:40, :] = jnp.zeros((8, 128), jnp.int32) + live
@@ -124,7 +130,10 @@
         kv_ref[2 * span :, :] = size.astype(F32).astype(BF)
         turned(kv_ref, span, fresh, live - n * half, vt_ref)
         first_token = 4 * (SIDE * place_ref[0] + place_ref[1])
-        bounds_of(first_token, seg_ref[...], live - n * half, b_ref)
+        if fresh:
+            bounds_of(first_token, seg_ref[...], live - n * half, b_ref)
+        else:
+            b_ref[...] = jnp.zeros(b_ref.shape, jnp.int32) + live
 
 
 def ready_shapes(half, n, width):
@@ -146,7 +155,7 @@
     return tuple(got[:3]), tuple(got[3:])
 
 
-def unpack_body(place_ref, seg_ref, lower_ref, upper_ref, *outs):
+def unpack_body(place_ref, seg_ref, lower_ref, upper_ref, one_ref, two_ref, *outs):
     for n, kv_ref in enumerate((lower_ref, upper_ref)):
         vt_ref, b_ref = outs[2 * n : 2 * n + 2]
         span = (kv_ref.shape[0] - 16) // 2
@@ -155,14 +164,17 @@
         live = jnp.max(64.0 * size[0:1] + size[1:2]).astype(jnp.int32)
         live = live - n * (span - fresh)
         turned(kv_ref, span, fresh, live, vt_ref)
-        from_z = lax.rem(place_ref[1] + SIDE - 1 + 2 * n, SIDE)
-        bounds_of(4 * (SIDE * place_ref[0] + from_z), seg_ref[...], live, b_ref)
-
-
-def unpack(place, seg, lower, upper):
+        from_z = lax.rem(place_ref[1] + 1, SIDE)
+        if fresh:
+            bounds_of(4 * (SIDE * place_ref[0] + from_z), seg_ref[...], live, b_ref)
+        else:
+            b_ref[...] = jnp.zeros(b_ref.shape, jnp.int32) + live
+
+
+def unpack(place, seg, lower, upper, one, two):
     half, width = (lower.shape[0] - 16) // 2, lower.shape[1]
     out = ready_shapes(half, 0, width) + ready_shapes(half, 1, width)
-    got = call(unpack_body, out, smem=1, args=(place, seg, lower, upper))
+    got = call(unpack_body, out, smem=1, args=(place, seg, lower, upper, one, two))
     return (lower, *got[:2]), (upper, *got[2:])
 
 
@@ -446,11 +458,12 @@
         new_keys[:, 0, :],
         new_values[:, 0, :],
     )
-    far = unpack(place, seg, shift(near[0][0], (0, 1)), shift(near[1][0], (0, -1)))
+    lower, upper = shift(near[0][0], (0, 1)), shift(near[1][0], (0, -1))
     mine = turn(near[0][2], share(queries.reshape(block * heads, width)))
     theirs = shift(mine, (1, 0))
     sums = attend(place, mine, near, (0, 0))
     their_sums = attend(place, theirs, near, (1, 0))
+    far = unpack(place, seg, lower, upper, sums[1], their_sums[1])
     their_part = attend_on(place, theirs, near, far, their_sums, (1, 0))
     part = attend_on(place, mine, near, far, sums, (0, 0))
     part = first_merge([part, shift(their_part, (-1, 0))])

time: 133 us -> 124 us (0.932)
  waiting for transfers between devices: 17.4 us -> 12 us
  starting transfers between devices: 37.7 us -> 34.3 us
  blocking collectives: 51.6 us -> 53.3 us
  Pallas kernels: 21.6 us -> 20 us
    ppermute x7, waiting for transfers between devices: 15.3 us -> 9.19 us  [shift(): return lax.ppermute(value, 'ctx', pairs)]
    ppermute x7, starting transfers between devices: 21.5 us -> 18.1 us  [shift(): return lax.ppermute(value, 'ctx', pairs)]
    pallas_call x11, Pallas kernels: 21.6 us -> 20 us  [call(): pl.pallas_call(body, out_shape=out_shape, in_specs=specs, out_specs=jax.t...]
  transfers between devices with their start and end apart: 8 -> 8, of which waited for: 4 -> 6; matrix products, arithmetic and copies ran while one was open for 0% -> 0% of each run, Pallas kernels for 8% -> 10%
where the time goes in v7:
time: 124 us
  blocking collectives  53.3 us (43%)
  starting transfers between devices  34.3 us (28%)
  Pallas kernels  20 us (16%)
  waiting for transfers between devices  12 us (10%)
  local copies, waits for them, and re-layouts  3.31 us (3%)
    all_to_all x2, blocking collectives, exchange(): lax.all_to_all(value, 'ctx', 0, 0, axis_index_groups=cosets(), tiled=True)  36.6 us
    pallas_call x11, Pallas kernels, call(): pl.pallas_call(body, out_shape=out_shape, in_specs=specs, out_specs=jax.t...  20 us
    ppermute x7, starting transfers between devices, shift(): return lax.ppermute(value, 'ctx', pairs)  18.1 us
    all_to_all x1, blocking collectives, local(): got = lax.all_to_all(mixed, 'kvh', 0, 0, tiled=True)  16.8 us
    all_to_all x1, starting transfers between devices, exchange(): lax.all_to_all(value, 'ctx', 0, 0, axis_index_groups=cosets(), tiled=True)  16.2 us
    ppermute x7, waiting for transfers between devices, shift(): return lax.ppermute(value, 'ctx', pairs)  9.19 us
    all_to_all x1, waiting for transfers between devices, exchange(): lax.all_to_all(value, 'ctx', 0, 0, axis_index_groups=cosets(), tiled=True)  2.83 us
  transfers between devices with their start and end apart: 8, of which 6 were waited for; matrix products, arithmetic and copies ran while one was open for 0% of the time, Pallas kernels for 10%

profile of v7, /device:TPU:1, one launch (start us, length us, event | category | flops | bytes accessed | tf_op | source)
XLA Modules:
  0.0 123.9 jit_solution(17808587332755517260)
XLA Ops:
  0.0 1.5 %broadcast_in_dim.14 = bf16[16,64,128]{2,1,0:T(8,128)(2,1)} broadcast(bf16[64,128]{1,0:T(8,128)(2,1)} %bitcast.23), dimensions={1,2} | broadcast | bytes 278528 | tf_op jit(solution)/shard_map/broadcast_in_dim | solution.py:49
  1.5 16.2 %all-to-all-start = ((bf16[16,64,128]{2,1,0:T(8,128)(2,1)}), bf16[16,64,128]{2,1,0:T(8,128)(2,1)S(1)}, u32[]{:S(2)}, u32[]{:S(2)}) async-start(bf16[16,64,128]{2,1,0:T(8,128)(2,1)} %broadcast_in_dim.14), calls=%async_computation | async-start | bytes 524288 | tf_op jit(solution)/shard_map/all_to_all | solution.py:45
  19.2 1.0 copy-done.2
  20.3 0.9 shard_map.82
  21.2 4.7 %collective-permute-start.1 = (bf16[2096,128]{1,0:T(8,128)(2,1)S(1)}, bf16[2096,128]{1,0:T(8,128)(2,1)S(1)}, u32[]{:S(2)}, u32[]{:S(2)}) collective-permute-start(bf16[2096,128]{1,0:T(8,128)(2,1)S(1)} %get-tuple-element.22.refs_3_), channel_id=1, source_target_pairs={{0,56},{8,0},{16,8},{24,16},{32,24},{40,32},{48,40},{56,48},{64,12... | collective-permute-start | bytes 1609736 | tf_op jit(solution)/shard_map/ppermute | solution.py:26
  25.9 1.9 %collective-permute-start = (bf16[2064,128]{1,0:T(8,128)(2,1)S(1)}, bf16[2064,128]{1,0:T(8,128)(2,1)S(1)}, u32[]{:S(2)}, u32[]{:S(2)}) collective-permute-start(bf16[2064,128]{1,0:T(8,128)(2,1)S(1)} %get-tuple-element.20.refs_0_), channel_id=1, source_target_pairs={{0,8},{8,16},{16,24},{24,32},{32,40},{40,48},{48,56},{56,0},{64,72... | collective-permute-start | bytes 1585160 | tf_op jit(solution)/shard_map/ppermute | solution.py:26
  27.8 2.8 %all-to-all-done = bf16[16,64,128]{2,1,0:T(8,128)(2,1)S(1)} async-done(((bf16[16,64,128]{2,1,0:T(8,128)(2,1)}), bf16[16,64,128]{2,1,0:T(8,128)(2,1)S(1)}, u32[]{:S(2)}, u32[]{:S(2)}) %all-to-all-start) | async-done | bytes 262176 | tf_op jit(solution)/shard_map/all_to_all | solution.py:45
  30.8 2.1 %collective-permute-start.2 = (bf16[128,1024]{1,0:T(8,128)(2,1)S(1)}, bf16[128,1024]{1,0:T(8,128)(2,1)S(1)}, u32[]{:S(2)}, u32[]{:S(2)}) collective-permute-start(bf16[128,1024]{1,0:T(8,128)(2,1)S(1)} %shard_map.83.qt_ref), channel_id=1, source_target_pairs={{0,64},{8,72},{16,80},{24,88},{32,96},{40,104},{48,112},{56,120},{... | collective-permute-start | bytes 786440 | tf_op jit(solution)/shard_map/ppermute | solution.py:26
  32.9 3.6 %shard_map.84 = (f32[144,1024]{1,0:T(8,128)S(1)}, f32[8,1024]{1,0:T(8,128)S(1)}) custom-call(s32[2]{0:T(128)S(1)} %pad_add_fusion.place_ref, bf16[128,1024]{1,0:T(8,128)(2,1)S(1)} %shard_map.83.qt_ref, bf16[2064,128]{1,0:T(8,128)(2,1)S(1)} %get-tuple-element.20.refs_0_, bf16[144,1024]{1,0:T(8,128)(2,1)S(1)} %get-tuple-element.21.refs_1_, ...), custom_call_target="tpu_custom_call" | custom-call | flops 2147483648 | bytes 2113536 | tf_op jit(solution)/shard_map/pallas_call | solution.py:57
  36.5 3.0 %collective-permute-done.2.qt_ref = bf16[128,1024]{1,0:T(8,128)(2,1)S(1)} collective-permute-done((bf16[128,1024]{1,0:T(8,128)(2,1)S(1)}, bf16[128,1024]{1,0:T(8,128)(2,1)S(1)}, u32[]{:S(2)}, u32[]{:S(2)}) %collective-permute-start.2) | collective-permute-done | bytes 262176 | tf_op jit(solution)/shard_map/ppermute | solution.py:26
  39.5 3.6 %shard_map.85 = (f32[144,1024]{1,0:T(8,128)S(1)}, f32[8,1024]{1,0:T(8,128)S(1)}) custom-call(s32[2]{0:T(128)S(1)} %pad_add_fusion.place_ref, bf16[128,1024]{1,0:T(8,128)(2,1)S(1)} %collective-permute-done.2.qt_ref, bf16[2064,128]{1,0:T(8,128)(2,1)S(1)} %get-tuple-element.20.refs_0_, bf16[144,1024]{1,0:T(8,128)(2,1)S(1)} %get-tuple-element.21.refs_1_, ...), custom_call_target="tpu_custom_call" | custom-call | flops 2147483648 | bytes 2113536 | tf_op jit(solution)/shard_map/pallas_call | solution.py:57
  44.1 3.8 %shard_map.88 = bf16[1056,128]{1,0:T(8,128)(2,1)S(1)} custom-call(s32[2]{0:T(128)S(1)} %pad_add_fusion.place_ref, bf16[128,1024]{1,0:T(8,128)(2,1)S(1)} %collective-permute-done.2.qt_ref, bf16[2064,128]{1,0:T(8,128)(2,1)S(1)} %get-tuple-element.20.refs_0_, bf16[144,1024]{1,0:T(8,128)(2,1)S(1)} %get-tuple-element.21.refs_1_, ...), custom_call_target="tpu_custom_call" | custom-call | flops 2147483648 | bytes 2113536 | tf_op jit(solution)/shard_map/pallas_call | solution.py:57
  47.8 2.2 %collective-permute-start.3 = (bf16[1056,128]{1,0:T(8,128)(2,1)S(1)}, bf16[1056,128]{1,0:T(8,128)(2,1)S(1)}, u32[]{:S(2)}, u32[]{:S(2)}) collective-permute-start(bf16[1056,128]{1,0:T(8,128)(2,1)S(1)} %shard_map.88), channel_id=1, source_target_pairs={{0,448},{8,456},{16,464},{24,472},{32,480},{40,488},{48,496},{56,5... | collective-permute-start | bytes 811016 | tf_op jit(solution)/shard_map/ppermute | solution.py:26
  50.1 3.8 %shard_map.87.refs_0_ = bf16[1056,128]{1,0:T(8,128)(2,1)S(1)} custom-call(s32[2]{0:T(128)S(1)} %pad_add_fusion.place_ref, bf16[128,1024]{1,0:T(8,128)(2,1)S(1)} %shard_map.83.qt_ref, bf16[2064,128]{1,0:T(8,128)(2,1)S(1)} %get-tuple-element.20.refs_0_, bf16[144,1024]{1,0:T(8,128)(2,1)S(1)} %get-tuple-element.21.refs_1_, ...), custom_call_target="tpu_custom_call" | custom-call | flops 2147483648 | bytes 2113536 | tf_op jit(solution)/shard_map/pallas_call | solution.py:57
  53.8 1.2 collective-permute-done.3.refs_1_
  55.4 20.1 %all_to_all.20.got_ref = bf16[16,72,128]{2,1,0:T(8,128)(2,1)S(1)} all-to-all(bf16[16,72,128]{2,1,0:T(8,128)(2,1)S(1)} %shard_map.89), channel_id=1, replica_groups={{0,256,136,392,16,272,152,408,32,288,168,424,48,304,184,440},{64,320,20..., dimensions={0} | all-to-all | bytes 589824 | tf_op jit(solution)/shard_map/all_to_all | solution.py:45
  76.5 16.4 %all_to_all.21 = bf16[16,64,128]{2,1,0:T(8,128)(2,1)S(1)} all-to-all(bf16[16,64,128]{2,1,0:T(8,128)(2,1)S(1)} %broadcast_in_dim.15), channel_id=1, replica_groups={{0,256,136,392,16,272,152,408,32,288,168,424,48,304,184,440},{64,320,20..., dimensions={0} | all-to-all | bytes 524288 | tf_op jit(solution)/shard_map/all_to_all | solution.py:45
  92.9 1.9 %collective-permute-start.6 = (bf16[1024,128]{1,0:T(8,128)(2,1)S(1)}, bf16[1024,128]{1,0:T(8,128)(2,1)S(1)}, u32[]{:S(2)}, u32[]{:S(2)}) collective-permute-start(bf16[1024,128]{1,0:T(8,128)(2,1)S(1)} %bitcast.11), channel_id=1, source_target_pairs={{0,8},{8,16},{16,24},{24,32},{32,40},{40,48},{48,56},{56,0},{64,72... | collective-permute-start | bytes 786440 | tf_op jit(solution)/shard_map/ppermute | solution.py:26
  94.8 1.9 %collective-permute-start.5 = (bf16[1024,128]{1,0:T(8,128)(2,1)S(1)}, bf16[1024,128]{1,0:T(8,128)(2,1)S(1)}, u32[]{:S(2)}, u32[]{:S(2)}) collective-permute-start(bf16[1024,128]{1,0:T(8,128)(2,1)S(1)} %bitcast.12), channel_id=1, source_target_pairs={{0,448},{8,456},{16,464},{24,472},{32,480},{40,488},{48,496},{56,5... | collective-permute-start | bytes 786440 | tf_op jit(solution)/shard_map/ppermute | solution.py:26
  96.8 3.4 %collective-permute-start.4 = (bf16[1024,128]{1,0:T(8,128)(2,1)S(1)}, bf16[1024,128]{1,0:T(8,128)(2,1)S(1)}, u32[]{:S(2)}, u32[]{:S(2)}) collective-permute-start(bf16[1024,128]{1,0:T(8,128)(2,1)S(1)} %bitcast.13), channel_id=1, source_target_pairs={{0,64},{8,72},{16,80},{24,88},{32,96},{40,104},{48,112},{56,120},{... | collective-permute-start | bytes 786440 | tf_op jit(solution)/shard_map/ppermute | solution.py:26
  100.1 1.1 collective-permute-done.6.refs_3_
  101.9 3.1 %collective-permute-done.4.refs_1_ = bf16[1024,128]{1,0:T(8,128)(2,1)S(1)} collective-permute-done((bf16[1024,128]{1,0:T(8,128)(2,1)S(1)}, bf16[1024,128]{1,0:T(8,128)(2,1)S(1)}, u32[]{:S(2)}, u32[]{:S(2)}) %collective-permute-start.4) | collective-permute-done | bytes 262176 | tf_op jit(solution)/shard_map/ppermute | solution.py:26
  105.1 1.4 %shard_map.91 = bf16[256,256]{1,0:T(8,128)(2,1)S(1)} custom-call(s32[2]{0:T(128)S(1)} %pad_add_fusion.place_ref, bf16[2048,256]{1,0:T(8,128)(2,1)S(1)} %copy-done, bf16[1024,128]{1,0:T(8,128)(2,1)S(1)} %bitcast.14, bf16[1024,128]{1,0:T(8,128)(2,1)S(1)} %collective-permute-done.4.refs_1_, bf16[1024,128]{1,0:T(8,128)(2,1)S(1)} %collective-permute-done.5.refs_2_, ...), custom_call_target="tpu_custom_call" | custom-call | flops 268435456 | tf_op jit(solution)/shard_map/pallas_call | solution.py:57
  106.5 16.8 %all_to_all.22.got_ref = bf16[8,32,256]{2,1,0:T(8,128)(2,1)S(1)} all-to-all(bf16[8,32,256]{2,1,0:T(8,128)(2,1)S(1)} %bitcast.16), channel_id=1, replica_groups=mesh['ctx'=64,'kvh'=8] {'kvh'}, dimensions={0} | all-to-all | bytes 262144 | tf_op jit(solution)/shard_map/all_to_all | solution.py:475
  (21 shorter events, 4.4 us)
Async XLA Ops:
  0.0 18.5 %copy-start.1 = (bf16[2048,1,128]{2,0,1:T(8,128)(2,1)S(1)}, bf16[2048,1,128]{2,0,1:T(8,128)(2,1)}, u32[]{:S(2)}) copy-start(bf16[2048,1,128]{2,0,1:T(8,128)(2,1)} %param.9) | copy-start | bytes 1572868
  1.5 29.1 %all-to-all-start = ((bf16[16,64,128]{2,1,0:T(8,128)(2,1)}), bf16[16,64,128]{2,1,0:T(8,128)(2,1)S(1)}, u32[]{:S(2)}, u32[]{:S(2)}) async-start(bf16[16,64,128]{2,1,0:T(8,128)(2,1)} %broadcast_in_dim.14), calls=%async_computation | async-start | bytes 524288 | tf_op jit(solution)/shard_map/all_to_all | solution.py:45
  18.4 0.7 copy-start.4
  18.4 0.7 copy-start.5
  18.5 0.7 copy-start.3
  19.2 1.0 copy-start.2
  21.2 21.9 %collective-permute-start.1 = (bf16[2096,128]{1,0:T(8,128)(2,1)S(1)}, bf16[2096,128]{1,0:T(8,128)(2,1)S(1)}, u32[]{:S(2)}, u32[]{:S(2)}) collective-permute-start(bf16[2096,128]{1,0:T(8,128)(2,1)S(1)} %get-tuple-element.22.refs_3_), channel_id=1, source_target_pairs={{0,56},{8,0},{16,8},{24,16},{32,24},{40,32},{48,40},{56,48},{64,12... | collective-permute-start | bytes 1609736 | tf_op jit(solution)/shard_map/ppermute | solution.py:26
  25.9 17.2 %collective-permute-start = (bf16[2064,128]{1,0:T(8,128)(2,1)S(1)}, bf16[2064,128]{1,0:T(8,128)(2,1)S(1)}, u32[]{:S(2)}, u32[]{:S(2)}) collective-permute-start(bf16[2064,128]{1,0:T(8,128)(2,1)S(1)} %get-tuple-element.20.refs_0_), channel_id=1, source_target_pairs={{0,8},{8,16},{16,24},{24,32},{32,40},{40,48},{48,56},{56,0},{64,72... | collective-permute-start | bytes 1585160 | tf_op jit(solution)/shard_map/ppermute | solution.py:26
  30.8 8.7 %collective-permute-start.2 = (bf16[128,1024]{1,0:T(8,128)(2,1)S(1)}, bf16[128,1024]{1,0:T(8,128)(2,1)S(1)}, u32[]{:S(2)}, u32[]{:S(2)}) collective-permute-start(bf16[128,1024]{1,0:T(8,128)(2,1)S(1)} %shard_map.83.qt_ref), channel_id=1, source_target_pairs={{0,64},{8,72},{16,80},{24,88},{32,96},{40,104},{48,112},{56,120},{... | collective-permute-start | bytes 786440 | tf_op jit(solution)/shard_map/ppermute | solution.py:26
  47.8 7.2 %collective-permute-start.3 = (bf16[1056,128]{1,0:T(8,128)(2,1)S(1)}, bf16[1056,128]{1,0:T(8,128)(2,1)S(1)}, u32[]{:S(2)}, u32[]{:S(2)}) collective-permute-start(bf16[1056,128]{1,0:T(8,128)(2,1)S(1)} %shard_map.88), channel_id=1, source_target_pairs={{0,448},{8,456},{16,464},{24,472},{32,480},{40,488},{48,496},{56,5... | collective-permute-start | bytes 811016 | tf_op jit(solution)/shard_map/ppermute | solution.py:26
  55.4 49.7 %copy-start = (bf16[2048,256]{1,0:T(8,128)(2,1)S(1)}, bf16[2048,256]{1,0:T(8,128)(2,1)}, u32[]{:S(2)}) copy-start(bf16[2048,256]{1,0:T(8,128)(2,1)} %w_ref.1) | copy-start | bytes 3145732
  92.9 8.3 %collective-permute-start.6 = (bf16[1024,128]{1,0:T(8,128)(2,1)S(1)}, bf16[1024,128]{1,0:T(8,128)(2,1)S(1)}, u32[]{:S(2)}, u32[]{:S(2)}) collective-permute-start(bf16[1024,128]{1,0:T(8,128)(2,1)S(1)} %bitcast.11), channel_id=1, source_target_pairs={{0,8},{8,16},{16,24},{24,32},{32,40},{40,48},{48,56},{56,0},{64,72... | collective-permute-start | bytes 786440 | tf_op jit(solution)/shard_map/ppermute | solution.py:26
  94.8 7.1 %collective-permute-start.5 = (bf16[1024,128]{1,0:T(8,128)(2,1)S(1)}, bf16[1024,128]{1,0:T(8,128)(2,1)S(1)}, u32[]{:S(2)}, u32[]{:S(2)}) collective-permute-start(bf16[1024,128]{1,0:T(8,128)(2,1)S(1)} %bitcast.12), channel_id=1, source_target_pairs={{0,448},{8,456},{16,464},{24,472},{32,480},{40,488},{48,496},{56,5... | collective-permute-start | bytes 786440 | tf_op jit(solution)/shard_map/ppermute | solution.py:26
  96.8 8.3 %collective-permute-start.4 = (bf16[1024,128]{1,0:T(8,128)(2,1)S(1)}, bf16[1024,128]{1,0:T(8,128)(2,1)S(1)}, u32[]{:S(2)}, u32[]{:S(2)}) collective-permute-start(bf16[1024,128]{1,0:T(8,128)(2,1)S(1)} %bitcast.13), channel_id=1, source_target_pairs={{0,64},{8,72},{16,80},{24,88},{32,96},{40,104},{48,112},{56,120},{... | collective-permute-start | bytes 786440 | tf_op jit(solution)/shard_map/ppermute | solution.py:26

commit v8 on v7

--- a/solution.py
+++ b/solution.py
@@ -24,6 +24,14 @@
             to = ((y + step[0]) % SIDE) * SIDE + (z + step[1]) % SIDE
             pairs.append((y * SIDE + z, to))
     return lax.ppermute(value, "ctx", pairs)
+
+
+def row_of(place_ref):
+    return lax.shift_right_logical(place_ref[0], 3)
+
+
+def column_of(place_ref):
+    return lax.bitwise_and(place_ref[0], SIDE - 1)
 
 
 def coset(y, z):
@@ -129,7 +137,7 @@
                 kv_ref[at : at + 16, :] = new.astype(BF)
         kv_ref[2 * span :, :] = size.astype(F32).astype(BF)
         turned(kv_ref, span, fresh, live - n * half, vt_ref)
-        first_token = 4 * (SIDE * place_ref[0] + place_ref[1])
+        first_token = 4 * (SIDE * row_of(place_ref) + column_of(place_ref))
         if fresh:
             bounds_of(first_token, seg_ref[...], live - n * half, b_ref)
         else:
@@ -164,9 +172,9 @@
         live = jnp.max(64.0 * size[0:1] + size[1:2]).astype(jnp.int32)
         live = live - n * (span - fresh)
         turned(kv_ref, span, fresh, live, vt_ref)
-        from_z = lax.rem(place_ref[1] + 1, SIDE)
+        from_z = lax.rem(column_of(place_ref) + 1, SIDE)
         if fresh:
-            bounds_of(4 * (SIDE * place_ref[0] + from_z), seg_ref[...], live, b_ref)
+            bounds_of(4 * (SIDE * row_of(place_ref) + from_z), seg_ref[...], live, b_ref)
         else:
             b_ref[...] = jnp.zeros(b_ref.shape, jnp.int32) + live
 
@@ -211,7 +219,7 @@
     pieces = qt_ref.shape[1] // rows
     factor = LOG2E / width**0.5
     lane = lax.broadcasted_iota(jnp.int32, (16, rows), 1)
-    which = coset(place_ref[0] - step[0], place_ref[1] - step[1])
+    which = coset(row_of(place_ref) - step[0], column_of(place_ref) - step[1])
 
     def cuts_of(n):
         return [(n, at, 256) for at in range(0, slots, 256)] + [(n, slots, 16)] * (n % 2)
@@ -388,14 +396,21 @@
         tail = got_ref[c, 64:72, :].astype(F32)
         logs[c : c + 1, :] = tail[0:1] + tail[1:2] + tail[2:3]
     lse = logs[...]
-    lse = jnp.where(place_ref[0] // 4 == 1, pltpu.roll(lse, 64, 1), lse)
+    lse = jnp.where(row_of(place_ref) // 4 == 1, pltpu.roll(lse, 64, 1), lse)
     weight = jnp.exp2(lse - jnp.max(lse, axis=0, keepdims=True))
     weight = weight / jnp.sum(weight, axis=0, keepdims=True)
-    eye = diagonal(64)
-    total = None
-    for c in range(parts):
-        term = got_ref[c, 0:64, :].astype(F32) * spread(weight[c : c + 1, :], eye)
-        total = term if total is None else total + term
+    lane = lax.broadcasted_iota(jnp.int32, (64, 128), 1)
+    eye = lax.bitwise_and(lane, 63) == lax.broadcasted_iota(jnp.int32, (64, 128), 0)
+    moved = pltpu.roll(weight, 64, 1)
+    high, low = [], []
+    for c in range(0, parts, 2):
+        pair = jnp.where(lane[0:1] < 64, weight[c : c + 1], moved[c + 1 : c + 2])
+        pair = jnp.where(eye, pair, 0.0)
+        high.append(pair.astype(BF))
+        low.append((pair - high[-1].astype(F32)).astype(BF))
+    rows = jnp.concatenate([got_ref[c, 0:64, :] for c in range(parts)], 0)
+    total = jnp.dot(jnp.concatenate(high, 1), rows, preferred_element_type=F32)
+    total = total + jnp.dot(jnp.concatenate(low, 1), rows, preferred_element_type=F32)
     out_ref[...] = total.astype(BF)
 
 
@@ -414,7 +429,7 @@
     heads = w_ref.shape[0] // ins[0].shape[1]
     tokens = rows.shape[0] // heads
     for ref, step in zip(ins, STEPS):
-        which = coset(place_ref[0] - step[0], place_ref[1] - step[1])
+        which = coset(row_of(place_ref) - step[0], column_of(place_ref) - step[1])
         for n in range(ref.shape[0] // 64):
             to = pl.multiple_of(64 * (SIDE * member_y(which, n) + n // 2), 64)
             rows[pl.ds(to, 64), :] = ref[64 * n : 64 * n + 64, :].astype(F32)
@@ -445,8 +460,7 @@
 
 
 def local(queries, cache_keys, cache_values, new_keys, new_values, cache_len, segment, out_weight):
-    me = lax.axis_index("ctx").astype(jnp.int32)
-    place = jnp.stack([me // SIDE, me % SIDE])
+    place = lax.axis_index("ctx").astype(jnp.int32).reshape(1)
     block, heads, width = queries.shape
     seg = segment.reshape(-1, 128)
     near = prepare(

time: 124 us -> 122 us (0.984)
  Pallas kernels: 20 us -> 15.8 us
  waiting for transfers between devices: 12 us -> 13.9 us
    pallas_call x11, Pallas kernels: 20 us -> 15.8 us  [call(): pl.pallas_call(body, out_shape=out_shape, in_specs=specs, out_specs=jax.t...]
    ppermute x7, waiting for transfers between devices: 9.19 us -> 10.5 us  [shift(): return lax.ppermute(value, 'ctx', pairs)]
  transfers between devices with their start and end apart: 8 -> 8, of which waited for: 6 -> 6; matrix products, arithmetic and copies ran while one was open for 0% -> 0% of each run, Pallas kernels for 10% -> 8%
where the time goes in v8:
time: 122 us; the launch traced here: 121 us
  blocking collectives  52.8 us (43%)
  starting transfers between devices  34.3 us (28%)
  Pallas kernels  15.8 us (13%)
  waiting for transfers between devices  13.9 us (11%)
  local copies, waits for them, and re-layouts  3.31 us (3%)
    all_to_all x2, blocking collectives, exchange(): lax.all_to_all(value, 'ctx', 0, 0, axis_index_groups=cosets(), tiled=True)  36.2 us
    ppermute x7, starting transfers between devices, shift(): return lax.ppermute(value, 'ctx', pairs)  18.1 us
    all_to_all x1, blocking collectives, local(): got = lax.all_to_all(mixed, 'kvh', 0, 0, tiled=True)  16.6 us
    all_to_all x1, starting transfers between devices, exchange(): lax.all_to_all(value, 'ctx', 0, 0, axis_index_groups=cosets(), tiled=True)  16.2 us
    pallas_call x11, Pallas kernels, call(): pl.pallas_call(body, out_shape=out_shape, in_specs=specs, out_specs=jax.t...  15.8 us
    ppermute x7, waiting for transfers between devices, shift(): return lax.ppermute(value, 'ctx', pairs)  10.5 us
    all_to_all x1, waiting for transfers between devices, exchange(): lax.all_to_all(value, 'ctx', 0, 0, axis_index_groups=cosets(), tiled=True)  3.44 us
  transfers between devices with their start and end apart: 8, of which 6 were waited for; matrix products, arithmetic and copies ran while one was open for 0% of the time, Pallas kernels for 8%

profile of v8, /device:TPU:1, one launch (start us, length us, event | category | flops | bytes accessed | tf_op | source)
XLA Modules:
  0.0 121.0 jit_solution(2723685447556272937)
XLA Ops:
  0.0 1.5 %broadcast_in_dim.14 = bf16[16,64,128]{2,1,0:T(8,128)(2,1)} broadcast(bf16[64,128]{1,0:T(8,128)(2,1)} %bitcast.22), dimensions={1,2} | broadcast | bytes 278528 | tf_op jit(solution)/shard_map/broadcast_in_dim | solution.py:57
  1.5 16.2 %all-to-all-start = ((bf16[16,64,128]{2,1,0:T(8,128)(2,1)}), bf16[16,64,128]{2,1,0:T(8,128)(2,1)S(1)}, u32[]{:S(2)}, u32[]{:S(2)}) async-start(bf16[16,64,128]{2,1,0:T(8,128)(2,1)} %broadcast_in_dim.14), calls=%async_computation | async-start | bytes 524288 | tf_op jit(solution)/shard_map/all_to_all | solution.py:53
  19.1 1.0 copy-done.2
  20.6 4.7 %collective-permute-start.1 = (bf16[2096,128]{1,0:T(8,128)(2,1)S(1)}, bf16[2096,128]{1,0:T(8,128)(2,1)S(1)}, u32[]{:S(2)}, u32[]{:S(2)}) collective-permute-start(bf16[2096,128]{1,0:T(8,128)(2,1)S(1)} %get-tuple-element.22.refs_3_), channel_id=1, source_target_pairs={{0,56},{8,0},{16,8},{24,16},{32,24},{40,32},{48,40},{56,48},{64,12... | collective-permute-start | bytes 1609736 | tf_op jit(solution)/shard_map/ppermute | solution.py:26
  25.3 1.9 %collective-permute-start = (bf16[2064,128]{1,0:T(8,128)(2,1)S(1)}, bf16[2064,128]{1,0:T(8,128)(2,1)S(1)}, u32[]{:S(2)}, u32[]{:S(2)}) collective-permute-start(bf16[2064,128]{1,0:T(8,128)(2,1)S(1)} %get-tuple-element.20.refs_0_), channel_id=1, source_target_pairs={{0,8},{8,16},{16,24},{24,32},{32,40},{40,48},{48,56},{56,0},{64,72... | collective-permute-start | bytes 1585160 | tf_op jit(solution)/shard_map/ppermute | solution.py:26
  27.2 3.4 %all-to-all-done = bf16[16,64,128]{2,1,0:T(8,128)(2,1)S(1)} async-done(((bf16[16,64,128]{2,1,0:T(8,128)(2,1)}), bf16[16,64,128]{2,1,0:T(8,128)(2,1)S(1)}, u32[]{:S(2)}, u32[]{:S(2)}) %all-to-all-start) | async-done | bytes 262176 | tf_op jit(solution)/shard_map/all_to_all | solution.py:53
  30.8 2.1 %collective-permute-start.2 = (bf16[128,1024]{1,0:T(8,128)(2,1)S(1)}, bf16[128,1024]{1,0:T(8,128)(2,1)S(1)}, u32[]{:S(2)}, u32[]{:S(2)}) collective-permute-start(bf16[128,1024]{1,0:T(8,128)(2,1)S(1)} %shard_map.83.qt_ref), channel_id=1, source_target_pairs={{0,64},{8,72},{16,80},{24,88},{32,96},{40,104},{48,112},{56,120},{... | collective-permute-start | bytes 786440 | tf_op jit(solution)/shard_map/ppermute | solution.py:26
  32.9 3.1 %shard_map.84 = (f32[144,1024]{1,0:T(8,128)S(1)}, f32[8,1024]{1,0:T(8,128)S(1)}) custom-call(s32[1]{0:T(128)} %bitcast.place_ref, bf16[128,1024]{1,0:T(8,128)(2,1)S(1)} %shard_map.83.qt_ref, bf16[2064,128]{1,0:T(8,128)(2,1)S(1)} %get-tuple-element.20.refs_0_, bf16[144,1024]{1,0:T(8,128)(2,1)S(1)} %get-tuple-element.21.refs_1_, ...), custom_call_target="tpu_custom_call" | custom-call | flops 2147483648 | bytes 2113536 | tf_op jit(solution)/shard_map/pallas_call | solution.py:65
  36.0 3.5 %collective-permute-done.2.qt_ref = bf16[128,1024]{1,0:T(8,128)(2,1)S(1)} collective-permute-done((bf16[128,1024]{1,0:T(8,128)(2,1)S(1)}, bf16[128,1024]{1,0:T(8,128)(2,1)S(1)}, u32[]{:S(2)}, u32[]{:S(2)}) %collective-permute-start.2) | collective-permute-done | bytes 262176 | tf_op jit(solution)/shard_map/ppermute | solution.py:26
  39.5 3.1 %shard_map.85 = (f32[144,1024]{1,0:T(8,128)S(1)}, f32[8,1024]{1,0:T(8,128)S(1)}) custom-call(s32[1]{0:T(128)} %bitcast.place_ref, bf16[128,1024]{1,0:T(8,128)(2,1)S(1)} %collective-permute-done.2.qt_ref, bf16[2064,128]{1,0:T(8,128)(2,1)S(1)} %get-tuple-element.20.refs_0_, bf16[144,1024]{1,0:T(8,128)(2,1)S(1)} %get-tuple-element.21.refs_1_, ...), custom_call_target="tpu_custom_call" | custom-call | flops 2147483648 | bytes 2113536 | tf_op jit(solution)/shard_map/pallas_call | solution.py:65
  43.0 3.2 %shard_map.88 = bf16[1056,128]{1,0:T(8,128)(2,1)S(1)} custom-call(s32[1]{0:T(128)} %bitcast.place_ref, bf16[128,1024]{1,0:T(8,128)(2,1)S(1)} %collective-permute-done.2.qt_ref, bf16[2064,128]{1,0:T(8,128)(2,1)S(1)} %get-tuple-element.20.refs_0_, bf16[144,1024]{1,0:T(8,128)(2,1)S(1)} %get-tuple-element.21.refs_1_, ...), custom_call_target="tpu_custom_call" | custom-call | flops 2147483648 | bytes 2113536 | tf_op jit(solution)/shard_map/pallas_call | solution.py:65
  46.2 2.2 %collective-permute-start.3 = (bf16[1056,128]{1,0:T(8,128)(2,1)S(1)}, bf16[1056,128]{1,0:T(8,128)(2,1)S(1)}, u32[]{:S(2)}, u32[]{:S(2)}) collective-permute-start(bf16[1056,128]{1,0:T(8,128)(2,1)S(1)} %shard_map.88), channel_id=1, source_target_pairs={{0,448},{8,456},{16,464},{24,472},{32,480},{40,488},{48,496},{56,5... | collective-permute-start | bytes 811016 | tf_op jit(solution)/shard_map/ppermute | solution.py:26
  48.4 3.2 %shard_map.87.refs_0_ = bf16[1056,128]{1,0:T(8,128)(2,1)S(1)} custom-call(s32[1]{0:T(128)} %bitcast.place_ref, bf16[128,1024]{1,0:T(8,128)(2,1)S(1)} %shard_map.83.qt_ref, bf16[2064,128]{1,0:T(8,128)(2,1)S(1)} %get-tuple-element.20.refs_0_, bf16[144,1024]{1,0:T(8,128)(2,1)S(1)} %get-tuple-element.21.refs_1_, ...), custom_call_target="tpu_custom_call" | custom-call | flops 2147483648 | bytes 2113536 | tf_op jit(solution)/shard_map/pallas_call | solution.py:65
  51.6 1.8 %collective-permute-done.3.refs_1_ = bf16[1056,128]{1,0:T(8,128)(2,1)S(1)} collective-permute-done((bf16[1056,128]{1,0:T(8,128)(2,1)S(1)}, bf16[1056,128]{1,0:T(8,128)(2,1)S(1)}, u32[]{:S(2)}, u32[]{:S(2)}) %collective-permute-start.3) | collective-permute-done | bytes 270368 | tf_op jit(solution)/shard_map/ppermute | solution.py:26
  53.8 19.7 %all_to_all.20.got_ref = bf16[16,72,128]{2,1,0:T(8,128)(2,1)S(1)} all-to-all(bf16[16,72,128]{2,1,0:T(8,128)(2,1)S(1)} %shard_map.89), channel_id=1, replica_groups={{0,256,136,392,16,272,152,408,32,288,168,424,48,304,184,440},{64,320,20..., dimensions={0} | all-to-all | bytes 589824 | tf_op jit(solution)/shard_map/all_to_all | solution.py:53
  74.0 16.4 %all_to_all.21 = bf16[16,64,128]{2,1,0:T(8,128)(2,1)S(1)} all-to-all(bf16[16,64,128]{2,1,0:T(8,128)(2,1)S(1)} %broadcast_in_dim.15), channel_id=1, replica_groups={{0,256,136,392,16,272,152,408,32,288,168,424,48,304,184,440},{64,320,20..., dimensions={0} | all-to-all | bytes 524288 | tf_op jit(solution)/shard_map/all_to_all | solution.py:53
  90.4 1.9 %collective-permute-start.6 = (bf16[1024,128]{1,0:T(8,128)(2,1)S(1)}, bf16[1024,128]{1,0:T(8,128)(2,1)S(1)}, u32[]{:S(2)}, u32[]{:S(2)}) collective-permute-start(bf16[1024,128]{1,0:T(8,128)(2,1)S(1)} %bitcast.10), channel_id=1, source_target_pairs={{0,8},{8,16},{16,24},{24,32},{32,40},{40,48},{48,56},{56,0},{64,72... | collective-permute-start | bytes 786440 | tf_op jit(solution)/shard_map/ppermute | solution.py:26
  92.4 1.9 %collective-permute-start.5 = (bf16[1024,128]{1,0:T(8,128)(2,1)S(1)}, bf16[1024,128]{1,0:T(8,128)(2,1)S(1)}, u32[]{:S(2)}, u32[]{:S(2)}) collective-permute-start(bf16[1024,128]{1,0:T(8,128)(2,1)S(1)} %bitcast.11), channel_id=1, source_target_pairs={{0,448},{8,456},{16,464},{24,472},{32,480},{40,488},{48,496},{56,5... | collective-permute-start | bytes 786440 | tf_op jit(solution)/shard_map/ppermute | solution.py:26
  94.3 3.4 %collective-permute-start.4 = (bf16[1024,128]{1,0:T(8,128)(2,1)S(1)}, bf16[1024,128]{1,0:T(8,128)(2,1)S(1)}, u32[]{:S(2)}, u32[]{:S(2)}) collective-permute-start(bf16[1024,128]{1,0:T(8,128)(2,1)S(1)} %bitcast.12), channel_id=1, source_target_pairs={{0,64},{8,72},{16,80},{24,88},{32,96},{40,104},{48,112},{56,120},{... | collective-permute-start | bytes 786440 | tf_op jit(solution)/shard_map/ppermute | solution.py:26
  97.7 1.1 collective-permute-done.6.refs_3_
  98.8 0.7 collective-permute-done.5.refs_2_
  99.5 3.4 %collective-permute-done.4.refs_1_ = bf16[1024,128]{1,0:T(8,128)(2,1)S(1)} collective-permute-done((bf16[1024,128]{1,0:T(8,128)(2,1)S(1)}, bf16[1024,128]{1,0:T(8,128)(2,1)S(1)}, u32[]{:S(2)}, u32[]{:S(2)}) %collective-permute-start.4) | collective-permute-done | bytes 262176 | tf_op jit(solution)/shard_map/ppermute | solution.py:26
  102.9 0.9 shard_map.91
  103.8 16.6 %all_to_all.22.got_ref = bf16[8,32,256]{2,1,0:T(8,128)(2,1)S(1)} all-to-all(bf16[8,32,256]{2,1,0:T(8,128)(2,1)S(1)} %bitcast.15), channel_id=1, replica_groups=mesh['ctx'=64,'kvh'=8] {'kvh'}, dimensions={0} | all-to-all | bytes 262144 | tf_op jit(solution)/shard_map/all_to_all | solution.py:489
  (20 shorter events, 3.1 us)
Async XLA Ops:
  0.0 18.5 %copy-start.1 = (bf16[2048,1,128]{2,0,1:T(8,128)(2,1)S(1)}, bf16[2048,1,128]{2,0,1:T(8,128)(2,1)}, u32[]{:S(2)}) copy-start(bf16[2048,1,128]{2,0,1:T(8,128)(2,1)} %param.9) | copy-start | bytes 1572868
  1.5 29.1 %all-to-all-start = ((bf16[16,64,128]{2,1,0:T(8,128)(2,1)}), bf16[16,64,128]{2,1,0:T(8,128)(2,1)S(1)}, u32[]{:S(2)}, u32[]{:S(2)}) async-start(bf16[16,64,128]{2,1,0:T(8,128)(2,1)} %broadcast_in_dim.14), calls=%async_computation | async-start | bytes 524288 | tf_op jit(solution)/shard_map/all_to_all | solution.py:53
  18.4 0.7 copy-start.4
  18.4 0.7 copy-start.5
  18.4 0.7 copy-start.3
  19.1 1.0 copy-start.2
  20.6 22.0 %collective-permute-start.1 = (bf16[2096,128]{1,0:T(8,128)(2,1)S(1)}, bf16[2096,128]{1,0:T(8,128)(2,1)S(1)}, u32[]{:S(2)}, u32[]{:S(2)}) collective-permute-start(bf16[2096,128]{1,0:T(8,128)(2,1)S(1)} %get-tuple-element.22.refs_3_), channel_id=1, source_target_pairs={{0,56},{8,0},{16,8},{24,16},{32,24},{40,32},{48,40},{56,48},{64,12... | collective-permute-start | bytes 1609736 | tf_op jit(solution)/shard_map/ppermute | solution.py:26
  25.3 17.3 %collective-permute-start = (bf16[2064,128]{1,0:T(8,128)(2,1)S(1)}, bf16[2064,128]{1,0:T(8,128)(2,1)S(1)}, u32[]{:S(2)}, u32[]{:S(2)}) collective-permute-start(bf16[2064,128]{1,0:T(8,128)(2,1)S(1)} %get-tuple-element.20.refs_0_), channel_id=1, source_target_pairs={{0,8},{8,16},{16,24},{24,32},{32,40},{40,48},{48,56},{56,0},{64,72... | collective-permute-start | bytes 1585160 | tf_op jit(solution)/shard_map/ppermute | solution.py:26
  30.8 8.7 %collective-permute-start.2 = (bf16[128,1024]{1,0:T(8,128)(2,1)S(1)}, bf16[128,1024]{1,0:T(8,128)(2,1)S(1)}, u32[]{:S(2)}, u32[]{:S(2)}) collective-permute-start(bf16[128,1024]{1,0:T(8,128)(2,1)S(1)} %shard_map.83.qt_ref), channel_id=1, source_target_pairs={{0,64},{8,72},{16,80},{24,88},{32,96},{40,104},{48,112},{56,120},{... | collective-permute-start | bytes 786440 | tf_op jit(solution)/shard_map/ppermute | solution.py:26
  46.2 7.2 %collective-permute-start.3 = (bf16[1056,128]{1,0:T(8,128)(2,1)S(1)}, bf16[1056,128]{1,0:T(8,128)(2,1)S(1)}, u32[]{:S(2)}, u32[]{:S(2)}) collective-permute-start(bf16[1056,128]{1,0:T(8,128)(2,1)S(1)} %shard_map.88), channel_id=1, source_target_pairs={{0,448},{8,456},{16,464},{24,472},{32,480},{40,488},{48,496},{56,5... | collective-permute-start | bytes 811016 | tf_op jit(solution)/shard_map/ppermute | solution.py:26
  53.8 49.1 %copy-start = (bf16[2048,256]{1,0:T(8,128)(2,1)S(1)}, bf16[2048,256]{1,0:T(8,128)(2,1)}, u32[]{:S(2)}) copy-start(bf16[2048,256]{1,0:T(8,128)(2,1)} %w_ref.1) | copy-start | bytes 3145732
  90.4 8.3 %collective-permute-start.6 = (bf16[1024,128]{1,0:T(8,128)(2,1)S(1)}, bf16[1024,128]{1,0:T(8,128)(2,1)S(1)}, u32[]{:S(2)}, u32[]{:S(2)}) collective-permute-start(bf16[1024,128]{1,0:T(8,128)(2,1)S(1)} %bitcast.10), channel_id=1, source_target_pairs={{0,8},{8,16},{16,24},{24,32},{32,40},{40,48},{48,56},{56,0},{64,72... | collective-permute-start | bytes 786440 | tf_op jit(solution)/shard_map/ppermute | solution.py:26
  92.4 7.1 %collective-permute-start.5 = (bf16[1024,128]{1,0:T(8,128)(2,1)S(1)}, bf16[1024,128]{1,0:T(8,128)(2,1)S(1)}, u32[]{:S(2)}, u32[]{:S(2)}) collective-permute-start(bf16[1024,128]{1,0:T(8,128)(2,1)S(1)} %bitcast.11), channel_id=1, source_target_pairs={{0,448},{8,456},{16,464},{24,472},{32,480},{40,488},{48,496},{56,5... | collective-permute-start | bytes 786440 | tf_op jit(solution)/shard_map/ppermute | solution.py:26
  94.3 8.6 %collective-permute-start.4 = (bf16[1024,128]{1,0:T(8,128)(2,1)S(1)}, bf16[1024,128]{1,0:T(8,128)(2,1)S(1)}, u32[]{:S(2)}, u32[]{:S(2)}) collective-permute-start(bf16[1024,128]{1,0:T(8,128)(2,1)S(1)} %bitcast.12), channel_id=1, source_target_pairs={{0,64},{8,72},{16,80},{24,88},{32,96},{40,104},{48,112},{56,120},{... | collective-permute-start | bytes 786440 | tf_op jit(solution)/shard_map/ppermute | solution.py:26

commit v9 on v8

--- a/solution.py
+++ b/solution.py
@@ -35,11 +35,11 @@
 
 
 def coset(y, z):
-    return lax.rem(y + 2 * z + 4 * SIDE, 4)
+    return (y + 2 * z + 4 * SIDE) & 3
 
 
 def member_y(which, i):
-    return lax.rem(which + 2 * (i // 2), 4) + 4 * (i % 2)
+    return ((which + 2 * (i >> 1)) & 3) + 4 * (i & 1)
 
 
 def cosets():
@@ -118,7 +118,7 @@
     step = 256
     first = k_ref[0:16, :].astype(F32)[0:1, :]
     line = lax.broadcasted_iota(jnp.int32, (16, width), 0)
-    size = jnp.where(line == 0, live // 64, jnp.where(line == 1, lax.rem(live, 64), 0))
+    size = jnp.where(line == 0, live >> 6, jnp.where(line == 1, live & 63, 0))
     pad = jnp.zeros((16 - fk_ref.shape[0], width), F32)
     for n in range(2):
         kv_ref, vt_ref, b_ref = outs[3 * n : 3 * n + 3]
@@ -172,7 +172,7 @@
         live = jnp.max(64.0 * size[0:1] + size[1:2]).astype(jnp.int32)
         live = live - n * (span - fresh)
         turned(kv_ref, span, fresh, live, vt_ref)
-        from_z = lax.rem(column_of(place_ref) + 1, SIDE)
+        from_z = (column_of(place_ref) + 1) & (SIDE - 1)
         if fresh:
             bounds_of(4 * (SIDE * row_of(place_ref) + from_z), seg_ref[...], live, b_ref)
         else:
@@ -215,7 +215,6 @@
     width = qt_ref.shape[0]
     slots = shards[0][1].shape[1]
     rows = 256
-    heads = 16
     pieces = qt_ref.shape[1] // rows
     factor = LOG2E / width**0.5
     lane = lax.broadcasted_iota(jnp.int32, (16, rows), 1)
@@ -231,9 +230,9 @@
         if deep == 16:
             opens = jnp.concatenate([b_ref[0:16, :]] * 2, 1)
             ends = jnp.concatenate([b_ref[16:32, :]] * 2, 1)
-            member = 4 * i + lane // 64
-            token = 32 * member_y(which, member) + 4 * (member // 2)
-            token = token + lax.rem(lane // heads, 4)
+            member = 4 * i + (lane >> 6)
+            token = 32 * member_y(which, member) + 4 * (member >> 1)
+            token = token + ((lane >> 4) & 3)
             part = jnp.where((token >= opens) & (token < ends), part, -jnp.inf)
         elif exact:
             live = jnp.concatenate([b_ref[32:33, :]] * 2, 1)
@@ -396,7 +395,7 @@
         tail = got_ref[c, 64:72, :].astype(F32)
         logs[c : c + 1, :] = tail[0:1] + tail[1:2] + tail[2:3]
     lse = logs[...]
-    lse = jnp.where(row_of(place_ref) // 4 == 1, pltpu.roll(lse, 64, 1), lse)
+    lse = jnp.where(row_of(place_ref) >= 4, pltpu.roll(lse, 64, 1), lse)
     weight = jnp.exp2(lse - jnp.max(lse, axis=0, keepdims=True))
     weight = weight / jnp.sum(weight, axis=0, keepdims=True)
     lane = lax.broadcasted_iota(jnp.int32, (64, 128), 1)

time: 122 us -> 122 us (level)
  no operation moved by 1% of the time
where the time goes in v9:
time: 122 us; the launch traced here: 121 us
  blocking collectives  52.7 us (43%)
  starting transfers between devices  34.3 us (28%)
  Pallas kernels  15.9 us (13%)
  waiting for transfers between devices  13.9 us (11%)
  local copies, waits for them, and re-layouts  3.31 us (3%)
    all_to_all x2, blocking collectives, exchange(): lax.all_to_all(value, 'ctx', 0, 0, axis_index_groups=cosets(), tiled=True)  36.2 us
    ppermute x7, starting transfers between devices, shift(): return lax.ppermute(value, 'ctx', pairs)  18.1 us
    all_to_all x1, blocking collectives, local(): got = lax.all_to_all(mixed, 'kvh', 0, 0, tiled=True)  16.6 us
    all_to_all x1, starting transfers between devices, exchange(): lax.all_to_all(value, 'ctx', 0, 0, axis_index_groups=cosets(), tiled=True)  16.2 us
    pallas_call x11, Pallas kernels, call(): pl.pallas_call(body, out_shape=out_shape, in_specs=specs, out_specs=jax.t...  15.9 us
    ppermute x7, waiting for transfers between devices, shift(): return lax.ppermute(value, 'ctx', pairs)  10.5 us
    all_to_all x1, waiting for transfers between devices, exchange(): lax.all_to_all(value, 'ctx', 0, 0, axis_index_groups=cosets(), tiled=True)  3.44 us
  transfers between devices with their start and end apart: 8, of which 6 were waited for; matrix products, arithmetic and copies ran while one was open for 0% of the time, Pallas kernels for 8%

profile of v9, /device:TPU:1, one launch (start us, length us, event | category | flops | bytes accessed | tf_op | source)
XLA Modules:
  0.0 121.0 jit_solution(14141150529722131752)
XLA Ops:
  0.0 1.5 %broadcast_in_dim.14 = bf16[16,64,128]{2,1,0:T(8,128)(2,1)} broadcast(bf16[64,128]{1,0:T(8,128)(2,1)} %bitcast.22), dimensions={1,2} | broadcast | bytes 278528 | tf_op jit(solution)/shard_map/broadcast_in_dim | solution.py:57
  1.5 16.2 %all-to-all-start = ((bf16[16,64,128]{2,1,0:T(8,128)(2,1)}), bf16[16,64,128]{2,1,0:T(8,128)(2,1)S(1)}, u32[]{:S(2)}, u32[]{:S(2)}) async-start(bf16[16,64,128]{2,1,0:T(8,128)(2,1)} %broadcast_in_dim.14), calls=%async_computation | async-start | bytes 524288 | tf_op jit(solution)/shard_map/all_to_all | solution.py:53
  19.1 1.0 copy-done.2
  20.6 4.7 %collective-permute-start.1 = (bf16[2096,128]{1,0:T(8,128)(2,1)S(1)}, bf16[2096,128]{1,0:T(8,128)(2,1)S(1)}, u32[]{:S(2)}, u32[]{:S(2)}) collective-permute-start(bf16[2096,128]{1,0:T(8,128)(2,1)S(1)} %get-tuple-element.22.refs_3_), channel_id=1, source_target_pairs={{0,56},{8,0},{16,8},{24,16},{32,24},{40,32},{48,40},{56,48},{64,12... | collective-permute-start | bytes 1609736 | tf_op jit(solution)/shard_map/ppermute | solution.py:26
  25.3 1.9 %collective-permute-start = (bf16[2064,128]{1,0:T(8,128)(2,1)S(1)}, bf16[2064,128]{1,0:T(8,128)(2,1)S(1)}, u32[]{:S(2)}, u32[]{:S(2)}) collective-permute-start(bf16[2064,128]{1,0:T(8,128)(2,1)S(1)} %get-tuple-element.20.refs_0_), channel_id=1, source_target_pairs={{0,8},{8,16},{16,24},{24,32},{32,40},{40,48},{48,56},{56,0},{64,72... | collective-permute-start | bytes 1585160 | tf_op jit(solution)/shard_map/ppermute | solution.py:26
  27.2 3.4 %all-to-all-done = bf16[16,64,128]{2,1,0:T(8,128)(2,1)S(1)} async-done(((bf16[16,64,128]{2,1,0:T(8,128)(2,1)}), bf16[16,64,128]{2,1,0:T(8,128)(2,1)S(1)}, u32[]{:S(2)}, u32[]{:S(2)}) %all-to-all-start) | async-done | bytes 262176 | tf_op jit(solution)/shard_map/all_to_all | solution.py:53
  30.8 2.1 %collective-permute-start.2 = (bf16[128,1024]{1,0:T(8,128)(2,1)S(1)}, bf16[128,1024]{1,0:T(8,128)(2,1)S(1)}, u32[]{:S(2)}, u32[]{:S(2)}) collective-permute-start(bf16[128,1024]{1,0:T(8,128)(2,1)S(1)} %shard_map.83.qt_ref), channel_id=1, source_target_pairs={{0,64},{8,72},{16,80},{24,88},{32,96},{40,104},{48,112},{56,120},{... | collective-permute-start | bytes 786440 | tf_op jit(solution)/shard_map/ppermute | solution.py:26
  32.9 3.1 %shard_map.84 = (f32[144,1024]{1,0:T(8,128)S(1)}, f32[8,1024]{1,0:T(8,128)S(1)}) custom-call(s32[1]{0:T(128)} %bitcast.place_ref, bf16[128,1024]{1,0:T(8,128)(2,1)S(1)} %shard_map.83.qt_ref, bf16[2064,128]{1,0:T(8,128)(2,1)S(1)} %get-tuple-element.20.refs_0_, bf16[144,1024]{1,0:T(8,128)(2,1)S(1)} %get-tuple-element.21.refs_1_, ...), custom_call_target="tpu_custom_call" | custom-call | flops 2147483648 | bytes 2113536 | tf_op jit(solution)/shard_map/pallas_call | solution.py:65
  36.0 3.4 %collective-permute-done.2.qt_ref = bf16[128,1024]{1,0:T(8,128)(2,1)S(1)} collective-permute-done((bf16[128,1024]{1,0:T(8,128)(2,1)S(1)}, bf16[128,1024]{1,0:T(8,128)(2,1)S(1)}, u32[]{:S(2)}, u32[]{:S(2)}) %collective-permute-start.2) | collective-permute-done | bytes 262176 | tf_op jit(solution)/shard_map/ppermute | solution.py:26
  39.5 3.1 %shard_map.85 = (f32[144,1024]{1,0:T(8,128)S(1)}, f32[8,1024]{1,0:T(8,128)S(1)}) custom-call(s32[1]{0:T(128)} %bitcast.place_ref, bf16[128,1024]{1,0:T(8,128)(2,1)S(1)} %collective-permute-done.2.qt_ref, bf16[2064,128]{1,0:T(8,128)(2,1)S(1)} %get-tuple-element.20.refs_0_, bf16[144,1024]{1,0:T(8,128)(2,1)S(1)} %get-tuple-element.21.refs_1_, ...), custom_call_target="tpu_custom_call" | custom-call | flops 2147483648 | bytes 2113536 | tf_op jit(solution)/shard_map/pallas_call | solution.py:65
  43.0 3.2 %shard_map.88 = bf16[1056,128]{1,0:T(8,128)(2,1)S(1)} custom-call(s32[1]{0:T(128)} %bitcast.place_ref, bf16[128,1024]{1,0:T(8,128)(2,1)S(1)} %collective-permute-done.2.qt_ref, bf16[2064,128]{1,0:T(8,128)(2,1)S(1)} %get-tuple-element.20.refs_0_, bf16[144,1024]{1,0:T(8,128)(2,1)S(1)} %get-tuple-element.21.refs_1_, ...), custom_call_target="tpu_custom_call" | custom-call | flops 2147483648 | bytes 2113536 | tf_op jit(solution)/shard_map/pallas_call | solution.py:65
  46.2 2.2 %collective-permute-start.3 = (bf16[1056,128]{1,0:T(8,128)(2,1)S(1)}, bf16[1056,128]{1,0:T(8,128)(2,1)S(1)}, u32[]{:S(2)}, u32[]{:S(2)}) collective-permute-start(bf16[1056,128]{1,0:T(8,128)(2,1)S(1)} %shard_map.88), channel_id=1, source_target_pairs={{0,448},{8,456},{16,464},{24,472},{32,480},{40,488},{48,496},{56,5... | collective-permute-start | bytes 811016 | tf_op jit(solution)/shard_map/ppermute | solution.py:26
  48.4 3.2 %shard_map.87.refs_0_ = bf16[1056,128]{1,0:T(8,128)(2,1)S(1)} custom-call(s32[1]{0:T(128)} %bitcast.place_ref, bf16[128,1024]{1,0:T(8,128)(2,1)S(1)} %shard_map.83.qt_ref, bf16[2064,128]{1,0:T(8,128)(2,1)S(1)} %get-tuple-element.20.refs_0_, bf16[144,1024]{1,0:T(8,128)(2,1)S(1)} %get-tuple-element.21.refs_1_, ...), custom_call_target="tpu_custom_call" | custom-call | flops 2147483648 | bytes 2113536 | tf_op jit(solution)/shard_map/pallas_call | solution.py:65
  51.6 1.8 %collective-permute-done.3.refs_1_ = bf16[1056,128]{1,0:T(8,128)(2,1)S(1)} collective-permute-done((bf16[1056,128]{1,0:T(8,128)(2,1)S(1)}, bf16[1056,128]{1,0:T(8,128)(2,1)S(1)}, u32[]{:S(2)}, u32[]{:S(2)}) %collective-permute-start.3) | collective-permute-done | bytes 270368 | tf_op jit(solution)/shard_map/ppermute | solution.py:26
  53.8 19.7 %all_to_all.20.got_ref = bf16[16,72,128]{2,1,0:T(8,128)(2,1)S(1)} all-to-all(bf16[16,72,128]{2,1,0:T(8,128)(2,1)S(1)} %shard_map.89), channel_id=1, replica_groups={{0,256,136,392,16,272,152,408,32,288,168,424,48,304,184,440},{64,320,20..., dimensions={0} | all-to-all | bytes 589824 | tf_op jit(solution)/shard_map/all_to_all | solution.py:53
  74.0 16.4 %all_to_all.21 = bf16[16,64,128]{2,1,0:T(8,128)(2,1)S(1)} all-to-all(bf16[16,64,128]{2,1,0:T(8,128)(2,1)S(1)} %broadcast_in_dim.15), channel_id=1, replica_groups={{0,256,136,392,16,272,152,408,32,288,168,424,48,304,184,440},{64,320,20..., dimensions={0} | all-to-all | bytes 524288 | tf_op jit(solution)/shard_map/all_to_all | solution.py:53
  90.4 1.9 %collective-permute-start.6 = (bf16[1024,128]{1,0:T(8,128)(2,1)S(1)}, bf16[1024,128]{1,0:T(8,128)(2,1)S(1)}, u32[]{:S(2)}, u32[]{:S(2)}) collective-permute-start(bf16[1024,128]{1,0:T(8,128)(2,1)S(1)} %bitcast.10), channel_id=1, source_target_pairs={{0,8},{8,16},{16,24},{24,32},{32,40},{40,48},{48,56},{56,0},{64,72... | collective-permute-start | bytes 786440 | tf_op jit(solution)/shard_map/ppermute | solution.py:26
  92.4 1.9 %collective-permute-start.5 = (bf16[1024,128]{1,0:T(8,128)(2,1)S(1)}, bf16[1024,128]{1,0:T(8,128)(2,1)S(1)}, u32[]{:S(2)}, u32[]{:S(2)}) collective-permute-start(bf16[1024,128]{1,0:T(8,128)(2,1)S(1)} %bitcast.11), channel_id=1, source_target_pairs={{0,448},{8,456},{16,464},{24,472},{32,480},{40,488},{48,496},{56,5... | collective-permute-start | bytes 786440 | tf_op jit(solution)/shard_map/ppermute | solution.py:26
  94.3 3.4 %collective-permute-start.4 = (bf16[1024,128]{1,0:T(8,128)(2,1)S(1)}, bf16[1024,128]{1,0:T(8,128)(2,1)S(1)}, u32[]{:S(2)}, u32[]{:S(2)}) collective-permute-start(bf16[1024,128]{1,0:T(8,128)(2,1)S(1)} %bitcast.12), channel_id=1, source_target_pairs={{0,64},{8,72},{16,80},{24,88},{32,96},{40,104},{48,112},{56,120},{... | collective-permute-start | bytes 786440 | tf_op jit(solution)/shard_map/ppermute | solution.py:26
  97.7 1.1 collective-permute-done.6.refs_3_
  98.8 0.7 collective-permute-done.5.refs_2_
  99.5 3.4 %collective-permute-done.4.refs_1_ = bf16[1024,128]{1,0:T(8,128)(2,1)S(1)} collective-permute-done((bf16[1024,128]{1,0:T(8,128)(2,1)S(1)}, bf16[1024,128]{1,0:T(8,128)(2,1)S(1)}, u32[]{:S(2)}, u32[]{:S(2)}) %collective-permute-start.4) | collective-permute-done | bytes 262176 | tf_op jit(solution)/shard_map/ppermute | solution.py:26
  102.9 0.9 shard_map.91
  103.8 16.6 %all_to_all.22.got_ref = bf16[8,32,256]{2,1,0:T(8,128)(2,1)S(1)} all-to-all(bf16[8,32,256]{2,1,0:T(8,128)(2,1)S(1)} %bitcast.15), channel_id=1, replica_groups=mesh['ctx'=64,'kvh'=8] {'kvh'}, dimensions={0} | all-to-all | bytes 262144 | tf_op jit(solution)/shard_map/all_to_all | solution.py:488
  (20 shorter events, 3.1 us)
Async XLA Ops:
  0.0 18.5 %copy-start.1 = (bf16[2048,1,128]{2,0,1:T(8,128)(2,1)S(1)}, bf16[2048,1,128]{2,0,1:T(8,128)(2,1)}, u32[]{:S(2)}) copy-start(bf16[2048,1,128]{2,0,1:T(8,128)(2,1)} %param.9) | copy-start | bytes 1572868
  1.5 29.1 %all-to-all-start = ((bf16[16,64,128]{2,1,0:T(8,128)(2,1)}), bf16[16,64,128]{2,1,0:T(8,128)(2,1)S(1)}, u32[]{:S(2)}, u32[]{:S(2)}) async-start(bf16[16,64,128]{2,1,0:T(8,128)(2,1)} %broadcast_in_dim.14), calls=%async_computation | async-start | bytes 524288 | tf_op jit(solution)/shard_map/all_to_all | solution.py:53
  18.4 0.7 copy-start.4
  18.4 0.7 copy-start.5
  18.4 0.7 copy-start.3
  19.1 1.0 copy-start.2
  20.6 22.0 %collective-permute-start.1 = (bf16[2096,128]{1,0:T(8,128)(2,1)S(1)}, bf16[2096,128]{1,0:T(8,128)(2,1)S(1)}, u32[]{:S(2)}, u32[]{:S(2)}) collective-permute-start(bf16[2096,128]{1,0:T(8,128)(2,1)S(1)} %get-tuple-element.22.refs_3_), channel_id=1, source_target_pairs={{0,56},{8,0},{16,8},{24,16},{32,24},{40,32},{48,40},{56,48},{64,12... | collective-permute-start | bytes 1609736 | tf_op jit(solution)/shard_map/ppermute | solution.py:26
  25.3 17.3 %collective-permute-start = (bf16[2064,128]{1,0:T(8,128)(2,1)S(1)}, bf16[2064,128]{1,0:T(8,128)(2,1)S(1)}, u32[]{:S(2)}, u32[]{:S(2)}) collective-permute-start(bf16[2064,128]{1,0:T(8,128)(2,1)S(1)} %get-tuple-element.20.refs_0_), channel_id=1, source_target_pairs={{0,8},{8,16},{16,24},{24,32},{32,40},{40,48},{48,56},{56,0},{64,72... | collective-permute-start | bytes 1585160 | tf_op jit(solution)/shard_map/ppermute | solution.py:26
  30.8 8.7 %collective-permute-start.2 = (bf16[128,1024]{1,0:T(8,128)(2,1)S(1)}, bf16[128,1024]{1,0:T(8,128)(2,1)S(1)}, u32[]{:S(2)}, u32[]{:S(2)}) collective-permute-start(bf16[128,1024]{1,0:T(8,128)(2,1)S(1)} %shard_map.83.qt_ref), channel_id=1, source_target_pairs={{0,64},{8,72},{16,80},{24,88},{32,96},{40,104},{48,112},{56,120},{... | collective-permute-start | bytes 786440 | tf_op jit(solution)/shard_map/ppermute | solution.py:26
  46.2 7.2 %collective-permute-start.3 = (bf16[1056,128]{1,0:T(8,128)(2,1)S(1)}, bf16[1056,128]{1,0:T(8,128)(2,1)S(1)}, u32[]{:S(2)}, u32[]{:S(2)}) collective-permute-start(bf16[1056,128]{1,0:T(8,128)(2,1)S(1)} %shard_map.88), channel_id=1, source_target_pairs={{0,448},{8,456},{16,464},{24,472},{32,480},{40,488},{48,496},{56,5... | collective-permute-start | bytes 811016 | tf_op jit(solution)/shard_map/ppermute | solution.py:26
  53.8 49.1 %copy-start = (bf16[2048,256]{1,0:T(8,128)(2,1)S(1)}, bf16[2048,256]{1,0:T(8,128)(2,1)}, u32[]{:S(2)}) copy-start(bf16[2048,256]{1,0:T(8,128)(2,1)} %w_ref.1) | copy-start | bytes 3145732
  90.4 8.3 %collective-permute-start.6 = (bf16[1024,128]{1,0:T(8,128)(2,1)S(1)}, bf16[1024,128]{1,0:T(8,128)(2,1)S(1)}, u32[]{:S(2)}, u32[]{:S(2)}) collective-permute-start(bf16[1024,128]{1,0:T(8,128)(2,1)S(1)} %bitcast.10), channel_id=1, source_target_pairs={{0,8},{8,16},{16,24},{24,32},{32,40},{40,48},{48,56},{56,0},{64,72... | collective-permute-start | bytes 786440 | tf_op jit(solution)/shard_map/ppermute | solution.py:26
  92.4 7.1 %collective-permute-start.5 = (bf16[1024,128]{1,0:T(8,128)(2,1)S(1)}, bf16[1024,128]{1,0:T(8,128)(2,1)S(1)}, u32[]{:S(2)}, u32[]{:S(2)}) collective-permute-start(bf16[1024,128]{1,0:T(8,128)(2,1)S(1)} %bitcast.11), channel_id=1, source_target_pairs={{0,448},{8,456},{16,464},{24,472},{32,480},{40,488},{48,496},{56,5... | collective-permute-start | bytes 786440 | tf_op jit(solution)/shard_map/ppermute | solution.py:26
  94.3 8.6 %collective-permute-start.4 = (bf16[1024,128]{1,0:T(8,128)(2,1)S(1)}, bf16[1024,128]{1,0:T(8,128)(2,1)S(1)}, u32[]{:S(2)}, u32[]{:S(2)}) collective-permute-start(bf16[1024,128]{1,0:T(8,128)(2,1)S(1)} %bitcast.12), channel_id=1, source_target_pairs={{0,64},{8,72},{16,80},{24,88},{32,96},{40,104},{48,112},{56,120},{... | collective-permute-start | bytes 786440 | tf_op jit(solution)/shard_map/ppermute | solution.py:26

commit v10 on v8

--- a/solution.py
+++ b/solution.py
@@ -53,8 +53,13 @@
     return lax.all_to_all(value, "ctx", 0, 0, axis_index_groups=cosets(), tiled=True)
 
 
+def copy_body(in_ref, out_ref):
+    for i in range(out_ref.shape[0]):
+        out_ref[i] = in_ref[...]
+
+
 def share(value):
-    copies = jnp.broadcast_to(value[None], (16,) + value.shape)
+    copies = call(copy_body, jax.ShapeDtypeStruct((16,) + value.shape, BF), args=(value,))
     return exchange(copies).reshape(16 * value.shape[0], value.shape[1])
 
 
@@ -111,14 +116,14 @@
     b_ref[32:40, :] = jnp.zeros((8, 128), jnp.int32) + live
 
 
-def prepare_body(live_ref, place_ref, seg_ref, k_ref, v_ref, fk_ref, fv_ref, *outs):
-    live = live_ref[0]
+def prepare_body(place_ref, live_ref, seg_ref, k_ref, v_ref, fk_ref, fv_ref, *outs):
+    live = live_ref[...]
     slots, width = k_ref.shape
     half = slots // 2
     step = 256
     first = k_ref[0:16, :].astype(F32)[0:1, :]
     line = lax.broadcasted_iota(jnp.int32, (16, width), 0)
-    size = jnp.where(line == 0, live // 64, jnp.where(line == 1, lax.rem(live, 64), 0))
+    size = jnp.where(line == 0, live >> 6, jnp.where(line == 1, live & 63, 0))
     pad = jnp.zeros((16 - fk_ref.shape[0], width), F32)
     for n in range(2):
         kv_ref, vt_ref, b_ref = outs[3 * n : 3 * n + 3]
@@ -158,8 +163,8 @@
     for n in range(2):
         out.append(jax.ShapeDtypeStruct((2 * (half + 16 * n) + 16, width), BF))
         out += ready_shapes(half, n, width)
-    args = (live, place, seg, keys, vals, fresh_k, fresh_v)
-    got = call(prepare_body, out, smem=2, args=args)
+    args = (place, live.reshape(1, 1), seg, keys, vals, fresh_k, fresh_v)
+    got = call(prepare_body, out, smem=1, args=args)
     return tuple(got[:3]), tuple(got[3:])
 
 

time: 122 us -> 122 us (level)
    broadcast_in_dim x2 -> x0, local copies, waits for them, and re-layouts: 1.58 us -> none  [share(): copies = jnp.broadcast_to(value[None], (16,) + value.shape)]
    pallas_call x11 -> x13, Pallas kernels: 15.8 us -> 16.7 us  [call(): pl.pallas_call(body, out_shape=out_shape, in_specs=specs, out_specs=jax.t...]
    unnamed x12 -> x14, local copies, waits for them, and re-layouts: 1.73 us -> 2.51 us
where the time goes in v10:
time: 122 us; the launch traced here: 121 us
  blocking collectives  52.8 us (43%)
  starting transfers between devices  34.4 us (28%)
  Pallas kernels  16.7 us (14%)
  waiting for transfers between devices  13.8 us (11%)
  local copies, waits for them, and re-layouts  2.51 us (2%)
    all_to_all x2, blocking collectives, exchange(): lax.all_to_all(value, 'ctx', 0, 0, axis_index_groups=cosets(), tiled=True)  36.2 us
    ppermute x7, starting transfers between devices, shift(): return lax.ppermute(value, 'ctx', pairs)  18.2 us
    pallas_call x13, Pallas kernels, call(): pl.pallas_call(body, out_shape=out_shape, in_specs=specs, out_specs=jax.t...  16.7 us
    all_to_all x1, blocking collectives, local(): got = lax.all_to_all(mixed, 'kvh', 0, 0, tiled=True)  16.7 us
    all_to_all x1, starting transfers between devices, exchange(): lax.all_to_all(value, 'ctx', 0, 0, axis_index_groups=cosets(), tiled=True)  16.2 us
    ppermute x7, waiting for transfers between devices, shift(): return lax.ppermute(value, 'ctx', pairs)  10.4 us
    all_to_all x1, waiting for transfers between devices, exchange(): lax.all_to_all(value, 'ctx', 0, 0, axis_index_groups=cosets(), tiled=True)  3.37 us
    unnamed x14, local copies, waits for them, and re-layouts  2.51 us
  transfers between devices with their start and end apart: 8, of which 6 were waited for; matrix products, arithmetic and copies ran while one was open for 0% of the time, Pallas kernels for 8%

profile of v10, /device:TPU:1, one launch (start us, length us, event | category | flops | bytes accessed | tf_op | source)
XLA Modules:
  0.0 121.0 jit_solution(4490550877027161013)
XLA Ops:
  0.0 0.8 copy-done.3
  0.8 0.7 shard_map.83
  1.5 16.2 %all-to-all-start = ((bf16[16,64,128]{2,1,0:T(8,128)(2,1)}), bf16[16,64,128]{2,1,0:T(8,128)(2,1)S(1)}, u32[]{:S(2)}, u32[]{:S(2)}) async-start(bf16[16,64,128]{2,1,0:T(8,128)(2,1)} %shard_map.83), calls=%async_computation | async-start | bytes 524288 | tf_op jit(solution)/shard_map/all_to_all | solution.py:53
  19.1 1.0 copy-done.2
  20.6 4.7 %collective-permute-start.1 = (bf16[2096,128]{1,0:T(8,128)(2,1)S(1)}, bf16[2096,128]{1,0:T(8,128)(2,1)S(1)}, u32[]{:S(2)}, u32[]{:S(2)}) collective-permute-start(bf16[2096,128]{1,0:T(8,128)(2,1)S(1)} %get-tuple-element.22.refs_3_), channel_id=1, source_target_pairs={{0,56},{8,0},{16,8},{24,16},{32,24},{40,32},{48,40},{56,48},{64,12... | collective-permute-start | bytes 1609736 | tf_op jit(solution)/shard_map/ppermute | solution.py:26
  25.3 1.9 %collective-permute-start = (bf16[2064,128]{1,0:T(8,128)(2,1)S(1)}, bf16[2064,128]{1,0:T(8,128)(2,1)S(1)}, u32[]{:S(2)}, u32[]{:S(2)}) collective-permute-start(bf16[2064,128]{1,0:T(8,128)(2,1)S(1)} %get-tuple-element.20.refs_0_), channel_id=1, source_target_pairs={{0,8},{8,16},{16,24},{24,32},{32,40},{40,48},{48,56},{56,0},{64,72... | collective-permute-start | bytes 1585160 | tf_op jit(solution)/shard_map/ppermute | solution.py:26
  27.3 3.4 %all-to-all-done = bf16[16,64,128]{2,1,0:T(8,128)(2,1)S(1)} async-done(((bf16[16,64,128]{2,1,0:T(8,128)(2,1)}), bf16[16,64,128]{2,1,0:T(8,128)(2,1)S(1)}, u32[]{:S(2)}, u32[]{:S(2)}) %all-to-all-start) | async-done | bytes 262176 | tf_op jit(solution)/shard_map/all_to_all | solution.py:53
  30.8 2.1 %collective-permute-start.2 = (bf16[128,1024]{1,0:T(8,128)(2,1)S(1)}, bf16[128,1024]{1,0:T(8,128)(2,1)S(1)}, u32[]{:S(2)}, u32[]{:S(2)}) collective-permute-start(bf16[128,1024]{1,0:T(8,128)(2,1)S(1)} %shard_map.84.qt_ref), channel_id=1, source_target_pairs={{0,64},{8,72},{16,80},{24,88},{32,96},{40,104},{48,112},{56,120},{... | collective-permute-start | bytes 786440 | tf_op jit(solution)/shard_map/ppermute | solution.py:26
  32.9 3.1 %shard_map.85 = (f32[144,1024]{1,0:T(8,128)S(1)}, f32[8,1024]{1,0:T(8,128)S(1)}) custom-call(s32[1]{0:T(128)} %bitcast.place_ref, bf16[128,1024]{1,0:T(8,128)(2,1)S(1)} %shard_map.84.qt_ref, bf16[2064,128]{1,0:T(8,128)(2,1)S(1)} %get-tuple-element.20.refs_0_, bf16[144,1024]{1,0:T(8,128)(2,1)S(1)} %get-tuple-element.21.refs_1_, ...), custom_call_target="tpu_custom_call" | custom-call | flops 2147483648 | bytes 2113536 | tf_op jit(solution)/shard_map/pallas_call | solution.py:70
  36.0 3.4 %collective-permute-done.2.qt_ref = bf16[128,1024]{1,0:T(8,128)(2,1)S(1)} collective-permute-done((bf16[128,1024]{1,0:T(8,128)(2,1)S(1)}, bf16[128,1024]{1,0:T(8,128)(2,1)S(1)}, u32[]{:S(2)}, u32[]{:S(2)}) %collective-permute-start.2) | collective-permute-done | bytes 262176 | tf_op jit(solution)/shard_map/ppermute | solution.py:26
  39.4 3.1 %shard_map.86 = (f32[144,1024]{1,0:T(8,128)S(1)}, f32[8,1024]{1,0:T(8,128)S(1)}) custom-call(s32[1]{0:T(128)} %bitcast.place_ref, bf16[128,1024]{1,0:T(8,128)(2,1)S(1)} %collective-permute-done.2.qt_ref, bf16[2064,128]{1,0:T(8,128)(2,1)S(1)} %get-tuple-element.20.refs_0_, bf16[144,1024]{1,0:T(8,128)(2,1)S(1)} %get-tuple-element.21.refs_1_, ...), custom_call_target="tpu_custom_call" | custom-call | flops 2147483648 | bytes 2113536 | tf_op jit(solution)/shard_map/pallas_call | solution.py:70
  42.9 3.2 %shard_map.89 = bf16[1056,128]{1,0:T(8,128)(2,1)S(1)} custom-call(s32[1]{0:T(128)} %bitcast.place_ref, bf16[128,1024]{1,0:T(8,128)(2,1)S(1)} %collective-permute-done.2.qt_ref, bf16[2064,128]{1,0:T(8,128)(2,1)S(1)} %get-tuple-element.20.refs_0_, bf16[144,1024]{1,0:T(8,128)(2,1)S(1)} %get-tuple-element.21.refs_1_, ...), custom_call_target="tpu_custom_call" | custom-call | flops 2147483648 | bytes 2113536 | tf_op jit(solution)/shard_map/pallas_call | solution.py:70
  46.2 2.2 %collective-permute-start.3 = (bf16[1056,128]{1,0:T(8,128)(2,1)S(1)}, bf16[1056,128]{1,0:T(8,128)(2,1)S(1)}, u32[]{:S(2)}, u32[]{:S(2)}) collective-permute-start(bf16[1056,128]{1,0:T(8,128)(2,1)S(1)} %shard_map.89), channel_id=1, source_target_pairs={{0,448},{8,456},{16,464},{24,472},{32,480},{40,488},{48,496},{56,5... | collective-permute-start | bytes 811016 | tf_op jit(solution)/shard_map/ppermute | solution.py:26
  48.4 3.2 %shard_map.88.refs_0_ = bf16[1056,128]{1,0:T(8,128)(2,1)S(1)} custom-call(s32[1]{0:T(128)} %bitcast.place_ref, bf16[128,1024]{1,0:T(8,128)(2,1)S(1)} %shard_map.84.qt_ref, bf16[2064,128]{1,0:T(8,128)(2,1)S(1)} %get-tuple-element.20.refs_0_, bf16[144,1024]{1,0:T(8,128)(2,1)S(1)} %get-tuple-element.21.refs_1_, ...), custom_call_target="tpu_custom_call" | custom-call | flops 2147483648 | bytes 2113536 | tf_op jit(solution)/shard_map/pallas_call | solution.py:70
  51.7 1.7 %collective-permute-done.3.refs_1_ = bf16[1056,128]{1,0:T(8,128)(2,1)S(1)} collective-permute-done((bf16[1056,128]{1,0:T(8,128)(2,1)S(1)}, bf16[1056,128]{1,0:T(8,128)(2,1)S(1)}, u32[]{:S(2)}, u32[]{:S(2)}) %collective-permute-start.3) | collective-permute-done | bytes 270368 | tf_op jit(solution)/shard_map/ppermute | solution.py:26
  53.8 19.8 %all_to_all.20.got_ref = bf16[16,72,128]{2,1,0:T(8,128)(2,1)S(1)} all-to-all(bf16[16,72,128]{2,1,0:T(8,128)(2,1)S(1)} %shard_map.90), channel_id=1, replica_groups={{0,256,136,392,16,272,152,408,32,288,168,424,48,304,184,440},{64,320,20..., dimensions={0} | all-to-all | bytes 589824 | tf_op jit(solution)/shard_map/all_to_all | solution.py:53
  74.0 16.4 %all_to_all.21 = bf16[16,64,128]{2,1,0:T(8,128)(2,1)S(1)} all-to-all(bf16[16,64,128]{2,1,0:T(8,128)(2,1)S(1)} %shard_map.92), channel_id=1, replica_groups={{0,256,136,392,16,272,152,408,32,288,168,424,48,304,184,440},{64,320,20..., dimensions={0} | all-to-all | bytes 524288 | tf_op jit(solution)/shard_map/all_to_all | solution.py:53
  90.4 1.9 %collective-permute-start.6 = (bf16[1024,128]{1,0:T(8,128)(2,1)S(1)}, bf16[1024,128]{1,0:T(8,128)(2,1)S(1)}, u32[]{:S(2)}, u32[]{:S(2)}) collective-permute-start(bf16[1024,128]{1,0:T(8,128)(2,1)S(1)} %bitcast.12), channel_id=1, source_target_pairs={{0,8},{8,16},{16,24},{24,32},{32,40},{40,48},{48,56},{56,0},{64,72... | collective-permute-start | bytes 786440 | tf_op jit(solution)/shard_map/ppermute | solution.py:26
  92.3 1.9 %collective-permute-start.5 = (bf16[1024,128]{1,0:T(8,128)(2,1)S(1)}, bf16[1024,128]{1,0:T(8,128)(2,1)S(1)}, u32[]{:S(2)}, u32[]{:S(2)}) collective-permute-start(bf16[1024,128]{1,0:T(8,128)(2,1)S(1)} %bitcast.13), channel_id=1, source_target_pairs={{0,448},{8,456},{16,464},{24,472},{32,480},{40,488},{48,496},{56,5... | collective-permute-start | bytes 786440 | tf_op jit(solution)/shard_map/ppermute | solution.py:26
  94.2 3.4 %collective-permute-start.4 = (bf16[1024,128]{1,0:T(8,128)(2,1)S(1)}, bf16[1024,128]{1,0:T(8,128)(2,1)S(1)}, u32[]{:S(2)}, u32[]{:S(2)}) collective-permute-start(bf16[1024,128]{1,0:T(8,128)(2,1)S(1)} %bitcast.14), channel_id=1, source_target_pairs={{0,64},{8,72},{16,80},{24,88},{32,96},{40,104},{48,112},{56,120},{... | collective-permute-start | bytes 786440 | tf_op jit(solution)/shard_map/ppermute | solution.py:26
  97.6 1.1 collective-permute-done.6.refs_3_
  99.4 3.4 %collective-permute-done.4.refs_1_ = bf16[1024,128]{1,0:T(8,128)(2,1)S(1)} collective-permute-done((bf16[1024,128]{1,0:T(8,128)(2,1)S(1)}, bf16[1024,128]{1,0:T(8,128)(2,1)S(1)}, u32[]{:S(2)}, u32[]{:S(2)}) %collective-permute-start.4) | collective-permute-done | bytes 262176 | tf_op jit(solution)/shard_map/ppermute | solution.py:26
  102.9 0.9 shard_map.93
  103.8 16.7 %all_to_all.22.got_ref = bf16[8,32,256]{2,1,0:T(8,128)(2,1)S(1)} all-to-all(bf16[8,32,256]{2,1,0:T(8,128)(2,1)S(1)} %bitcast.17), channel_id=1, replica_groups=mesh['ctx'=64,'kvh'=8] {'kvh'}, dimensions={0} | all-to-all | bytes 262144 | tf_op jit(solution)/shard_map/all_to_all | solution.py:494
  (22 shorter events, 3.8 us)
Async XLA Ops:
  0.0 18.4 %copy-start.1 = (bf16[2048,1,128]{2,0,1:T(8,128)(2,1)S(1)}, bf16[2048,1,128]{2,0,1:T(8,128)(2,1)}, u32[]{:S(2)}) copy-start(bf16[2048,1,128]{2,0,1:T(8,128)(2,1)} %param.9) | copy-start | bytes 1572868
  0.0 0.8 copy-start.3
  1.5 29.1 %all-to-all-start = ((bf16[16,64,128]{2,1,0:T(8,128)(2,1)}), bf16[16,64,128]{2,1,0:T(8,128)(2,1)S(1)}, u32[]{:S(2)}, u32[]{:S(2)}) async-start(bf16[16,64,128]{2,1,0:T(8,128)(2,1)} %shard_map.83), calls=%async_computation | async-start | bytes 524288 | tf_op jit(solution)/shard_map/all_to_all | solution.py:53
  18.4 0.7 copy-start.5
  18.4 0.7 copy-start.6
  18.4 0.7 copy-start.4
  19.1 1.0 copy-start.2
  20.6 21.9 %collective-permute-start.1 = (bf16[2096,128]{1,0:T(8,128)(2,1)S(1)}, bf16[2096,128]{1,0:T(8,128)(2,1)S(1)}, u32[]{:S(2)}, u32[]{:S(2)}) collective-permute-start(bf16[2096,128]{1,0:T(8,128)(2,1)S(1)} %get-tuple-element.22.refs_3_), channel_id=1, source_target_pairs={{0,56},{8,0},{16,8},{24,16},{32,24},{40,32},{48,40},{56,48},{64,12... | collective-permute-start | bytes 1609736 | tf_op jit(solution)/shard_map/ppermute | solution.py:26
  25.3 17.2 %collective-permute-start = (bf16[2064,128]{1,0:T(8,128)(2,1)S(1)}, bf16[2064,128]{1,0:T(8,128)(2,1)S(1)}, u32[]{:S(2)}, u32[]{:S(2)}) collective-permute-start(bf16[2064,128]{1,0:T(8,128)(2,1)S(1)} %get-tuple-element.20.refs_0_), channel_id=1, source_target_pairs={{0,8},{8,16},{16,24},{24,32},{32,40},{40,48},{48,56},{56,0},{64,72... | collective-permute-start | bytes 1585160 | tf_op jit(solution)/shard_map/ppermute | solution.py:26
  30.8 8.7 %collective-permute-start.2 = (bf16[128,1024]{1,0:T(8,128)(2,1)S(1)}, bf16[128,1024]{1,0:T(8,128)(2,1)S(1)}, u32[]{:S(2)}, u32[]{:S(2)}) collective-permute-start(bf16[128,1024]{1,0:T(8,128)(2,1)S(1)} %shard_map.84.qt_ref), channel_id=1, source_target_pairs={{0,64},{8,72},{16,80},{24,88},{32,96},{40,104},{48,112},{56,120},{... | collective-permute-start | bytes 786440 | tf_op jit(solution)/shard_map/ppermute | solution.py:26
  46.2 7.2 %collective-permute-start.3 = (bf16[1056,128]{1,0:T(8,128)(2,1)S(1)}, bf16[1056,128]{1,0:T(8,128)(2,1)S(1)}, u32[]{:S(2)}, u32[]{:S(2)}) collective-permute-start(bf16[1056,128]{1,0:T(8,128)(2,1)S(1)} %shard_map.89), channel_id=1, source_target_pairs={{0,448},{8,456},{16,464},{24,472},{32,480},{40,488},{48,496},{56,5... | collective-permute-start | bytes 811016 | tf_op jit(solution)/shard_map/ppermute | solution.py:26
  53.8 49.1 %copy-start = (bf16[2048,256]{1,0:T(8,128)(2,1)S(1)}, bf16[2048,256]{1,0:T(8,128)(2,1)}, u32[]{:S(2)}) copy-start(bf16[2048,256]{1,0:T(8,128)(2,1)} %w_ref.1) | copy-start | bytes 3145732
  90.4 8.3 %collective-permute-start.6 = (bf16[1024,128]{1,0:T(8,128)(2,1)S(1)}, bf16[1024,128]{1,0:T(8,128)(2,1)S(1)}, u32[]{:S(2)}, u32[]{:S(2)}) collective-permute-start(bf16[1024,128]{1,0:T(8,128)(2,1)S(1)} %bitcast.12), channel_id=1, source_target_pairs={{0,8},{8,16},{16,24},{24,32},{32,40},{40,48},{48,56},{56,0},{64,72... | collective-permute-start | bytes 786440 | tf_op jit(solution)/shard_map/ppermute | solution.py:26
  92.3 7.1 %collective-permute-start.5 = (bf16[1024,128]{1,0:T(8,128)(2,1)S(1)}, bf16[1024,128]{1,0:T(8,128)(2,1)S(1)}, u32[]{:S(2)}, u32[]{:S(2)}) collective-permute-start(bf16[1024,128]{1,0:T(8,128)(2,1)S(1)} %bitcast.13), channel_id=1, source_target_pairs={{0,448},{8,456},{16,464},{24,472},{32,480},{40,488},{48,496},{56,5... | collective-permute-start | bytes 786440 | tf_op jit(solution)/shard_map/ppermute | solution.py:26
  94.2 8.6 %collective-permute-start.4 = (bf16[1024,128]{1,0:T(8,128)(2,1)S(1)}, bf16[1024,128]{1,0:T(8,128)(2,1)S(1)}, u32[]{:S(2)}, u32[]{:S(2)}) collective-permute-start(bf16[1024,128]{1,0:T(8,128)(2,1)S(1)} %bitcast.14), channel_id=1, source_target_pairs={{0,64},{8,72},{16,80},{24,88},{32,96},{40,104},{48,112},{56,120},{... | collective-permute-start | bytes 786440 | tf_op jit(solution)/shard_map/ppermute | solution.py:26
